TPU v7x, 256 devices: a whole 4x4x8 slice. The times are simulated.
256 devices in a mesh: nodes: 32 (over x, y, core), heads: 8 (over z).
Axes of the slice: x: 4, y: 4, z: 8, core: 2. Of those that a mesh axis runs over, the one named last changes fastest.
Arguments:
- node_states: bfloat16 [131072, 512], P('nodes'), may hold values from -6 to 6
- virtual_states: bfloat16 [32, 512], P('nodes'), may hold values from -6 to 6
- project_weight: bfloat16 [512, 1536], P(None, 'heads'), may hold values from -0.4375 to 0.4375
- output_weight: bfloat16 [512, 512], replicated, may hold values from -0.25 to 0.25
- expand_weight: bfloat16 [512, 2048], P(None, 'heads'), may hold values from -0.25 to 0.25
- expand_bias: float32 [2048], replicated, may hold values from -5 to 5
- contract_weight: bfloat16 [2048, 512], P('heads'), may hold values from -0.125 to 0.125
- neigh_source: int32 [1024, 4], P('nodes'), may hold values from 0 to 1023, as said below
- neigh_rows: int32 [1024, 4, 128], P('nodes'), may hold values from 0 to 127
- neigh_count: int32 [1024, 4], P('nodes'), may hold values from 1 to 128
- expander_source: int32 [1024, 4], P('nodes'), may hold values from 0 to 1023, as said below
- expander_rows: int32 [1024, 4, 128], P('nodes'), may hold values from 0 to 127, each once within a row
- expander_count: int32 [1024, 4], P('nodes'), may hold values from 112 to 128
Outputs:
- updated: bfloat16 [131072, 512], P(('nodes', 'heads'))
Inputs may be any that keep to these rules, and one draw needn't show every extreme that they name: `neigh_source`: the neighbour tiles of block b have source block b - 1, b or b + 1 modulo 1024. `expander_source`: for the blocks of one index of nodes and any one index of nodes, at most 8 expander tiles have their source block there, naming at most 4 distinct source blocks; both bounds are reached.
All inputs are finite; a program needn't handle non-finite values.
Results may differ from a plain program's by a relative error of at most 0.012.
Values may be sent and summed in bfloat16 or wider, within the bound.
No kernel may reach another device: no remote copies, remote signals or barrier semaphores. Data moves between devices by JAX's collectives and lax.ppermute only.
A program may use at most 128 MiB of HBM per device.

v0:
```python
import jax
import jax.numpy as jnp
from jax import lax
from jax.sharding import PartitionSpec as P

HEAD_DIM = 64


eps_norm = 1e-05
clip_level = 5.0


def with_halo(cells, sides, width):
    for axis, dim in sides:
        count = lax.axis_size(axis)
        head = lax.slice_in_dim(cells, 0, width, axis=dim)
        tail = lax.slice_in_dim(cells, cells.shape[dim] - width, cells.shape[dim], axis=dim)
        cells = jnp.concatenate(
            [
                lax.ppermute(tail, axis, [(i, (i + 1) % count) for i in range(count)]),
                cells,
                lax.ppermute(head, axis, [((i + 1) % count, i) for i in range(count)]),
            ],
            axis=dim,
        )
    return cells


def layer_norm(values):
    values = values.astype(jnp.float32)
    center = values - jnp.mean(values, axis=-1, keepdims=True)
    spread = jnp.mean(center * center, axis=-1, keepdims=True)
    return center * lax.rsqrt(spread + eps_norm)


def attend(query, graph_pairs, usable, virtual_pairs):
    scaling = HEAD_DIM ** (-0.5)
    graph_score = (
        jnp.einsum(
            "nbhd,ngbhd->ngbh", query, graph_pairs[..., 0, :], preferred_element_type=jnp.float32
        )
        * scaling
    )
    virtual_score = (
        jnp.einsum(
            "nbhd,vhd->nbvh", query, virtual_pairs[:, :, 0, :], preferred_element_type=jnp.float32
        )
        * scaling
    )
    graph_weight = jnp.where(
        usable[..., None], jnp.exp(jnp.clip(graph_score, -clip_level, clip_level)), 0.0
    )
    virtual_weight = jnp.exp(jnp.clip(virtual_score, -clip_level, clip_level))
    summed = jnp.sum(graph_weight, axis=1) + jnp.sum(virtual_weight, axis=2)
    graph_prob = (graph_weight / summed[:, None]).astype(jnp.bfloat16)
    virtual_prob = (virtual_weight / summed[:, :, None]).astype(jnp.bfloat16)
    result = jnp.einsum(
        "ngbh,ngbhd->nbhd", graph_prob, graph_pairs[..., 1, :], preferred_element_type=jnp.float32
    )
    result = result + jnp.einsum(
        "nbvh,vhd->nbhd",
        virtual_prob,
        virtual_pairs[:, :, 1, :],
        preferred_element_type=jnp.float32,
    )
    return result.astype(jnp.bfloat16)


def pick_rows(within, slabs, block_rows):
    chooser = (within[..., None] == jnp.arange(block_rows, dtype=jnp.int32)).astype(jnp.bfloat16)
    return jnp.einsum("krq,kqw->krw", chooser, slabs, preferred_element_type=jnp.float32).astype(
        jnp.bfloat16
    )


def local(
    node_states,
    virtual_states,
    project_weight,
    output_weight,
    expand_weight,
    expand_bias,
    contract_weight,
    neigh_source,
    neigh_rows,
    neigh_count,
    expander_source,
    expander_rows,
    expander_count,
):
    node_span = lax.axis_size("nodes")
    node_index = lax.axis_index("nodes")
    head_span = lax.axis_size("heads")
    head_index = lax.axis_index("heads")
    local_blocks, neigh_tiles, block_rows = neigh_rows.shape
    expander_degree = expander_rows.shape[1]
    row_total, features = node_states.shape
    share_rows = row_total // head_span
    head_size = HEAD_DIM
    local_heads = project_weight.shape[1] // (3 * head_size)
    pair_width = 2 * local_heads * head_size
    all_blocks = local_blocks * node_span
    normed = layer_norm(node_states).astype(jnp.bfloat16)
    projected = jnp.dot(normed, project_weight, preferred_element_type=jnp.float32).astype(
        jnp.bfloat16
    )
    projected = projected.reshape(row_total, local_heads, 3, head_size)
    query = projected[:, :, 0, :].reshape(local_blocks, block_rows, local_heads, head_size)
    keyval = projected[:, :, 1:, :].reshape(row_total, pair_width)
    virtual_normed = layer_norm(virtual_states).astype(jnp.bfloat16)
    virtual_projected = jnp.dot(
        virtual_normed, project_weight, preferred_element_type=jnp.float32
    ).astype(jnp.bfloat16)
    virtual_local = virtual_projected.reshape(-1, local_heads, 3, head_size)[:, :, 1:, :].reshape(
        -1, pair_width
    )
    virtual_pairs = lax.all_gather(virtual_local, "nodes", axis=0, tiled=True).reshape(
        -1, local_heads, 2, head_size
    )
    pair_blocks = keyval.reshape(local_blocks, block_rows, pair_width)
    extended = with_halo(pair_blocks, (("nodes", 0),), 1)
    windows = jnp.concatenate([extended[:-2], extended[1:-1], extended[2:]], axis=1)
    local_ids = jnp.arange(local_blocks, dtype=jnp.int32)
    global_ids = node_index * local_blocks + local_ids
    shift_by = jnp.mod(neigh_source - global_ids[:, None] + 1, all_blocks) - 1
    window_col = (1 + shift_by)[:, :, None] * block_rows + neigh_rows
    window_pick = (window_col[..., None] == jnp.arange(3 * block_rows, dtype=jnp.int32)).astype(
        jnp.bfloat16
    )
    neighbour_pairs = jnp.einsum(
        "bgrc,bcw->bgrw", window_pick, windows, preferred_element_type=jnp.float32
    ).astype(jnp.bfloat16)
    tile_count = local_blocks * expander_degree
    source = expander_source.reshape(tile_count)
    owner_node = source // local_blocks
    owner_block = source % local_blocks
    tile_rows = expander_rows.reshape(tile_count, block_rows)
    cap_tiles = 2 * tile_count // node_span
    slot_total = node_span * cap_tiles
    positions = jnp.arange(tile_count, dtype=jnp.int32)
    earlier = positions[:, None] > positions[None, :]
    same_owner = owner_node[:, None] == owner_node[None, :]
    slot_rank = jnp.sum(earlier & same_owner, axis=1)
    tile_slot = owner_node * cap_tiles + slot_rank
    slot_table = (jnp.arange(slot_total, dtype=jnp.int32)[:, None] == tile_slot[None, :]).astype(
        jnp.float32
    )
    wanted_values = (owner_block[:, None] * block_rows + tile_rows).astype(jnp.float32)
    requests = jnp.dot(slot_table, wanted_values, precision=lax.Precision.HIGHEST).astype(jnp.int32)
    requests = requests.reshape(node_span, cap_tiles, block_rows)
    requested = lax.all_to_all(requests, "nodes", split_axis=0, concat_axis=0, tiled=True)
    spans, items, _ = requested.shape
    flat = requested.reshape(spans * items, block_rows)
    block_pick = (flat[:, 0:1] // block_rows == local_ids[None, :]).astype(jnp.bfloat16)
    slabs = jnp.einsum(
        "kl,lrw->krw", block_pick, pair_blocks, preferred_element_type=jnp.float32
    ).astype(jnp.bfloat16)
    picked = pick_rows(flat % block_rows, slabs, block_rows).reshape(
        spans, items, block_rows, pair_width
    )
    replies = lax.all_to_all(picked, "nodes", split_axis=0, concat_axis=0, tiled=True)
    reply_pick = (tile_slot[:, None] == jnp.arange(slot_total, dtype=jnp.int32)[None, :]).astype(
        jnp.bfloat16
    )
    expander_pairs = jnp.einsum(
        "ts,srw->trw",
        reply_pick,
        replies.reshape(slot_total, block_rows, pair_width),
        preferred_element_type=jnp.float32,
    ).astype(jnp.bfloat16)
    expander_pairs = expander_pairs.reshape(local_blocks, expander_degree, block_rows, pair_width)
    graph_pairs = jnp.concatenate([neighbour_pairs, expander_pairs], axis=1)
    graph_pairs = graph_pairs.reshape(
        local_blocks, neigh_tiles + expander_degree, block_rows, local_heads, 2, head_size
    )
    counts = jnp.concatenate([neigh_count, expander_count], axis=1)
    usable = jnp.arange(block_rows, dtype=jnp.int32)[None, None, :] < counts[:, :, None]
    attended = attend(query, graph_pairs, usable, virtual_pairs).reshape(
        row_total, local_heads * head_size
    )
    own_rows = lax.dynamic_slice_in_dim(node_states, head_index * share_rows, share_rows, 0).astype(
        jnp.float32
    )
    regrouped = lax.all_to_all(attended, "heads", split_axis=0, concat_axis=1, tiled=True)
    residual = own_rows + jnp.dot(regrouped, output_weight, preferred_element_type=jnp.float32)
    normed_two = layer_norm(residual).astype(jnp.bfloat16)
    inner = (
        jnp.dot(
            normed_two,
            lax.all_gather(expand_weight, "heads", axis=1, tiled=True),
            preferred_element_type=jnp.float32,
        )
        + expand_bias
    )
    hidden = jax.nn.gelu(inner, approximate=False).astype(jnp.bfloat16)
    update = jnp.dot(
        hidden,
        lax.all_gather(contract_weight, "heads", axis=0, tiled=True),
        preferred_element_type=jnp.float32,
    )
    return (residual + update).astype(jnp.bfloat16)


def solution(mesh):
    return jax.shard_map(
        local,
        mesh=mesh,
        in_specs=(
            P("nodes", None),
            P("nodes", None),
            P(None, "heads"),
            P(),
            P(None, "heads"),
            P(),
            P("heads", None),
            P("nodes", None),
            P("nodes", None, None),
            P("nodes", None),
            P("nodes", None),
            P("nodes", None, None),
            P("nodes", None),
        ),
        out_specs=P(("nodes", "heads"), None),
        check_vma=False,
    )
```

profile of v0, /device:TPU:8, one launch (start us, length us, event | category | flops | bytes accessed | tf_op | source)
XLA Modules:
  0.0 282.1 jit_solution(16513967208969000580)
XLA Ops:
  7.7 1.8 fusion.51
  9.4 7.5 %all-to-all-start = ((s32[32,8,128]{2,1,0:T(8,128)}), s32[32,8,128]{2,1,0:T(8,128)S(1)}, u32[]{:S(2)}, u32[]{:S(2)}) async-start(s32[32,8,128]{2,1,0:T(8,128)} %fusion.51), calls=%async_computation | async-start | bytes 262144 | tf_op jit(solution)/shard_map/all_to_all | solution.py:151
  17.0 3.0 %convert_reduce_fusion = f32[4096]{0:T(1024)S(1)} fusion(bf16[4096,512]{1,0:T(8,128)(2,1)} %param.13), kind=kLoop, calls=%fused_computation.6 | loop fusion | flops 4190208 | bytes 4210688 | tf_op jit(solution)/shard_map/reduce_sum | solution.py:31
  20.4 1.8 fusion.5
  22.2 2.8 convolution_convert_fusion.1
  26.2 1.5 copy.83
  27.9 2.4 convolution_convert_fusion
  30.3 21.7 %fusion.12 = bf16[256,128,128]{2,1,0:T(8,128)(2,1)} fusion(bf16[256,128,128]{2,0,1:T(8,128)(2,1)S(1)} %convolution_convert_fusion, s32[256,128]{1,0:T(8,128)S(1)} %add_select_fusion.1), kind=kOutput, calls=%fused_computation.20 | convolution fusion | flops 1082130432 | bytes 16908288 | tf_op jit(solution)/shard_map/krq,kqw->krw/dot_general | solution.py:71
  52.0 7.6 %all-to-all-start.1 = ((bf16[32,8,128,128]{3,2,1,0:T(8,128)(2,1)}), bf16[32,8,128,128]{3,2,1,0:T(8,128)(2,1)}, u32[]{:S(2)}, u32[]{:S(2)}) async-start(bf16[32,8,128,128]{3,2,1,0:T(8,128)(2,1)} %bitcast.124), calls=%async_computation.1 | async-start | bytes 16777216 | tf_op jit(solution)/shard_map/all_to_all | solution.py:161
  61.3 1.6 collective-permute-start.1
  63.1 1.1 slice_bitcast_fusion
  67.2 128.4 %all-gather = bf16[32,1,128]{2,1,0:T(2,128)(2,1)S(1)} all-gather(bf16[1,1,128]{2,1,0:T(2,128)(2,1)S(1)} %reshape.315), channel_id=1, replica_groups=mesh['nodes'=32,'heads'=8] {'nodes'}, dimensions={0}, use_global_device_ids=true | all-gather | bytes 8448 | tf_op jit(solution)/shard_map/all_gather | solution.py:117
  196.4 1.5 copy.79
  198.6 8.9 %fusion.39 = bf16[32,4,128,128]{2,3,1,0:T(8,128)(2,1)} fusion(bf16[1,128,128]{1,2,0:T(8,128)(2,1)S(1)} %collective-permute-done.1, bf16[32,128,128]{1,2,0:T(8,128)(2,1)} %copy.79, bf16[1,128,128]{1,2,0:T(8,128)(2,1)S(1)} %collective-permute-done, s32[32,4,128]{2,1,0:T(4,128)S(1)} %broadcast_add_fusion), kind=kOutput, calls=%fused_computation.56 | convolution fusion | flops 1634729984 | bytes 5373952 | tf_op jit(solution)/shard_map/bgrc,bcw->bgrw/dot_general | solution.py:130
  207.4 11.0 %fusion.42 = bf16[128,128,128]{2,0,1:T(8,128)(2,1)} fusion(bf16[32,8,128,128]{3,2,1,0:T(8,128)(2,1)} %all-to-all-done.1, s32[128]{0:T(128)S(1)} %multiply_add_fusion), kind=kOutput, calls=%fused_computation.57 | convolution fusion | flops 1075871744 | bytes 12583424 | tf_op jit(solution)/shard_map/ts,srw->trw/dot_general | solution.py:165
  218.5 6.9 %copy.86 = bf16[128,128,128]{1,2,0:T(8,128)(2,1)} copy(bf16[128,128,128]{2,0,1:T(8,128)(2,1)} %fusion.42) | data formatting | bytes 8388608 | tf_op jit(solution)/shard_map/convert_element_type | solution.py:170
  225.4 3.5 %multiply_reduce_fusion.1 = f32[32,128,8]{1,2,0:T(8,128)S(1)} fusion(bf16[32,4,128,1,2,64]{2,5,4,1,0,3:T(8,128)(2,1)} %bitcast.120, bf16[32,4,128,1,2,64]{2,5,4,1,0,3:T(8,128)(2,1)} %bitcast.118, f32[32,128,64]{1,2,0:T(8,128)S(1)} %copy.112), kind=kLoop, calls=%fused_computation.16 | loop fusion | flops 8355840 | bytes 9568256 | tf_op jit(solution)/shard_map/nbhd,ngbhd->ngbh/dot_general | solution.py:39
  229.2 1.0 copy-done.3
  230.1 1.5 multiply_reduce_fusion
  233.6 8.5 %all-to-all-start.2 = ((bf16[8,512,64]{1,2,0:T(8,128)(2,1)}), bf16[8,512,64]{1,2,0:T(8,128)(2,1)S(1)}, u32[]{:S(2)}, u32[]{:S(2)}) async-start(bf16[8,512,64]{1,2,0:T(8,128)(2,1)} %copy.91), calls=%async_computation.2 | async-start | bytes 1048576 | tf_op jit(solution)/shard_map/all_to_all | solution.py:184
  242.1 1.1 constant_dynamic-slice_fusion
  243.4 16.7 %all-to-all-done.2 = bf16[8,512,64]{1,2,0:T(8,128)(2,1)S(1)} async-done(((bf16[8,512,64]{1,2,0:T(8,128)(2,1)}), bf16[8,512,64]{1,2,0:T(8,128)(2,1)S(1)}, u32[]{:S(2)}, u32[]{:S(2)}) %all-to-all-start.2) | async-done | bytes 524320 | tf_op jit(solution)/shard_map/all_to_all | solution.py:184
  260.8 13.4 %fusion.47 = bf16[512,512]{0,1:T(8,128)(2,1)S(1)} fusion(f32[512,512]{0,1:T(8,128)S(1)} %get-tuple-element.14, bf16[2048,512]{1,0:T(8,128)(2,1)} %all-gather.6.cloned.1.call-done, bf16[512,2048]{1,0:T(8,128)(2,1)} %all-gather.4.cloned.1.call-done, f32[2048]{0:T(1024)S(1)} %copy-done.11, f32[512]{0:T(512)S(1)} %add_rsqrt_fusion.1, ...), kind=kOutput, calls=%fused_computation.62 | convolution fusion | flops 2218000384 | bytes 5779456 | tf_op jit(solution)/shard_map/dot_general | solution.py:196
  274.3 1.0 copy.93
  (78 shorter events, 10.9 us)
Async XLA Ops:
  6.5 253.5 %copy-start = (bf16[512,512]{1,0:T(8,128)(2,1)S(1)}, bf16[512,512]{1,0:T(8,128)(2,1)}, u32[]{:S(2)}) copy-start(bf16[512,512]{1,0:T(8,128)(2,1)} %param.16) | copy-start | bytes 1572868
  9.4 18.3 %all-to-all-start = ((s32[32,8,128]{2,1,0:T(8,128)}), s32[32,8,128]{2,1,0:T(8,128)S(1)}, u32[]{:S(2)}, u32[]{:S(2)}) async-start(s32[32,8,128]{2,1,0:T(8,128)} %fusion.51), calls=%async_computation | async-start | bytes 262144 | tf_op jit(solution)/shard_map/all_to_all | solution.py:151
  17.0 3.5 %copy-start.2 = (bf16[4096,512]{1,0:T(8,128)(2,1)S(1)}, bf16[4096,512]{1,0:T(8,128)(2,1)}, u32[]{:S(2)}) copy-start(bf16[4096,512]{1,0:T(8,128)(2,1)} %param.13) | copy-start | bytes 12582916
  17.0 5.2 %copy-start.5 = (bf16[512,192]{0,1:T(8,128)(2,1)S(1)}, bf16[512,192]{0,1:T(8,128)(2,1)}, u32[]{:S(2)}) copy-start(bf16[512,192]{0,1:T(8,128)(2,1)} %param.15) | copy-start | bytes 589828
  25.0 1.2 copy-start.4
  52.0 11.0 %copy-start.8 = (s32[32,4]{0,1:T(4,128)S(1)}, s32[32,4]{0,1:T(4,128)}, u32[]{:S(2)}) copy-start(s32[32,4]{0,1:T(4,128)} %param.20) | copy-start | bytes 1540
  52.0 12.3 %copy-start.7 = (bf16[1,512]{1,0:T(2,128)(2,1)S(1)}, bf16[1,512]{1,0:T(2,128)(2,1)}, u32[]{:S(2)}) copy-start(bf16[1,512]{1,0:T(2,128)(2,1)} %param.14) | copy-start | bytes 3076
  52.0 155.4 %all-to-all-start.1 = ((bf16[32,8,128,128]{3,2,1,0:T(8,128)(2,1)}), bf16[32,8,128,128]{3,2,1,0:T(8,128)(2,1)}, u32[]{:S(2)}, u32[]{:S(2)}) async-start(bf16[32,8,128,128]{3,2,1,0:T(8,128)(2,1)} %bitcast.124), calls=%async_computation.1 | async-start | bytes 16777216 | tf_op jit(solution)/shard_map/all_to_all | solution.py:161
  59.6 136.5 %copy-start.6 = (s32[32,4,128]{2,1,0:T(4,128)S(1)}, s32[32,4,128]{2,1,0:T(4,128)}, u32[]{:S(2)}) copy-start(s32[32,4,128]{2,1,0:T(4,128)} %param.21) | copy-start | bytes 196612
  59.6 136.8 %copy-start.9 = (s32[32,4]{0,1:T(4,128)S(1)}, s32[32,4]{0,1:T(4,128)}, u32[]{:S(2)}) copy-start(s32[32,4]{0,1:T(4,128)} %param.25) | copy-start | bytes 1540
  59.6 136.8 %copy-start.10 = (s32[32,4]{0,1:T(4,128)S(1)}, s32[32,4]{0,1:T(4,128)}, u32[]{:S(2)}) copy-start(s32[32,4]{0,1:T(4,128)} %param.22) | copy-start | bytes 1540
  59.6 201.2 %all-gather.4.cloned.1.call-start = ((), (), s32[]{:S(2)}) async-start(), calls=%async_computation.3 | async-start | bytes 2359296 | tf_op jit(solution)/shard_map/all_gather | solution.py:190
  60.4 200.5 %all-gather.6.cloned.1.call-start = ((), (), s32[]{:S(2)}) async-start(), calls=%async_computation.4 | async-start | bytes 2359296 | tf_op jit(solution)/shard_map/all_gather | solution.py:198
  61.2 137.4 %collective-permute-start = (bf16[1,128,128]{1,2,0:T(8,128)(2,1)S(1)}, bf16[1,128,128]{1,2,0:T(8,128)(2,1)S(1)}, u32[]{:S(2)}, u32[]{:S(2)}) collective-permute-start(bf16[1,128,128]{1,2,0:T(8,128)(2,1)S(1)} %bitcast.134), channel_id=1, source_target_pairs={{0,8},{8,16},{16,24},{24,32},{32,40},{40,48},{48,56},{56,64},{64,7... | collective-permute-start | bytes 98312 | tf_op jit(solution)/shard_map/ppermute | solution.py:20
  61.3 137.2 %collective-permute-start.1 = (bf16[1,128,128]{1,2,0:T(8,128)(2,1)S(1)}, bf16[1,128,128]{1,2,0:T(8,128)(2,1)S(1)}, u32[]{:S(2)}, u32[]{:S(2)}) collective-permute-start(bf16[1,128,128]{1,2,0:T(8,128)(2,1)S(1)} %bitcast.133), channel_id=1, source_target_pairs={{8,0},{16,8},{24,16},{32,24},{40,32},{48,40},{56,48},{64,56},{72,6... | collective-permute-start | bytes 98312 | tf_op jit(solution)/shard_map/ppermute | solution.py:22
  225.4 3.8 %copy-start.1 = (bf16[128,128,128]{1,2,0:T(8,128)(2,1)S(1)}, bf16[128,128,128]{1,2,0:T(8,128)(2,1)}, u32[]{:S(2)}) copy-start(bf16[128,128,128]{1,2,0:T(8,128)(2,1)} %copy.86) | copy-start | bytes 12582916
  225.4 4.7 %copy-start.3 = (bf16[32,4,128,128]{2,3,1,0:T(8,128)(2,1)S(1)}, bf16[32,4,128,128]{2,3,1,0:T(8,128)(2,1)}, u32[]{:S(2)}) copy-start(bf16[32,4,128,128]{2,3,1,0:T(8,128)(2,1)} %fusion.39) | copy-start | bytes 12582916
  232.7 28.2 %copy-start.11 = (f32[2048]{0:T(1024)S(1)}, f32[2048]{0:T(1024)}, u32[]{:S(2)}) copy-start(f32[2048]{0:T(1024)} %param.18) | copy-start | bytes 24580
  233.6 26.5 %all-to-all-start.2 = ((bf16[8,512,64]{1,2,0:T(8,128)(2,1)}), bf16[8,512,64]{1,2,0:T(8,128)(2,1)S(1)}, u32[]{:S(2)}, u32[]{:S(2)}) async-start(bf16[8,512,64]{1,2,0:T(8,128)(2,1)} %copy.91), calls=%async_computation.2 | async-start | bytes 1048576 | tf_op jit(solution)/shard_map/all_to_all | solution.py:184
Sparse Core Ops, SparseCore 0:
  62.2 49.3 all-gather.3
  113.3 39.9 all-gather.5
where the time goes:
time: 284 us; the launch traced here: 282 us
  blocking collectives  128 us (45%)
  matrix products  63.2 us (22%)
  starting transfers between devices  25.4 us (9%)
  local copies, waits for them, and re-layouts  20.3 us (7%)
  waiting for transfers between devices  17.4 us (6%)
  between operations  15.2 us (5%)
  other arithmetic  12.1 us (4%)
    all_gather x1, blocking collectives, local(): lax.all_gather(virtual_local, 'nodes', axis=0, tiled=True)  128 us
    dot_general x1, matrix products, pick_rows(): jnp.einsum('krq,kqw->krw', chooser, slabs, preferred_element_type=jnp.flo...  21.7 us
    all_to_all x1, waiting for transfers between devices, local(): lax.all_to_all(attended, 'heads', split_axis=0, concat_axis=1, tiled=True)  16.7 us
    dot_general x1, matrix products, local(): jnp.dot(hidden, lax.all_gather(contract_weight, 'heads', axis=0, tiled=Tr...  13.4 us
    dot_general x1, matrix products, local(): jnp.einsum('ts,srw->trw', reply_pick, replies.reshape(slot_total, block_r...  11 us
    dot_general x1, matrix products, local(): jnp.einsum('bgrc,bcw->bgrw', window_pick, windows, preferred_element_type...  8.89 us
    all_to_all x1, starting transfers between devices, local(): lax.all_to_all(attended, 'heads', split_axis=0, concat_axis=1, tiled=True)  8.45 us
    all_to_all x1, starting transfers between devices, local(): lax.all_to_all(picked, 'nodes', split_axis=0, concat_axis=0, tiled=True)  7.57 us
  transfers between devices with their start and end apart: 7, of which 1 were waited for; matrix products, arithmetic and copies ran while one was open for 18% of the time, Pallas kernels for 0%

commit v1 on v0

v1 whole, which is shorter than its diff:
```python
import functools

import jax
import jax.numpy as jnp
from jax import lax
from jax.experimental import pallas as pl
from jax.experimental.pallas import tpu as pltpu
from jax.sharding import PartitionSpec as P

HEAD_DIM = 64
BCAP = 4

eps_norm = 1e-05
clip_level = 5.0

f32 = jnp.float32
bf16 = jnp.bfloat16
VMEM_LIMIT = 56 * 2**20


def layer_norm(values):
    values = values.astype(f32)
    center = values - jnp.mean(values, axis=-1, keepdims=True)
    spread = jnp.mean(center * center, axis=-1, keepdims=True)
    return center * lax.rsqrt(spread + eps_norm)


def params():
    return pltpu.CompilerParams(vmem_limit_bytes=VMEM_LIMIT)


def project_kernel(x_ref, w_ref, query_ref, pack_ref, side_ref):
    head = HEAD_DIM

    @pl.when(pl.program_id(0) == 0)
    def _():
        weight = w_ref[...]
        side = jnp.concatenate([weight[:, :head], weight[:, 2 * head :]], axis=1)
        side_ref[...] = side.T

    normed = layer_norm(x_ref[...]).astype(bf16)
    sides = lax.dot_general(
        side_ref[...], normed, (((1,), (1,)), ((), ())), preferred_element_type=f32
    ).astype(bf16)
    keys = jnp.dot(normed, w_ref[:, head : 2 * head], preferred_element_type=f32).astype(bf16)
    query_ref[...] = sides[:head] * jnp.asarray(head**-0.5, bf16)
    rows = 2 * head
    for item in range(x_ref.shape[0] // rows):
        low = keys[item * rows : item * rows + head]
        high = keys[item * rows + head : (item + 1) * rows]
        pack_ref[item, :head, :] = jnp.concatenate([low, high], axis=1)
        pack_ref[item, head:, :] = sides[head:, item * rows : (item + 1) * rows]


def project(states, weight, step_rows):
    rows, features = states.shape
    wide = 2 * HEAD_DIM
    return pl.pallas_call(
        project_kernel,
        grid=(rows // step_rows,),
        in_specs=[
            pl.BlockSpec((step_rows, features), lambda i: (i, 0)),
            pl.BlockSpec(weight.shape, lambda i: (0, 0)),
        ],
        out_specs=[
            pl.BlockSpec((HEAD_DIM, step_rows), lambda i: (0, i)),
            pl.BlockSpec((step_rows // wide, wide, wide), lambda i: (i, 0, 0)),
        ],
        out_shape=[
            jax.ShapeDtypeStruct((HEAD_DIM, rows), bf16),
            jax.ShapeDtypeStruct((rows // wide, wide, wide), bf16),
        ],
        scratch_shapes=[pltpu.VMEM((wide, features), bf16)],
        compiler_params=params(),
        name="project",
    )(states, weight)


def select_kernel(wanted_ref, pack_ref, out_ref):
    count = out_ref.shape[0]
    base = pl.program_id(0) * count
    for item in range(count):
        out_ref[item] = pack_ref[wanted_ref[base + item]]


def select_blocks(wanted, packed, step_items):
    total = wanted.shape[0]
    return pl.pallas_call(
        select_kernel,
        grid_spec=pltpu.PrefetchScalarGridSpec(
            num_scalar_prefetch=1,
            grid=(total // step_items,),
            in_specs=[pl.BlockSpec(packed.shape, lambda i, s: (0, 0, 0))],
            out_specs=pl.BlockSpec((step_items,) + packed.shape[1:], lambda i, s: (i, 0, 0)),
        ),
        out_shape=jax.ShapeDtypeStruct((total,) + packed.shape[1:], bf16),
        compiler_params=params(),
        name="select_blocks",
    )(wanted, packed)


def wide_query(query):
    zero = jnp.zeros_like(query)
    return jnp.concatenate(
        [jnp.concatenate([query, zero], axis=1), jnp.concatenate([zero, query], axis=1)], axis=0
    )


def tile_terms(queries, blocks, rows, counts):
    head = HEAD_DIM
    lane = lax.broadcasted_iota(jnp.int32, (1, 2 * head), 1)
    spot = lax.broadcasted_iota(jnp.int32, (head, 2 * head), 0)
    tables = []
    total = None
    for tile, block in enumerate(blocks):
        scores = jnp.dot(block[:head], queries, preferred_element_type=f32)
        row = rows[tile : tile + 1]
        low = row < head
        chosen = jnp.where(low, scores[:, : 2 * head], scores[:, 2 * head :])
        hit = spot == jnp.where(low, row, row - head)
        score = jnp.sum(jnp.where(hit, chosen, 0.0), axis=0, keepdims=True)
        weight = jnp.exp(jnp.clip(score, -clip_level, clip_level))
        weight = jnp.where(lane < counts[tile], weight, 0.0)
        total = weight if total is None else total + weight
        tables.append(jnp.where(hit, jnp.where(low, weight, 0.0), 0.0).astype(bf16))
        tables.append(jnp.where(hit, jnp.where(low, 0.0, weight), 0.0).astype(bf16))
    values = jnp.concatenate([block[head:] for block in blocks], axis=1)
    summed = jnp.dot(values, jnp.concatenate(tables, axis=0), preferred_element_type=f32)
    return summed, total


def near_kernel(
    group, shift_ref, count_ref, query_ref, pack_ref, left_ref, right_ref, virtual_ref, rows_ref,
    sum_ref, total_ref, window_ref,
):
    head = HEAD_DIM
    blocks, tiles, wide = rows_ref.shape
    virtual_total = 32
    window_ref[0] = left_ref[...]
    window_ref[blocks + 1] = right_ref[...]

    def fill(block, _):
        window_ref[block + 1] = pack_ref[block]
        return 0

    lax.fori_loop(0, blocks, fill, 0, unroll=8)
    virtual_keys = virtual_ref[:virtual_total, :head]
    virtual_values = virtual_ref[head:, :virtual_total]

    def step(turn, _):
        for item in range(group):
            block = turn * group + item
            lanes = pl.ds(pl.multiple_of(block * wide, wide), wide)
            query = query_ref[:, lanes]
            tile_blocks = [window_ref[shift_ref[block * tiles + t]] for t in range(tiles)]
            counts = [count_ref[block * tiles + t] for t in range(tiles)]
            summed, total = tile_terms(wide_query(query), tile_blocks, rows_ref[block], counts)
            scores = jnp.dot(virtual_keys, query, preferred_element_type=f32)
            weights = jnp.exp(jnp.clip(scores, -clip_level, clip_level))
            total = total + jnp.sum(weights, axis=0, keepdims=True)
            summed = summed + jnp.dot(
                virtual_values, weights.astype(bf16), preferred_element_type=f32
            )
            sum_ref[:, lanes] = summed
            total_ref[:, lanes] = total
        return 0

    lax.fori_loop(0, blocks // group, step, 0)


def near_terms(shifts, counts, query, packed, left, right, virtual, rows, group):
    head, total = query.shape
    blocks = packed.shape[0]
    vmem = pl.BlockSpec(memory_space=pltpu.VMEM)
    smem = pl.BlockSpec(memory_space=pltpu.SMEM)
    return pl.pallas_call(
        functools.partial(near_kernel, group),
        in_specs=[smem, smem] + [vmem] * 6,
        out_specs=[vmem, vmem],
        out_shape=[
            jax.ShapeDtypeStruct((head, total), f32),
            jax.ShapeDtypeStruct((1, total), f32),
        ],
        scratch_shapes=[pltpu.VMEM((blocks + 2,) + packed.shape[1:], bf16)],
        compiler_params=params(),
        cost_estimate=pl.CostEstimate(
            flops=8 * 2**30, bytes_accessed=4 * 2**20, transcendentals=2**20
        ),
        name="near_terms",
    )(shifts, counts, query, packed, left, right, virtual, rows)


def far_kernel(
    group, slot_ref, count_ref, query_ref, reply_ref, rows_ref, sum_ref, total_ref, out_ref
):
    blocks, tiles, wide = rows_ref.shape
    share_blocks = blocks // out_ref.shape[0]

    def step(turn, _):
        for item in range(group):
            block = turn * group + item
            lanes = pl.ds(pl.multiple_of(block * wide, wide), wide)
            tile_blocks = [reply_ref[slot_ref[block * tiles + t]] for t in range(tiles)]
            counts = [count_ref[block * tiles + t] for t in range(tiles)]
            summed, total = tile_terms(
                wide_query(query_ref[:, lanes]), tile_blocks, rows_ref[block], counts
            )
            total = total + total_ref[:, lanes]
            result = (summed + sum_ref[:, lanes]) * (1.0 / total)
            inner = pl.ds(pl.multiple_of(lax.rem(block, share_blocks) * wide, wide), wide)
            out_ref[lax.div(block, share_blocks), :, inner] = result.astype(bf16)
        return 0

    lax.fori_loop(0, blocks // group, step, 0)


def far_terms(slots, counts, query, replies, rows, near_sum, near_total, shares, group):
    head, total = query.shape
    vmem = pl.BlockSpec(memory_space=pltpu.VMEM)
    smem = pl.BlockSpec(memory_space=pltpu.SMEM)
    return pl.pallas_call(
        functools.partial(far_kernel, group),
        in_specs=[smem, smem] + [vmem] * 5,
        out_specs=vmem,
        out_shape=jax.ShapeDtypeStruct((shares, head, total // shares), bf16),
        compiler_params=params(),
        name="far_terms",
    )(slots, counts, query, replies, rows, near_sum, near_total)


def tail_kernel(
    place_ref, att_ref, own_ref, output_ref, expand_ref, bias_ref, contract_ref, out_ref,
    normed_ref, sum_ref,
):
    step = pl.program_id(0)

    @pl.when(step == 0)
    def _():
        heads, head, rows = att_ref.shape
        attended = att_ref[...].reshape(heads * head, rows).T
        residual = own_ref[...].astype(f32) + jnp.dot(
            attended, output_ref[...], preferred_element_type=f32
        )
        normed_ref[...] = layer_norm(residual).astype(bf16)
        sum_ref[...] = residual

    inner = jnp.dot(normed_ref[...], expand_ref[...], preferred_element_type=f32) + bias_ref[...]
    hidden = (inner * 0.5) * (1.0 + lax.erf(inner * (0.5**0.5)))
    sum_ref[...] += jnp.dot(hidden.astype(bf16), contract_ref[...], preferred_element_type=f32)

    @pl.when(step == pl.num_programs(0) - 1)
    def _():
        out_ref[...] = sum_ref[...].astype(bf16)


def tail(place, regrouped, node_states, output_weight, expand, bias, contract):
    heads, head, rows = regrouped.shape
    features = heads * head
    parts, _, width = expand.shape
    return pl.pallas_call(
        tail_kernel,
        grid_spec=pltpu.PrefetchScalarGridSpec(
            num_scalar_prefetch=1,
            grid=(parts,),
            in_specs=[
                pl.BlockSpec(regrouped.shape, lambda i, s: (0, 0, 0)),
                pl.BlockSpec((rows, features), lambda i, s: (s[0], 0)),
                pl.BlockSpec(output_weight.shape, lambda i, s: (0, 0)),
                pl.BlockSpec((None, features, width), lambda i, s: (i, 0, 0)),
                pl.BlockSpec((None, 1, width), lambda i, s: (i, 0, 0)),
                pl.BlockSpec((None, width, features), lambda i, s: (i, 0, 0)),
            ],
            out_specs=pl.BlockSpec((rows, features), lambda i, s: (0, 0)),
            scratch_shapes=[pltpu.VMEM((rows, features), bf16), pltpu.VMEM((rows, features), f32)],
        ),
        out_shape=jax.ShapeDtypeStruct((rows, features), bf16),
        compiler_params=params(),
        name="tail",
    )(place, regrouped, node_states, output_weight, expand, bias, contract)


def ranked_blocks(present):
    size = present.shape[1]
    before = jnp.arange(size)[:, None] < jnp.arange(size)[None, :]
    return jnp.sum(jnp.where(present[:, :, None] & before[None], 1, 0), axis=1)


def local(
    node_states,
    virtual_states,
    project_weight,
    output_weight,
    expand_weight,
    expand_bias,
    contract_weight,
    neigh_source,
    neigh_rows,
    neigh_count,
    expander_source,
    expander_rows,
    expander_count,
):
    span = lax.axis_size("nodes")
    me = lax.axis_index("nodes")
    shares = lax.axis_size("heads")
    share = lax.axis_index("heads")
    blocks, neigh_tiles, block_rows = neigh_rows.shape
    features = node_states.shape[1]
    tile_count = expander_source.size
    all_blocks = blocks * span
    lanes = 128

    source = expander_source.reshape(1, tile_count)
    owner, place = source // blocks, source % blocks
    message = jnp.concatenate(
        [
            owner.astype(bf16),
            place.astype(bf16),
            virtual_states.reshape(features // lanes, lanes),
            jnp.zeros((2, lanes), bf16),
        ],
        axis=0,
    )
    message = jnp.broadcast_to(message[None], (span,) + message.shape)
    heard = lax.all_to_all(message, "nodes", split_axis=0, concat_axis=0, tiled=True)
    rightward = [(i, (i + 1) % span) for i in range(span)]
    leftward = [((i + 1) % span, i) for i in range(span)]
    left = lax.ppermute(node_states[-block_rows:], "nodes", rightward)
    right = lax.ppermute(node_states[:block_rows], "nodes", leftward)

    expand = lax.all_gather(expand_weight, "heads", axis=0)
    contract = lax.all_gather(contract_weight, "heads", axis=0)

    query, packed = project(node_states, project_weight, 512)

    local_ids = jnp.arange(blocks, dtype=jnp.int32)
    asked = jnp.where(heard[:, 0] == me.astype(bf16), heard[:, 1], jnp.asarray(-1, bf16))
    asked = asked.astype(jnp.int32)
    present = jnp.any(asked[:, :, None] == local_ids, axis=1)
    rank = ranked_blocks(present)
    slot_ids = jnp.arange(BCAP, dtype=jnp.int32)
    wanted = jnp.sum(
        jnp.where(present[:, None, :] & (rank[:, None, :] == slot_ids[:, None]), local_ids, 0),
        axis=2,
    )
    chosen = select_blocks(wanted.reshape(span * BCAP), packed, 16)
    replies = lax.all_to_all(
        chosen.reshape(span, BCAP * block_rows, lanes),
        "nodes",
        split_axis=0,
        concat_axis=0,
        tiled=True,
    ).reshape(span * BCAP, block_rows, lanes)

    extra = jnp.concatenate(
        [
            left,
            right,
            heard[:, 2 : 2 + features // lanes].reshape(span, features),
            jnp.zeros((block_rows - span, features), bf16),
        ],
        axis=0,
    )
    _, extra_packed = project(extra, project_weight, extra.shape[0])
    global_ids = me * blocks + local_ids
    shift = jnp.mod(neigh_source - global_ids[:, None] + 1, all_blocks) + local_ids[:, None]
    near_sum, near_total = near_terms(
        shift.reshape(-1),
        neigh_count.reshape(-1),
        query,
        packed,
        extra_packed[0],
        extra_packed[1],
        extra_packed[2],
        neigh_rows,
        4,
    )

    own_present = jnp.any(
        source[0][:, None] == jnp.arange(all_blocks, dtype=jnp.int32), axis=0
    ).reshape(span, blocks)
    own_rank = ranked_blocks(own_present).reshape(1, all_blocks)
    tile_rank = jnp.sum(
        jnp.where(source[0][:, None] == jnp.arange(all_blocks, dtype=jnp.int32), own_rank, 0), axis=1
    )
    slots = owner[0] * BCAP + tile_rank
    attended = far_terms(
        slots,
        expander_count.reshape(-1),
        query,
        replies,
        expander_rows,
        near_sum,
        near_total,
        shares,
        4,
    )
    regrouped = lax.all_to_all(attended, "heads", split_axis=0, concat_axis=0, tiled=True)
    return tail(
        share.reshape(1),
        regrouped,
        node_states,
        output_weight,
        expand,
        expand_bias.reshape(shares, 1, -1),
        contract,
    )


def solution(mesh):
    return jax.shard_map(
        local,
        mesh=mesh,
        in_specs=(
            P("nodes", None),
            P("nodes", None),
            P(None, "heads"),
            P(),
            P(None, "heads"),
            P(),
            P("heads", None),
            P("nodes", None),
            P("nodes", None, None),
            P("nodes", None),
            P("nodes", None),
            P("nodes", None, None),
            P("nodes", None),
        ),
        out_specs=P(("nodes", "heads"), None),
        check_vma=False,
    )
```

time: 284 us -> 167 us (0.59)
  the two profiles are of different devices: /device:TPU:8 before, /device:TPU:1 now
where the time goes in v1:
time: 167 us; the launch traced here: 166 us
  waiting for transfers between devices  63.5 us (38%)
  Pallas kernels  48.8 us (29%)
  starting transfers between devices  26.1 us (16%)
  between operations  13.5 us (8%)
  local copies, waits for them, and re-layouts  10.1 us (6%)
  other arithmetic  3.85 us (2%)
    ppermute x1, waiting for transfers between devices, local(): left = lax.ppermute(node_states[-block_rows:], 'nodes', rightward)  42.5 us
    all_to_all x1, waiting for transfers between devices, local(): lax.all_to_all(attended, 'heads', split_axis=0, concat_axis=0, tiled=True)  18 us
    pallas_call x2, Pallas kernels, project(): pl.pallas_call(project_kernel, grid=(rows // step_rows,), in_specs=[pl.Bl...  11.9 us
    pallas_call x1, Pallas kernels, far_terms(): pl.pallas_call(functools.partial(far_kernel, group), in_specs=[smem, smem...  11.3 us
    pallas_call x1, Pallas kernels, near_terms(): pl.pallas_call(functools.partial(near_kernel, group), in_specs=[smem, sme...  10.3 us
    pallas_call x1, Pallas kernels, tail(): pl.pallas_call(tail_kernel, grid_spec=pltpu.PrefetchScalarGridSpec(num_sc...  9.84 us
    all_to_all x1, starting transfers between devices, local(): lax.all_to_all(message, 'nodes', split_axis=0, concat_axis=0, tiled=True)  8.59 us
    all_to_all x1, starting transfers between devices, local(): lax.all_to_all(attended, 'heads', split_axis=0, concat_axis=0, tiled=True)  8.2 us
  transfers between devices with their start and end apart: 7, of which 3 were waited for; matrix products, arithmetic and copies ran while one was open for 8% of the time, Pallas kernels for 24%

profile of v1, /device:TPU:1, one launch (start us, length us, event | category | flops | bytes accessed | tf_op | source)
XLA Modules:
  0.0 165.8 jit_solution(14779690178778847330)
XLA Ops:
  6.5 0.7 all-gather.5.cloned.1.call-update
  7.3 0.8 copy.28
  8.1 0.7 reduce
  9.6 8.6 %all-to-all-start = ((bf16[32,8,128]{2,1,0:T(8,128)(2,1)}), bf16[32,8,128]{2,1,0:T(8,128)(2,1)S(1)}, u32[]{:S(2)}, u32[]{:S(2)}) async-start(bf16[32,8,128]{2,1,0:T(8,128)(2,1)} %broadcast_in_dim.69), calls=%async_computation | async-start | bytes 131072 | tf_op jit(solution)/shard_map/all_to_all | solution.py:325
  18.3 1.8 %copy.30.w_ref = bf16[512,192]{1,0:T(8,128)(2,1)} copy(bf16[512,192]{0,1:T(8,128)(2,1)} %param.15) | data formatting | bytes 393216 | tf_op args[2]
  20.3 9.2 %project.2 = (bf16[64,4096]{1,0:T(8,128)(2,1)}, bf16[32,128,128]{2,1,0:T(8,128)(2,1)}) custom-call(bf16[4096,512]{1,0:T(8,128)(2,1)} %own_ref.1, bf16[512,192]{1,0:T(8,128)(2,1)} %copy.30.w_ref), custom_call_target="tpu_custom_call" | custom-call | tf_op jit(solution)/shard_map/project/pallas_call | solution.py:58
  31.6 5.5 %select_blocks.1 = bf16[128,128,128]{2,1,0:T(8,128)(2,1)} custom-call(s32[128]{0:T(128)} %reshape.243.wanted_ref, bf16[32,128,128]{2,1,0:T(8,128)(2,1)} %get-tuple-element.11.pack_ref), custom_call_target="tpu_custom_call" | custom-call | tf_op jit(solution)/shard_map/select_blocks/pallas_call | solution.py:88
  37.1 7.6 %all-to-all-start.1 = ((bf16[32,512,128]{2,1,0:T(8,128)(2,1)}), bf16[32,512,128]{2,1,0:T(8,128)(2,1)}, u32[]{:S(2)}, u32[]{:S(2)}) async-start(bf16[32,512,128]{2,1,0:T(8,128)(2,1)} %bitcast.18), calls=%async_computation.1 | async-start | bytes 8388608 | tf_op jit(solution)/shard_map/all_to_all | solution.py:347
  44.7 0.7 all-gather.7.cloned.1.call-update
  45.4 1.0 fusion.8
  46.4 1.7 %collective-permute-start = (bf16[128,512]{1,0:T(8,128)(2,1)S(1)}, bf16[128,512]{1,0:T(8,128)(2,1)S(1)}, u32[]{:S(2)}, u32[]{:S(2)}) collective-permute-start(bf16[128,512]{1,0:T(8,128)(2,1)S(1)} %get-tuple-element.17), channel_id=1, source_target_pairs={{0,8},{8,16},{16,24},{24,32},{32,40},{40,48},{48,56},{56,64},{64,7... | collective-permute-start | bytes 393224 | tf_op jit(solution)/shard_map/ppermute | solution.py:328
  49.1 0.7 reshape.247.count_ref
  49.9 0.7 reshape.240.count_ref
  51.5 42.5 %collective-permute-done = bf16[128,512]{1,0:T(8,128)(2,1)S(1)} collective-permute-done((bf16[128,512]{1,0:T(8,128)(2,1)S(1)}, bf16[128,512]{1,0:T(8,128)(2,1)S(1)}, u32[]{:S(2)}, u32[]{:S(2)}) %collective-permute-start) | collective-permute-done | bytes 131104 | tf_op jit(solution)/shard_map/ppermute | solution.py:328
  93.9 1.6 collective-permute-done.1
  95.5 0.9 maximum_maximum_fusion.x_ref
  96.4 2.7 %project.3 = (bf16[64,384]{1,0:T(8,128)(2,1)}, bf16[3,128,128]{2,1,0:T(8,128)(2,1)}) custom-call(bf16[384,512]{1,0:T(8,128)(2,1)} %maximum_maximum_fusion.x_ref, bf16[512,192]{1,0:T(8,128)(2,1)} %copy.30.w_ref), custom_call_target="tpu_custom_call" | custom-call | tf_op jit(solution)/shard_map/project/pallas_call | solution.py:58
  99.1 1.4 slice_bitcast_fusion
  100.5 10.3 %near_terms.1 = (f32[64,4096]{1,0:T(8,128)}, f32[1,4096]{1,0:T(1,128)}) custom-call(s32[128]{0:T(128)} %reshape.246.shift_ref, s32[128]{0:T(128)} %reshape.247.count_ref, bf16[64,4096]{1,0:T(8,128)(2,1)} %get-tuple-element.10.query_ref, bf16[32,128,128]{2,1,0:T(8,128)(2,1)} %get-tuple-element.11.pack_ref, bf16[128,128]{1,0:T(8,128)(2,1)} %get-tuple-element.21.left_ref, ...), custom_call_target="tpu_custom_call" | custom-call | flops 8589934592 | bytes 4194304 | tf_op jit(solution)/shard_map/near_terms/pallas_call | solution.py:176
  110.8 11.3 %far_terms.1 = bf16[8,64,512]{2,1,0:T(8,128)(2,1)} custom-call(s32[128]{0:T(128)} %multiply_add_fusion.slot_ref, s32[128]{0:T(128)} %reshape.240.count_ref, bf16[64,4096]{1,0:T(8,128)(2,1)} %get-tuple-element.10.query_ref, bf16[128,128,128]{2,1,0:T(8,128)(2,1)} %bitcast.3.reply_ref, s32[32,4,128]{2,1,0:T(4,128)} %rows_ref.3, ...), custom_call_target="tpu_custom_call" | custom-call | tf_op jit(solution)/shard_map/far_terms/pallas_call | solution.py:221
  122.1 8.2 %all-to-all-start.2 = ((bf16[8,64,512]{2,1,0:T(8,128)(2,1)}), bf16[8,64,512]{2,1,0:T(8,128)(2,1)S(1)}, u32[]{:S(2)}, u32[]{:S(2)}) async-start(bf16[8,64,512]{2,1,0:T(8,128)(2,1)} %far_terms.1), calls=%async_computation.2 | async-start | bytes 1048576 | tf_op jit(solution)/shard_map/all_to_all | solution.py:398
  130.4 18.0 %all-to-all-done.2.att_ref = bf16[8,64,512]{2,1,0:T(8,128)(2,1)S(1)} async-done(((bf16[8,64,512]{2,1,0:T(8,128)(2,1)}), bf16[8,64,512]{2,1,0:T(8,128)(2,1)S(1)}, u32[]{:S(2)}, u32[]{:S(2)}) %all-to-all-start.2) | async-done | bytes 524320 | tf_op jit(solution)/shard_map/all_to_all | solution.py:398
  148.4 0.8 copy-done
  149.2 9.8 %tail.1 = bf16[512,512]{1,0:T(8,128)(2,1)} custom-call(s32[1]{0:T(128)} %bitcast.place_ref, bf16[8,64,512]{2,1,0:T(8,128)(2,1)} %copy-done, bf16[4096,512]{1,0:T(8,128)(2,1)} %own_ref.1, bf16[512,512]{1,0:T(8,128)(2,1)} %output_ref.1, bf16[8,512,256]{2,1,0:T(8,128)(2,1)} %bitcast.19, f32[8,1,256]{2,1,0:T(1,128)} %bitcast.24, bf16[8,256,512]{2,1,0:T(8,128)(2,1)} %bitcast.20), custom_call_target="tpu_custom_call" | custom-call | tf_op jit(solution)/shard_map/tail/pallas_call | solution.py:260
  (43 shorter events, 5.3 us)
Async XLA Ops:
  6.5 123.8 %all-gather.5.cloned.1.call-start = ((), (), s32[]{:S(2)}) async-start(), calls=%async_computation.3 | async-start | bytes 2359296 | tf_op jit(solution)/shard_map/all_gather | solution.py:331
  9.6 19.9 %all-to-all-start = ((bf16[32,8,128]{2,1,0:T(8,128)(2,1)}), bf16[32,8,128]{2,1,0:T(8,128)(2,1)S(1)}, u32[]{:S(2)}, u32[]{:S(2)}) async-start(bf16[32,8,128]{2,1,0:T(8,128)(2,1)} %broadcast_in_dim.69), calls=%async_computation | async-start | bytes 131072 | tf_op jit(solution)/shard_map/all_to_all | solution.py:325
  37.1 11.1 %copy-start.3 = (s32[32,4]{0,1:T(4,128)S(1)}, s32[32,4]{0,1:T(4,128)}, u32[]{:S(2)}) copy-start(s32[32,4]{0,1:T(4,128)} %param.20) | copy-start | bytes 1540
  37.1 11.9 %copy-start.1 = (s32[32,4]{0,1:T(4,128)S(1)}, s32[32,4]{0,1:T(4,128)}, u32[]{:S(2)}) copy-start(s32[32,4]{0,1:T(4,128)} %param.22) | copy-start | bytes 1540
  37.1 12.7 %copy-start.2 = (s32[32,4]{0,1:T(4,128)S(1)}, s32[32,4]{0,1:T(4,128)}, u32[]{:S(2)}) copy-start(s32[32,4]{0,1:T(4,128)} %param.25) | copy-start | bytes 1540
  37.1 73.7 %all-to-all-start.1 = ((bf16[32,512,128]{2,1,0:T(8,128)(2,1)}), bf16[32,512,128]{2,1,0:T(8,128)(2,1)}, u32[]{:S(2)}, u32[]{:S(2)}) async-start(bf16[32,512,128]{2,1,0:T(8,128)(2,1)} %bitcast.18), calls=%async_computation.1 | async-start | bytes 8388608 | tf_op jit(solution)/shard_map/all_to_all | solution.py:347
  44.7 85.7 %all-gather.7.cloned.1.call-start = ((), (), s32[]{:S(2)}) async-start(), calls=%async_computation.4 | async-start | bytes 2359296 | tf_op jit(solution)/shard_map/all_gather | solution.py:332
  46.4 47.5 %collective-permute-start = (bf16[128,512]{1,0:T(8,128)(2,1)S(1)}, bf16[128,512]{1,0:T(8,128)(2,1)S(1)}, u32[]{:S(2)}, u32[]{:S(2)}) collective-permute-start(bf16[128,512]{1,0:T(8,128)(2,1)S(1)} %get-tuple-element.17), channel_id=1, source_target_pairs={{0,8},{8,16},{16,24},{24,32},{32,40},{40,48},{48,56},{56,64},{64,7... | collective-permute-start | bytes 393224 | tf_op jit(solution)/shard_map/ppermute | solution.py:328
  48.1 47.4 %collective-permute-start.1 = (bf16[128,512]{1,0:T(8,128)(2,1)S(1)}, bf16[128,512]{1,0:T(8,128)(2,1)S(1)}, u32[]{:S(2)}, u32[]{:S(2)}) collective-permute-start(bf16[128,512]{1,0:T(8,128)(2,1)S(1)} %get-tuple-element.18), channel_id=1, source_target_pairs={{8,0},{16,8},{24,16},{32,24},{40,32},{48,40},{56,48},{64,56},{72,6... | collective-permute-start | bytes 393224 | tf_op jit(solution)/shard_map/ppermute | solution.py:329
  122.1 26.2 %all-to-all-start.2 = ((bf16[8,64,512]{2,1,0:T(8,128)(2,1)}), bf16[8,64,512]{2,1,0:T(8,128)(2,1)S(1)}, u32[]{:S(2)}, u32[]{:S(2)}) async-start(bf16[8,64,512]{2,1,0:T(8,128)(2,1)} %far_terms.1), calls=%async_computation.2 | async-start | bytes 1048576 | tf_op jit(solution)/shard_map/all_to_all | solution.py:398
  148.4 0.8 copy-start
Sparse Core Ops, SparseCore 0:
  9.1 41.1 all-gather.4
  52.2 39.5 all-gather.6

commit v2 on v1

v2 whole, which is shorter than its diff:
```python
import functools

import jax
import jax.numpy as jnp
from jax import lax
from jax.experimental import pallas as pl
from jax.experimental.pallas import tpu as pltpu
from jax.sharding import PartitionSpec as P

HEAD_DIM = 64
BCAP = 4

eps_norm = 1e-05
clip_level = 5.0
TAIL = 10
TIGHT = 58

f32 = jnp.float32
bf16 = jnp.bfloat16
def params(mib):
    return pltpu.CompilerParams(vmem_limit_bytes=mib * 2**20)


def layer_norm(values):
    values = values.astype(f32)
    center = values - jnp.mean(values, axis=-1, keepdims=True)
    spread = jnp.mean(center * center, axis=-1, keepdims=True)
    return center * lax.rsqrt(spread + eps_norm)


vmem = pl.BlockSpec(memory_space=pltpu.VMEM)
smem = pl.BlockSpec(memory_space=pltpu.SMEM)


def ask_kernel(source_ref, virtual_ref, out_ref, slot_ref, table_ref):
    tiles, blocks = source_ref.shape
    span, _, lanes = out_ref.shape
    bits = blocks.bit_length() - 1
    source = jnp.concatenate([source_ref[t : t + 1, :] for t in range(tiles)], axis=1)
    across = jnp.broadcast_to(source, (lanes, lanes))
    down = across.T
    up = lax.broadcasted_iota(jnp.int32, (lanes, lanes), 0)
    along = lax.broadcasted_iota(jnp.int32, (lanes, lanes), 1)
    again = jnp.where((across == down) & (along < up), 1.0, 0.0)
    first = jnp.sum(again, axis=1, keepdims=True) == 0.0
    same = lax.shift_right_logical(across, bits) == lax.shift_right_logical(down, bits)
    below = jnp.where(same & (down < across) & first, 1.0, 0.0)
    rank = jnp.sum(below, axis=0, keepdims=True).astype(jnp.int32)
    slot = lax.shift_right_logical(source, bits) * BCAP + rank
    slot_ref[...] = slot
    slot_down = jnp.broadcast_to(slot, (lanes, lanes)).T
    place = jnp.where((slot_down == along) & first, (down & (blocks - 1)).astype(f32), 0.0)
    table_ref[...] = jnp.zeros_like(table_ref)
    table_ref[0:1, :] = jnp.sum(place, axis=0, keepdims=True)
    for part in range(virtual_ref.shape[1] // lanes):
        table_ref[8 + part : 9 + part, :] = virtual_ref[
            :, part * lanes : (part + 1) * lanes
        ].astype(f32)
    table = table_ref[...].astype(bf16)
    for item in range(span):
        out_ref[item] = table


def ask(source, virtual_states, span):
    lanes = 128
    return pl.pallas_call(
        ask_kernel,
        in_specs=[vmem, vmem],
        out_specs=[vmem, vmem],
        out_shape=[
            jax.ShapeDtypeStruct((span, 16, lanes), bf16),
            jax.ShapeDtypeStruct((1, lanes), jnp.int32),
        ],
        scratch_shapes=[pltpu.VMEM((16, lanes), f32)],
        compiler_params=params(56),
        name="ask",
    )(source, virtual_states)


def project_kernel(x_ref, w_ref, query_ref, pack_ref):
    head = HEAD_DIM
    wide = 2 * head
    rows = min(x_ref.shape[0], 512)
    for start in range(0, x_ref.shape[0], rows):
        normed = layer_norm(x_ref[start : start + rows, :]).astype(bf16)
        sides = lax.dot_general(
            w_ref[...], normed, (((1,), (1,)), ((), ())), preferred_element_type=f32
        ).astype(bf16)
        query_ref[:, start : start + rows] = sides[:head] * jnp.asarray(head**-0.5, bf16)
        for item in range(rows // wide):
            pack_ref[start // wide + item] = sides[head:, item * wide : (item + 1) * wide]


def project(states, weight_t, step_rows, mib):
    rows, features = states.shape
    wide = 2 * HEAD_DIM
    return pl.pallas_call(
        project_kernel,
        grid=(rows // step_rows,),
        in_specs=[
            pl.BlockSpec((step_rows, features), lambda i: (i, 0)),
            pl.BlockSpec(weight_t.shape, lambda i: (0, 0)),
        ],
        out_specs=[
            pl.BlockSpec((HEAD_DIM, step_rows), lambda i: (0, i)),
            pl.BlockSpec((step_rows // wide, wide, wide), lambda i: (i, 0, 0)),
        ],
        out_shape=[
            jax.ShapeDtypeStruct((HEAD_DIM, rows), bf16),
            jax.ShapeDtypeStruct((rows // wide, wide, wide), bf16),
        ],
        compiler_params=params(mib),
        name="project",
    )(states, weight_t)


def select_kernel(
    me_ref, heard_ref, pack_ref, out_ref, heard_buf, pack_buf, table_ref, place_ref, copy_sem, sems
):
    span = heard_ref.shape[0]
    fetch_pack = pltpu.make_async_copy(pack_ref, pack_buf, sems.at[0])
    fetch_heard = pltpu.make_async_copy(heard_ref, heard_buf, sems.at[1])
    fetch_heard.start()
    fetch_pack.start()
    fetch_heard.wait()
    table_ref[...] = heard_buf[:, 0, :].astype(f32).astype(jnp.int32)
    fetch_place = pltpu.make_async_copy(table_ref, place_ref, sems.at[2])
    fetch_place.start()
    fetch_place.wait()
    fetch_pack.wait()
    base = me_ref[0] * BCAP

    def send(item, _):
        for slot in range(BCAP):
            pltpu.make_async_copy(
                pack_buf.at[place_ref[item, base + slot]],
                out_ref.at[item * BCAP + slot],
                copy_sem,
            ).start()
        return 0

    lax.fori_loop(0, span, send, 0, unroll=2)
    pltpu.make_async_copy(out_ref, out_ref, copy_sem).wait()


def select_blocks(me, heard, packed):
    span, _, lanes = heard.shape
    anywhere = pl.BlockSpec(memory_space=pl.ANY)
    return pl.pallas_call(
        select_kernel,
        in_specs=[smem, anywhere, anywhere],
        out_specs=anywhere,
        out_shape=jax.ShapeDtypeStruct((span * BCAP,) + packed.shape[1:], bf16),
        scratch_shapes=[
            pltpu.VMEM(heard.shape, bf16),
            pltpu.VMEM(packed.shape, bf16),
            pltpu.VMEM((span, lanes), jnp.int32),
            pltpu.SMEM((span, lanes), jnp.int32),
            pltpu.SemaphoreType.DMA,
            pltpu.SemaphoreType.DMA((3,)),
        ],
        compiler_params=params(TIGHT),
        name="select_blocks",
    )(me, heard, packed)


def tile_terms(query, blocks, rows, counts):
    head = HEAD_DIM
    wide = 2 * head
    lane = lax.broadcasted_iota(jnp.int32, (1, wide), 1)
    spot = lax.broadcasted_iota(jnp.int32, (wide, wide), 0)
    summed, total = None, None
    for block, row, count in zip(blocks, rows, counts):
        pick = jnp.where(spot == row, 1.0, 0.0).astype(bf16)
        pairs = jnp.dot(block, pick, preferred_element_type=f32)
        score = jnp.sum(pairs[:head] * query, axis=0, keepdims=True)
        weight = jnp.exp(jnp.clip(score, -clip_level, clip_level))
        weight = jnp.where(lane < count, weight, 0.0)
        value = pairs[head:] * weight
        summed = value if summed is None else summed + value
        total = weight if total is None else total + weight
    return summed, total


def tile_rows(rows_ref, block):
    rows = rows_ref[block]
    return [rows[tile : tile + 1] for tile in range(rows.shape[0])]


def near_kernel(
    group, place_ref, count_ref, query_ref, pack_ref, virtual_ref, rows_ref, sum_ref, total_ref
):
    head = HEAD_DIM
    blocks, tiles, wide = rows_ref.shape
    virtual_total = 32
    virtual_keys = virtual_ref[0, :head, :].T[:virtual_total]
    virtual_values = virtual_ref[0, head:, :virtual_total]

    def step(turn, _):
        for item in range(group):
            block = turn * group + item
            lanes = pl.ds(pl.multiple_of(block * wide, wide), wide)
            query = query_ref[:, lanes]
            tile_blocks = [pack_ref[place_ref[block * tiles + t]] for t in range(tiles)]
            counts = [count_ref[block * tiles + t] for t in range(tiles)]
            summed, total = tile_terms(
                query.astype(f32), tile_blocks, tile_rows(rows_ref, block), counts
            )
            scores = jnp.dot(virtual_keys, query, preferred_element_type=f32)
            weights = jnp.exp(jnp.clip(scores, -clip_level, clip_level))
            total = total + jnp.sum(weights, axis=0, keepdims=True)
            summed = summed + jnp.dot(
                virtual_values, weights.astype(bf16), preferred_element_type=f32
            )
            sum_ref[:, lanes] = summed
            total_ref[:, lanes] = total
        return 0

    lax.fori_loop(0, blocks // group, step, 0)


def near_terms(places, counts, query, packed, virtual, rows, group):
    head, total = query.shape
    return pl.pallas_call(
        functools.partial(near_kernel, group),
        in_specs=[smem, smem] + [vmem] * 4,
        out_specs=[vmem, vmem],
        out_shape=[
            jax.ShapeDtypeStruct((head, total), f32),
            jax.ShapeDtypeStruct((1, total), f32),
        ],
        compiler_params=params(TIGHT),
        cost_estimate=pl.CostEstimate(
            flops=8 * 2**30, bytes_accessed=4 * 2**20, transcendentals=2**20
        ),
        name="near_terms",
    )(places, counts, query, packed, virtual, rows)


def far_kernel(
    group, slot_ref, count_ref, edge_ref, query_ref, reply_ref, rows_ref, left_ref, right_ref,
    edge_rows_ref, sum_ref, total_ref, out_ref,
):
    blocks, tiles, wide = rows_ref.shape
    share_blocks = blocks // out_ref.shape[0]

    def one(block, more_blocks=(), more_rows=(), more_counts=()):
        lanes = pl.ds(pl.multiple_of(block * wide, wide), wide)
        tile_blocks = [reply_ref[slot_ref[0, t * blocks + block]] for t in range(tiles)]
        counts = [count_ref[block * tiles + t] for t in range(tiles)]
        summed, total = tile_terms(
            query_ref[:, lanes].astype(f32),
            tile_blocks + list(more_blocks),
            tile_rows(rows_ref, block) + list(more_rows),
            counts + list(more_counts),
        )
        total = total + total_ref[:, lanes]
        result = (summed + sum_ref[:, lanes]) * (1.0 / total)
        inner = pl.ds(pl.multiple_of(lax.rem(block, share_blocks) * wide, wide), wide)
        out_ref[lax.div(block, share_blocks), :, inner] = result.astype(bf16)

    near_tiles = edge_rows_ref.shape[1]
    for end, halo_ref in enumerate((left_ref, right_ref)):
        one(
            jnp.int32(end * (blocks - 1)),
            [halo_ref[0]] * near_tiles,
            tile_rows(edge_rows_ref, end),
            [edge_ref[end * near_tiles + t] for t in range(near_tiles)],
        )

    def step(turn, _):
        for item in range(group):
            one(1 + turn * group + item)
        return 0

    lax.fori_loop(0, (blocks - 2) // group, step, 0)


def far_terms(
    slots, counts, edges, query, replies, rows, left, right, edge_rows, near_sum, near_total, shares,
    group,
):
    head, total = query.shape
    return pl.pallas_call(
        functools.partial(far_kernel, group),
        in_specs=[smem] * 3 + [vmem] * 8,
        out_specs=vmem,
        out_shape=jax.ShapeDtypeStruct((shares, head, total // shares), bf16),
        compiler_params=params(TIGHT),
        name="far_terms",
    )(slots, counts, edges, query, replies, rows, left, right, edge_rows, near_sum, near_total)


def piece_kernel(core_ref, expand_ref, contract_ref, out_ref):
    wide = out_ref.shape[0] // 2
    for core in range(2):

        @pl.when(core_ref[0] == core)
        def _():
            span = slice(core * wide, (core + 1) * wide)
            out_ref[:wide] = expand_ref[:, span].T
            out_ref[wide:] = contract_ref[span, :]


def weight_piece(core, expand, contract):
    features, width = expand.shape
    return pl.pallas_call(
        piece_kernel,
        in_specs=[smem, vmem, vmem],
        out_specs=vmem,
        out_shape=jax.ShapeDtypeStruct((width, features), bf16),
        compiler_params=params(16),
        name="weight_piece",
    )(core, expand, contract)


def tail_kernel(
    offsets, place_ref, att_ref, own_ref, output_ref, mine_ref, theirs_ref, bias_ref, out_ref
):
    heads, head, rows = att_ref.shape
    features = heads * head
    parts = len(offsets)
    wide = mine_ref.shape[1] // 2
    attended = att_ref[...].reshape(features, rows).T
    residual = own_ref[...].astype(f32) + jnp.dot(
        attended, output_ref[...], preferred_element_type=f32
    )
    normed = layer_norm(residual).astype(bf16)
    summed = residual
    for part, offset in enumerate(offsets):
        owner = lax.rem(place_ref[0] + offset + parts, parts)
        bias = jnp.concatenate(
            [bias_ref[2 * owner + place_ref[1]], bias_ref[2 * owner + 1 - place_ref[1]]], axis=1
        )
        first = jnp.concatenate([mine_ref[part, :wide], theirs_ref[part, :wide]], axis=0)
        second = jnp.concatenate([mine_ref[part, wide:], theirs_ref[part, wide:]], axis=0)
        inner = lax.dot_general(
            normed, first, (((1,), (1,)), ((), ())), preferred_element_type=f32
        )
        inner = inner + bias
        hidden = ((inner * 0.5) * (1.0 + lax.erf(inner * (0.5**0.5)))).astype(bf16)
        summed = summed + jnp.dot(hidden, second, preferred_element_type=f32)
    out_ref[...] = summed.astype(bf16)


def tail(place, regrouped, own, output_weight, mine, theirs, bias, offsets):
    return pl.pallas_call(
        functools.partial(tail_kernel, offsets),
        in_specs=[smem] + [vmem] * 6,
        out_specs=vmem,
        out_shape=jax.ShapeDtypeStruct(own.shape, bf16),
        compiler_params=params(TAIL),
        name="tail",
    )(place, regrouped, own, output_weight, mine, theirs, bias)


def local(
    node_states,
    virtual_states,
    project_weight,
    output_weight,
    expand_weight,
    expand_bias,
    contract_weight,
    neigh_source,
    neigh_rows,
    neigh_count,
    expander_source,
    expander_rows,
    expander_count,
):
    span = lax.axis_size("nodes")
    me = lax.axis_index("nodes").astype(jnp.int32)
    shares = lax.axis_size("heads")
    share = lax.axis_index("heads").astype(jnp.int32)
    core = jnp.bitwise_and(me, 1)
    blocks, neigh_tiles, block_rows = neigh_rows.shape
    rows, features = node_states.shape
    all_blocks = blocks * span
    lanes = 128
    barrier = lax.optimization_barrier

    message, slots = ask(expander_source.T, virtual_states, span)
    heard = lax.all_to_all(message, "nodes", split_axis=0, concat_axis=0, tiled=True)
    weight_t = project_weight.T
    query, packed = project(node_states, weight_t, rows // 2, TIGHT)
    chosen = select_blocks(me.reshape(1), heard, packed)
    replies = lax.all_to_all(
        chosen.reshape(span, BCAP * block_rows, lanes),
        "nodes",
        split_axis=0,
        concat_axis=0,
        tiled=True,
    ).reshape(span * BCAP, block_rows, lanes)

    heard, chosen = barrier((heard, chosen))
    extra = jnp.concatenate(
        [
            heard[:, 8 : 8 + features // lanes].reshape(span, features),
            jnp.zeros((block_rows - span, features), bf16),
        ],
        axis=0,
    )
    _, virtual_packed = project(extra, weight_t, extra.shape[0], 16)
    local_ids = jnp.arange(blocks, dtype=jnp.int32)[:, None]
    global_ids = me * blocks + local_ids
    place = jnp.mod(neigh_source - global_ids + 1, all_blocks) + local_ids - 1
    inside = (place >= 0) & (place < blocks)
    near_count = jnp.where(inside, neigh_count, 0)
    edge_count = jnp.where(inside, 0, neigh_count)
    near_sum, near_total = near_terms(
        jnp.clip(place, 0, blocks - 1).reshape(-1),
        near_count.reshape(-1),
        query,
        packed,
        virtual_packed,
        neigh_rows,
        4,
    )

    half = expand_weight.shape[1] // 2
    piece = weight_piece(core.reshape(1), expand_weight, contract_weight)
    piece, virtual_packed = barrier((piece, virtual_packed))
    upward = [(i, (i + 1) % shares) for i in range(shares)]
    downward = [((i + 1) % shares, i) for i in range(shares)]
    pieces, offsets = [piece], [0]
    above, below = piece, piece
    for step in range(1, shares // 2 + 1):
        below = lax.ppermute(below, "heads", upward)
        if step == 1:
            below, near_total = barrier((below, near_total))
        pieces.append(below)
        offsets.append(-step)
        if step < shares // 2:
            above = lax.ppermute(above, "heads", downward)
            pieces.append(above)
            offsets.append(step)
    mine = jnp.stack(pieces)
    theirs = lax.ppermute(mine, "nodes", [(i, i ^ 1) for i in range(span)])

    first_block, last_block, virtual_packed = barrier((packed[:1], packed[-1:], virtual_packed))
    left = lax.ppermute(last_block, "nodes", [(i, (i + 1) % span) for i in range(span)])
    right = lax.ppermute(first_block, "nodes", [((i + 1) % span, i) for i in range(span)])

    edge_rows = jnp.concatenate([neigh_rows[:1], neigh_rows[-1:]], axis=0)
    attended = far_terms(
        slots,
        expander_count.reshape(-1),
        jnp.concatenate([edge_count[0], edge_count[-1]]),
        query,
        replies,
        expander_rows,
        left,
        right,
        edge_rows,
        near_sum,
        near_total,
        shares,
        10,
    )
    own = lax.dynamic_slice_in_dim(node_states, share * (rows // shares), rows // shares, 0)
    attended, own, mine = barrier((attended, own, mine))
    regrouped = lax.all_to_all(attended, "heads", split_axis=0, concat_axis=0, tiled=True)
    return tail(
        jnp.stack([share, core]),
        regrouped,
        own,
        output_weight,
        mine,
        theirs,
        expand_bias.reshape(2 * shares, 1, half),
        tuple(offsets),
    )


def solution(mesh):
    return jax.shard_map(
        local,
        mesh=mesh,
        in_specs=(
            P("nodes", None),
            P("nodes", None),
            P(None, "heads"),
            P(),
            P(None, "heads"),
            P(),
            P("heads", None),
            P("nodes", None),
            P("nodes", None, None),
            P("nodes", None),
            P("nodes", None),
            P("nodes", None, None),
            P("nodes", None),
        ),
        out_specs=P(("nodes", "heads"), None),
        check_vma=False,
    )
```

time: 167 us -> 120 us (0.72)
  the two profiles are of different devices: /device:TPU:1 before, /device:TPU:8 now
where the time goes in v2:
time: 120 us
  waiting for transfers between devices  42.9 us (36%)
  starting transfers between devices  37 us (31%)
  Pallas kernels  29.9 us (25%)
  local copies, waits for them, and re-layouts  8.26 us (7%)
  other arithmetic  1.31 us (1%)
    ppermute x4, waiting for transfers between devices, local(): below = lax.ppermute(below, 'heads', upward)  18.6 us
    all_to_all x1, waiting for transfers between devices, local(): lax.all_to_all(attended, 'heads', split_axis=0, concat_axis=0, tiled=True)  17.2 us
    ppermute x3, starting transfers between devices, local(): above = lax.ppermute(above, 'heads', downward)  10.6 us
    all_to_all x1, starting transfers between devices, local(): lax.all_to_all(attended, 'heads', split_axis=0, concat_axis=0, tiled=True)  8.46 us
    all_to_all x1, starting transfers between devices, local(): lax.all_to_all(message, 'nodes', split_axis=0, concat_axis=0, tiled=True)  7.53 us
    all_to_all x1, starting transfers between devices, local(): lax.all_to_all(chosen.reshape(span, BCAP * block_rows, lanes), 'nodes', s...  6.73 us
    pallas_call x2, Pallas kernels, project(): pl.pallas_call(project_kernel, grid=(rows // step_rows,), in_specs=[pl.Bl...  6.61 us
    pallas_call x1, Pallas kernels, near_terms(): pl.pallas_call(functools.partial(near_kernel, group), in_specs=[smem, sme...  6.43 us
  transfers between devices with their start and end apart: 13, of which 7 were waited for; matrix products, arithmetic and copies ran while one was open for 6% of the time, Pallas kernels for 16%

profile of v2, /device:TPU:8, one launch (start us, length us, event | category | flops | bytes accessed | tf_op | source)
XLA Modules:
  0.0 119.7 jit_solution(13750831884125508465)
XLA Ops:
  0.0 1.7 %ask.1 = (bf16[32,16,128]{2,1,0:T(8,128)(2,1)}, s32[1,128]{1,0:T(1,128)}) custom-call(s32[4,32]{1,0:T(4,128)} %bitcast.34, bf16[1,512]{1,0:T(2,128)(2,1)} %virtual_ref.1), custom_call_target="tpu_custom_call" | custom-call | tf_op jit(solution)/shard_map/ask/pallas_call | solution.py:66
  1.7 7.5 %all-to-all-start = ((bf16[32,16,128]{2,1,0:T(8,128)(2,1)}), bf16[32,16,128]{2,1,0:T(8,128)(2,1)S(1)}, u32[]{:S(2)}, u32[]{:S(2)}) async-start(bf16[32,16,128]{2,1,0:T(8,128)(2,1)} %get-tuple-element.23), calls=%async_computation | async-start | bytes 262144 | tf_op jit(solution)/shard_map/all_to_all | solution.py:384
  9.3 5.7 %project.2 = (bf16[64,4096]{1,0:T(8,128)(2,1)}, bf16[32,128,128]{2,1,0:T(8,128)(2,1)}) custom-call(bf16[4096,512]{1,0:T(8,128)(2,1)} %x_ref.1, bf16[192,512]{1,0:T(8,128)(2,1)} %bitcast.28), custom_call_target="tpu_custom_call" | custom-call | tf_op jit(solution)/shard_map/project/pallas_call | solution.py:97
  15.0 0.9 all-to-all-done.heard_ref
  16.5 3.8 %select_blocks.1 = bf16[128,128,128]{2,1,0:T(8,128)(2,1)} custom-call(s32[1]{0:T(128)} %bitcast.4.me_ref, bf16[32,16,128]{2,1,0:T(8,128)(2,1)} %copy-done.6, bf16[32,128,128]{2,1,0:T(8,128)(2,1)} %get-tuple-element.24.pack_ref), custom_call_target="tpu_custom_call" | custom-call | tf_op jit(solution)/shard_map/select_blocks/pallas_call | solution.py:149
  20.4 6.7 %all-to-all-start.1 = ((bf16[32,512,128]{2,1,0:T(8,128)(2,1)}), bf16[32,512,128]{2,1,0:T(8,128)(2,1)}, u32[]{:S(2)}, u32[]{:S(2)}) async-start(bf16[32,512,128]{2,1,0:T(8,128)(2,1)} %bitcast.31), calls=%async_computation.1 | async-start | bytes 8388608 | tf_op jit(solution)/shard_map/all_to_all | solution.py:388
  28.7 0.9 slice.27
  29.6 0.9 project.3
  31.2 1.9 %collective-permute-start.2 = (bf16[256,512]{1,0:T(8,128)(2,1)S(1)}, bf16[256,512]{1,0:T(8,128)(2,1)S(1)}, u32[]{:S(2)}, u32[]{:S(2)}) collective-permute-start(bf16[256,512]{1,0:T(8,128)(2,1)S(1)} %weight_piece.1), channel_id=1, source_target_pairs={{0,1},{1,2},{2,3},{3,4},{4,5},{5,6},{6,7},{7,0},{8,9},{9,10},{10,1... | collective-permute-start | bytes 786440 | tf_op jit(solution)/shard_map/ppermute | solution.py:429
  33.1 3.9 %collective-permute-start.3 = (bf16[256,512]{1,0:T(8,128)(2,1)S(1)}, bf16[256,512]{1,0:T(8,128)(2,1)S(1)}, u32[]{:S(2)}, u32[]{:S(2)}) collective-permute-start(bf16[256,512]{1,0:T(8,128)(2,1)S(1)} %weight_piece.1), channel_id=1, source_target_pairs={{1,0},{2,1},{3,2},{4,3},{5,4},{6,5},{7,6},{0,7},{9,8},{10,9},{11,1... | collective-permute-start | bytes 786440 | tf_op jit(solution)/shard_map/ppermute | solution.py:435
  37.0 6.4 %near_terms.1 = (f32[64,4096]{1,0:T(8,128)}, f32[1,4096]{1,0:T(1,128)}) custom-call(s32[128]{0:T(128)} %reshape.34.place_ref, s32[128]{0:T(128)} %reshape.35.count_ref, bf16[64,4096]{1,0:T(8,128)(2,1)} %get-tuple-element.22.query_ref, bf16[32,128,128]{2,1,0:T(8,128)(2,1)} %get-tuple-element.24.pack_ref, bf16[1,128,128]{2,1,0:T(8,128)(2,1)} %copy-done.5, ...), custom_call_target="tpu_custom_call" | custom-call | flops 8589934592 | bytes 4194304 | tf_op jit(solution)/shard_map/near_terms/pallas_call | solution.py:224
  43.7 3.3 %collective-permute-start.5 = (bf16[256,512]{1,0:T(8,128)(2,1)S(1)}, bf16[256,512]{1,0:T(8,128)(2,1)S(1)}, u32[]{:S(2)}, u32[]{:S(2)}) collective-permute-start(bf16[256,512]{1,0:T(8,128)(2,1)S(1)} %collective-permute-done.3), channel_id=1, source_target_pairs={{1,0},{2,1},{3,2},{4,3},{5,4},{6,5},{7,6},{0,7},{9,8},{10,9},{11,1... | collective-permute-start | bytes 786440 | tf_op jit(solution)/shard_map/ppermute | solution.py:435
  47.0 5.8 %collective-permute-done.4 = bf16[256,512]{1,0:T(8,128)(2,1)S(1)} collective-permute-done((bf16[256,512]{1,0:T(8,128)(2,1)S(1)}, bf16[256,512]{1,0:T(8,128)(2,1)S(1)}, u32[]{:S(2)}, u32[]{:S(2)}) %collective-permute-start.4) | collective-permute-done | bytes 262176 | tf_op jit(solution)/shard_map/ppermute | solution.py:429
  52.9 3.3 %collective-permute-start.7 = (bf16[256,512]{1,0:T(8,128)(2,1)S(1)}, bf16[256,512]{1,0:T(8,128)(2,1)S(1)}, u32[]{:S(2)}, u32[]{:S(2)}) collective-permute-start(bf16[256,512]{1,0:T(8,128)(2,1)S(1)} %collective-permute-done.5), channel_id=1, source_target_pairs={{1,0},{2,1},{3,2},{4,3},{5,4},{6,5},{7,6},{0,7},{9,8},{10,9},{11,1... | collective-permute-start | bytes 786440 | tf_op jit(solution)/shard_map/ppermute | solution.py:435
  56.2 5.1 %collective-permute-done.6 = bf16[256,512]{1,0:T(8,128)(2,1)S(1)} collective-permute-done((bf16[256,512]{1,0:T(8,128)(2,1)S(1)}, bf16[256,512]{1,0:T(8,128)(2,1)S(1)}, u32[]{:S(2)}, u32[]{:S(2)}) %collective-permute-start.6) | collective-permute-done | bytes 262176 | tf_op jit(solution)/shard_map/ppermute | solution.py:429
  61.3 7.6 %collective-permute-done.8 = bf16[256,512]{1,0:T(8,128)(2,1)S(1)} collective-permute-done((bf16[256,512]{1,0:T(8,128)(2,1)S(1)}, bf16[256,512]{1,0:T(8,128)(2,1)S(1)}, u32[]{:S(2)}, u32[]{:S(2)}) %collective-permute-start.8) | collective-permute-done | bytes 262176 | tf_op jit(solution)/shard_map/ppermute | solution.py:429
  70.3 1.3 %collective-permute-start.1 = (bf16[1,128,128]{2,1,0:T(8,128)(2,1)S(1)}, bf16[1,128,128]{2,1,0:T(8,128)(2,1)S(1)}, u32[]{:S(2)}, u32[]{:S(2)}) collective-permute-start(bf16[1,128,128]{2,1,0:T(8,128)(2,1)S(1)} %get-tuple-element.26), channel_id=1, source_target_pairs={{8,0},{16,8},{24,16},{32,24},{40,32},{48,40},{56,48},{64,56},{72,6... | collective-permute-start | bytes 98312 | tf_op jit(solution)/shard_map/ppermute | solution.py:443
  73.0 1.1 constant_dynamic-slice_fusion.own_ref
  75.4 6.2 %all-to-all-done.1 = bf16[32,512,128]{2,1,0:T(8,128)(2,1)} async-done(((bf16[32,512,128]{2,1,0:T(8,128)(2,1)}), bf16[32,512,128]{2,1,0:T(8,128)(2,1)}, u32[]{:S(2)}, u32[]{:S(2)}) %all-to-all-start.1) | async-done | bytes 4194336 | tf_op jit(solution)/shard_map/all_to_all | solution.py:388
  81.6 5.7 %far_terms.1 = bf16[8,64,512]{2,1,0:T(8,128)(2,1)} custom-call(s32[1,128]{1,0:T(1,128)} %get-tuple-element.21.slot_ref, s32[128]{0:T(128)} %reshape.30.count_ref, s32[8]{0:T(128)} %pad_add_fusion.2.edge_ref, bf16[64,4096]{1,0:T(8,128)(2,1)} %get-tuple-element.22.query_ref, bf16[128,128,128]{2,1,0:T(8,128)(2,1)} %bitcast.6.reply_ref, s32[32,4,128]{2,1,0:T(4,128)} %rows_ref.3, ...), custom_call_target="tpu_custom_call" | custom-call | tf_op jit(solution)/shard_map/far_terms/pallas_call | solution.py:284
  87.4 8.5 %all-to-all-start.2 = ((bf16[8,64,512]{2,1,0:T(8,128)(2,1)}), bf16[8,64,512]{2,1,0:T(8,128)(2,1)S(1)}, u32[]{:S(2)}, u32[]{:S(2)}) async-start(bf16[8,64,512]{2,1,0:T(8,128)(2,1)} %far_terms.1), calls=%async_computation.2 | async-start | bytes 1048576 | tf_op jit(solution)/shard_map/all_to_all | solution.py:463
  95.9 17.2 %all-to-all-done.2.att_ref = bf16[8,64,512]{2,1,0:T(8,128)(2,1)S(1)} async-done(((bf16[8,64,512]{2,1,0:T(8,128)(2,1)}), bf16[8,64,512]{2,1,0:T(8,128)(2,1)S(1)}, u32[]{:S(2)}, u32[]{:S(2)}) %all-to-all-start.2) | async-done | bytes 524320 | tf_op jit(solution)/shard_map/all_to_all | solution.py:463
  113.1 1.0 copy-done.1
  114.2 5.6 %tail.1 = bf16[512,512]{1,0:T(8,128)(2,1)} custom-call(s32[2]{0:T(128)S(1)} %pad_add_fusion.1.place_ref, bf16[8,64,512]{2,1,0:T(8,128)(2,1)S(1)} %all-to-all-done.2.att_ref, bf16[512,512]{1,0:T(8,128)(2,1)S(1)} %constant_dynamic-slice_fusion.own_ref, bf16[512,512]{1,0:T(8,128)(2,1)S(1)} %copy-done.1, ...), custom_call_target="tpu_custom_call" | custom-call | tf_op jit(solution)/shard_map/tail/pallas_call | solution.py:347
  (61 shorter events, 7.4 us)
Async XLA Ops:
  1.7 14.1 %all-to-all-start = ((bf16[32,16,128]{2,1,0:T(8,128)(2,1)}), bf16[32,16,128]{2,1,0:T(8,128)(2,1)S(1)}, u32[]{:S(2)}, u32[]{:S(2)}) async-start(bf16[32,16,128]{2,1,0:T(8,128)(2,1)} %get-tuple-element.23), calls=%async_computation | async-start | bytes 262144 | tf_op jit(solution)/shard_map/all_to_all | solution.py:384
  9.3 5.7 %copy-start.9 = (s32[32,4]{0,1:T(4,128)S(1)}, s32[32,4]{0,1:T(4,128)}, u32[]{:S(2)}) copy-start(s32[32,4]{0,1:T(4,128)} %param.22) | copy-start | bytes 1540
  9.3 5.7 %copy-start.11 = (s32[32,4]{0,1:T(4,128)S(1)}, s32[32,4]{0,1:T(4,128)}, u32[]{:S(2)}) copy-start(s32[32,4]{0,1:T(4,128)} %param.20) | copy-start | bytes 1540
  15.9 0.7 copy-start.6
  20.3 8.3 %copy-start.2 = (bf16[512,256]{1,0:T(8,128)(2,1)S(1)}, bf16[512,256]{1,0:T(8,128)(2,1)}, u32[]{:S(2)}) copy-start(bf16[512,256]{1,0:T(8,128)(2,1)} %expand_ref.1) | copy-start | bytes 786436
  20.3 8.3 %copy-start.3 = (bf16[256,512]{1,0:T(8,128)(2,1)S(1)}, bf16[256,512]{1,0:T(8,128)(2,1)}, u32[]{:S(2)}) copy-start(bf16[256,512]{1,0:T(8,128)(2,1)} %contract_ref.1) | copy-start | bytes 786436
  20.4 9.2 %copy-start = (bf16[512,192]{0,1:T(8,128)(2,1)S(1)}, bf16[512,192]{0,1:T(8,128)(2,1)}, u32[]{:S(2)}) copy-start(bf16[512,192]{0,1:T(8,128)(2,1)} %param.15) | copy-start | bytes 589828
  20.4 61.3 %all-to-all-start.1 = ((bf16[32,512,128]{2,1,0:T(8,128)(2,1)}), bf16[32,512,128]{2,1,0:T(8,128)(2,1)}, u32[]{:S(2)}, u32[]{:S(2)}) async-start(bf16[32,512,128]{2,1,0:T(8,128)(2,1)} %bitcast.31), calls=%async_computation.1 | async-start | bytes 8388608 | tf_op jit(solution)/shard_map/all_to_all | solution.py:388
  31.2 12.5 %collective-permute-start.2 = (bf16[256,512]{1,0:T(8,128)(2,1)S(1)}, bf16[256,512]{1,0:T(8,128)(2,1)S(1)}, u32[]{:S(2)}, u32[]{:S(2)}) collective-permute-start(bf16[256,512]{1,0:T(8,128)(2,1)S(1)} %weight_piece.1), channel_id=1, source_target_pairs={{0,1},{1,2},{2,3},{3,4},{4,5},{5,6},{6,7},{7,0},{8,9},{9,10},{10,1... | collective-permute-start | bytes 786440 | tf_op jit(solution)/shard_map/ppermute | solution.py:429
  33.1 10.6 %collective-permute-start.3 = (bf16[256,512]{1,0:T(8,128)(2,1)S(1)}, bf16[256,512]{1,0:T(8,128)(2,1)S(1)}, u32[]{:S(2)}, u32[]{:S(2)}) collective-permute-start(bf16[256,512]{1,0:T(8,128)(2,1)S(1)} %weight_piece.1), channel_id=1, source_target_pairs={{1,0},{2,1},{3,2},{4,3},{5,4},{6,5},{7,6},{0,7},{9,8},{10,9},{11,1... | collective-permute-start | bytes 786440 | tf_op jit(solution)/shard_map/ppermute | solution.py:435
  43.6 9.2 %collective-permute-start.4 = (bf16[256,512]{1,0:T(8,128)(2,1)S(1)}, bf16[256,512]{1,0:T(8,128)(2,1)S(1)}, u32[]{:S(2)}, u32[]{:S(2)}) collective-permute-start(bf16[256,512]{1,0:T(8,128)(2,1)S(1)} %collective-permute-done.2), channel_id=1, source_target_pairs={{0,1},{1,2},{2,3},{3,4},{4,5},{5,6},{6,7},{7,0},{8,9},{9,10},{10,1... | collective-permute-start | bytes 786440 | tf_op jit(solution)/shard_map/ppermute | solution.py:429
  43.6 31.1 %copy-start.10 = (s32[32,4]{0,1:T(4,128)S(1)}, s32[32,4]{0,1:T(4,128)}, u32[]{:S(2)}) copy-start(s32[32,4]{0,1:T(4,128)} %param.25) | copy-start | bytes 1540
  43.7 9.2 %collective-permute-start.5 = (bf16[256,512]{1,0:T(8,128)(2,1)S(1)}, bf16[256,512]{1,0:T(8,128)(2,1)S(1)}, u32[]{:S(2)}, u32[]{:S(2)}) collective-permute-start(bf16[256,512]{1,0:T(8,128)(2,1)S(1)} %collective-permute-done.3), channel_id=1, source_target_pairs={{1,0},{2,1},{3,2},{4,3},{5,4},{6,5},{7,6},{0,7},{9,8},{10,9},{11,1... | collective-permute-start | bytes 786440 | tf_op jit(solution)/shard_map/ppermute | solution.py:435
  52.8 8.4 %collective-permute-start.6 = (bf16[256,512]{1,0:T(8,128)(2,1)S(1)}, bf16[256,512]{1,0:T(8,128)(2,1)S(1)}, u32[]{:S(2)}, u32[]{:S(2)}) collective-permute-start(bf16[256,512]{1,0:T(8,128)(2,1)S(1)} %collective-permute-done.4), channel_id=1, source_target_pairs={{0,1},{1,2},{2,3},{3,4},{4,5},{5,6},{6,7},{7,0},{8,9},{9,10},{10,1... | collective-permute-start | bytes 786440 | tf_op jit(solution)/shard_map/ppermute | solution.py:429
  52.9 8.4 %collective-permute-start.7 = (bf16[256,512]{1,0:T(8,128)(2,1)S(1)}, bf16[256,512]{1,0:T(8,128)(2,1)S(1)}, u32[]{:S(2)}, u32[]{:S(2)}) collective-permute-start(bf16[256,512]{1,0:T(8,128)(2,1)S(1)} %collective-permute-done.5), channel_id=1, source_target_pairs={{1,0},{2,1},{3,2},{4,3},{5,4},{6,5},{7,6},{0,7},{9,8},{10,9},{11,1... | collective-permute-start | bytes 786440 | tf_op jit(solution)/shard_map/ppermute | solution.py:435
  61.3 7.6 %collective-permute-start.8 = (bf16[256,512]{1,0:T(8,128)(2,1)S(1)}, bf16[256,512]{1,0:T(8,128)(2,1)S(1)}, u32[]{:S(2)}, u32[]{:S(2)}) collective-permute-start(bf16[256,512]{1,0:T(8,128)(2,1)S(1)} %collective-permute-done.6), channel_id=1, source_target_pairs={{0,1},{1,2},{2,3},{3,4},{4,5},{5,6},{6,7},{7,0},{8,9},{9,10},{10,1... | collective-permute-start | bytes 786440 | tf_op jit(solution)/shard_map/ppermute | solution.py:429
  68.9 27.0 %collective-permute-start.9 = (bf16[8,256,512]{2,1,0:T(8,128)(2,1)S(1)}, bf16[8,256,512]{2,1,0:T(8,128)(2,1)}, u32[]{:S(2)}, u32[]{:S(2)}) collective-permute-start(bf16[8,256,512]{2,1,0:T(8,128)(2,1)S(1)} %bitcast_dynamic-update-slice_fusion.mine_ref), channel_id=1, source_target_pairs={{0,8},{8,0},{16,24},{24,16},{32,40},{40,32},{48,56},{56,48},{64,72... | collective-permute-start | bytes 6291464 | tf_op jit(solution)/shard_map/ppermute | solution.py:439
  69.8 5.6 %collective-permute-start = (bf16[1,128,128]{2,1,0:T(8,128)(2,1)S(1)}, bf16[1,128,128]{2,1,0:T(8,128)(2,1)S(1)}, u32[]{:S(2)}, u32[]{:S(2)}) collective-permute-start(bf16[1,128,128]{2,1,0:T(8,128)(2,1)S(1)} %get-tuple-element.25), channel_id=1, source_target_pairs={{0,8},{8,16},{16,24},{24,32},{32,40},{40,48},{48,56},{56,64},{64,7... | collective-permute-start | bytes 98312 | tf_op jit(solution)/shard_map/ppermute | solution.py:442
  70.3 5.1 %collective-permute-start.1 = (bf16[1,128,128]{2,1,0:T(8,128)(2,1)S(1)}, bf16[1,128,128]{2,1,0:T(8,128)(2,1)S(1)}, u32[]{:S(2)}, u32[]{:S(2)}) collective-permute-start(bf16[1,128,128]{2,1,0:T(8,128)(2,1)S(1)} %get-tuple-element.26), channel_id=1, source_target_pairs={{8,0},{16,8},{24,16},{32,24},{40,32},{48,40},{56,48},{64,56},{72,6... | collective-permute-start | bytes 98312 | tf_op jit(solution)/shard_map/ppermute | solution.py:443
  75.4 6.2 %copy-start.7 = (bf16[1,128,128]{2,1,0:T(8,128)(2,1)}, bf16[1,128,128]{2,1,0:T(8,128)(2,1)S(1)}, u32[]{:S(2)}) copy-start(bf16[1,128,128]{2,1,0:T(8,128)(2,1)S(1)} %collective-permute-done.left_ref) | copy-start | bytes 98308
  75.4 6.2 %copy-start.8 = (bf16[1,128,128]{2,1,0:T(8,128)(2,1)}, bf16[1,128,128]{2,1,0:T(8,128)(2,1)S(1)}, u32[]{:S(2)}) copy-start(bf16[1,128,128]{2,1,0:T(8,128)(2,1)S(1)} %collective-permute-done.1.right_ref) | copy-start | bytes 98308
  81.6 31.5 %copy-start.4 = (f32[2048]{0:T(1024)S(1)}, f32[2048]{0:T(1024)}, u32[]{:S(2)}) copy-start(f32[2048]{0:T(1024)} %param.18) | copy-start | bytes 24580
  87.4 25.8 %all-to-all-start.2 = ((bf16[8,64,512]{2,1,0:T(8,128)(2,1)}), bf16[8,64,512]{2,1,0:T(8,128)(2,1)S(1)}, u32[]{:S(2)}, u32[]{:S(2)}) async-start(bf16[8,64,512]{2,1,0:T(8,128)(2,1)} %far_terms.1), calls=%async_computation.2 | async-start | bytes 1048576 | tf_op jit(solution)/shard_map/all_to_all | solution.py:463
  113.1 1.0 copy-start.1
  (1 other events, 0.6 us)

commit v3 on v2

--- a/solution.py
+++ b/solution.py
@@ -13,6 +13,8 @@
 eps_norm = 1e-05
 clip_level = 5.0
 TAIL = 10
+STAGE = 16
+SELECT = 52
 TIGHT = 58
 
 f32 = jnp.float32
@@ -77,7 +79,9 @@
     )(source, virtual_states)
 
 
-def project_kernel(x_ref, w_ref, query_ref, pack_ref):
+def project_kernel(core_ref, x_ref, w_ref, *refs):
+    query_ref, pack_ref = refs[2:4] if len(refs) > 2 else refs
+    rest = refs
     head = HEAD_DIM
     wide = 2 * head
     rows = min(x_ref.shape[0], 512)
@@ -89,29 +93,69 @@
         query_ref[:, start : start + rows] = sides[:head] * jnp.asarray(head**-0.5, bf16)
         for item in range(rows // wide):
             pack_ref[start // wide + item] = sides[head:, item * wide : (item + 1) * wide]
-
-
-def project(states, weight_t, step_rows, mib):
+    if len(rest) > 2:
+        expand_ref, contract_ref, _, _, outer_ref, inner_ref, piece_ref = rest
+        first = pl.program_id(0) == 0
+        last = pl.program_id(0) == pl.num_programs(0) - 1
+        even = core_ref[0] == 0
+        units = piece_ref.shape[0] // 2
+        for core in range(2):
+
+            @pl.when(first & (core_ref[0] == core))
+            def _():
+                span = slice(core * units, (core + 1) * units)
+                piece_ref[:units] = expand_ref[:, span].T
+                piece_ref[units:] = contract_ref[span, :]
+
+        @pl.when(first & even)
+        def _():
+            outer_ref[0] = pack_ref[0]
+
+        @pl.when(first & jnp.logical_not(even))
+        def _():
+            inner_ref[0] = pack_ref[0]
+
+        @pl.when(last & even)
+        def _():
+            inner_ref[0] = pack_ref[pack_ref.shape[0] - 1]
+
+        @pl.when(last & jnp.logical_not(even))
+        def _():
+            outer_ref[0] = pack_ref[pack_ref.shape[0] - 1]
+
+
+def project(core, states, weight_t, step_rows, mib, *feed):
     rows, features = states.shape
     wide = 2 * HEAD_DIM
+    whole = [pl.BlockSpec(array.shape, lambda i: (0, 0)) for array in feed]
+    more_specs, more_shapes = [], []
+    if feed:
+        more_specs = [pl.BlockSpec((1, wide, wide), lambda i: (0, 0, 0))] * 2
+        more_specs.append(pl.BlockSpec((wide * 2, features), lambda i: (0, 0)))
+        more_shapes = [jax.ShapeDtypeStruct((1, wide, wide), bf16)] * 2
+        more_shapes.append(jax.ShapeDtypeStruct((wide * 2, features), bf16))
     return pl.pallas_call(
         project_kernel,
         grid=(rows // step_rows,),
         in_specs=[
+            smem,
             pl.BlockSpec((step_rows, features), lambda i: (i, 0)),
             pl.BlockSpec(weight_t.shape, lambda i: (0, 0)),
-        ],
+        ]
+        + whole,
         out_specs=[
             pl.BlockSpec((HEAD_DIM, step_rows), lambda i: (0, i)),
             pl.BlockSpec((step_rows // wide, wide, wide), lambda i: (i, 0, 0)),
-        ],
+        ]
+        + more_specs,
         out_shape=[
             jax.ShapeDtypeStruct((HEAD_DIM, rows), bf16),
             jax.ShapeDtypeStruct((rows // wide, wide, wide), bf16),
-        ],
+        ]
+        + more_shapes,
         compiler_params=params(mib),
         name="project",
-    )(states, weight_t)
+    )(core, states, weight_t, *feed)
 
 
 def select_kernel(
@@ -159,7 +203,7 @@
             pltpu.SemaphoreType.DMA,
             pltpu.SemaphoreType.DMA((3,)),
         ],
-        compiler_params=params(TIGHT),
+        compiler_params=params(SELECT),
         name="select_blocks",
     )(me, heard, packed)
 
@@ -188,20 +232,28 @@
 
 
 def near_kernel(
-    group, place_ref, count_ref, query_ref, pack_ref, virtual_ref, rows_ref, sum_ref, total_ref
+    group, place_ref, count_ref, query_ref, pack_ref, inner_ref, virtual_ref, rows_ref, sum_ref,
+    total_ref, window_ref,
 ):
     head = HEAD_DIM
     blocks, tiles, wide = rows_ref.shape
     virtual_total = 32
     virtual_keys = virtual_ref[0, :head, :].T[:virtual_total]
     virtual_values = virtual_ref[0, head:, :virtual_total]
+    window_ref[blocks] = inner_ref[0]
+
+    def fill(block, _):
+        window_ref[block] = pack_ref[block]
+        return 0
+
+    lax.fori_loop(0, blocks, fill, 0, unroll=8)
 
     def step(turn, _):
         for item in range(group):
             block = turn * group + item
             lanes = pl.ds(pl.multiple_of(block * wide, wide), wide)
             query = query_ref[:, lanes]
-            tile_blocks = [pack_ref[place_ref[block * tiles + t]] for t in range(tiles)]
+            tile_blocks = [window_ref[place_ref[block * tiles + t]] for t in range(tiles)]
             counts = [count_ref[block * tiles + t] for t in range(tiles)]
             summed, total = tile_terms(
                 query.astype(f32), tile_blocks, tile_rows(rows_ref, block), counts
@@ -219,109 +271,126 @@
     lax.fori_loop(0, blocks // group, step, 0)
 
 
-def near_terms(places, counts, query, packed, virtual, rows, group):
+def near_terms(places, counts, query, packed, inner, virtual, rows, group):
     head, total = query.shape
+    blocks = packed.shape[0]
     return pl.pallas_call(
         functools.partial(near_kernel, group),
-        in_specs=[smem, smem] + [vmem] * 4,
+        in_specs=[smem, smem] + [vmem] * 5,
         out_specs=[vmem, vmem],
         out_shape=[
             jax.ShapeDtypeStruct((head, total), f32),
             jax.ShapeDtypeStruct((1, total), f32),
         ],
+        scratch_shapes=[pltpu.VMEM((blocks + 1,) + packed.shape[1:], bf16)],
         compiler_params=params(TIGHT),
-        cost_estimate=pl.CostEstimate(
-            flops=8 * 2**30, bytes_accessed=4 * 2**20, transcendentals=2**20
-        ),
+        cost_estimate=pl.CostEstimate(flops=1, bytes_accessed=1, transcendentals=0),
         name="near_terms",
-    )(places, counts, query, packed, virtual, rows)
+    )(places, counts, query, packed, inner, virtual, rows)
 
 
 def far_kernel(
-    group, slot_ref, count_ref, edge_ref, query_ref, reply_ref, rows_ref, left_ref, right_ref,
-    edge_rows_ref, sum_ref, total_ref, out_ref,
+    group, share_ref, slot_ref, count_ref, edge_ref, edge_count_ref, query_ref, reply_ref, rows_ref,
+    outer_ref, edge_rows_ref, sum_ref, total_ref, *rest
 ):
+    outs, (out_ref, sem) = rest[:-2], rest[-2:]
     blocks, tiles, wide = rows_ref.shape
     share_blocks = blocks // out_ref.shape[0]
-
-    def one(block, more_blocks=(), more_rows=(), more_counts=()):
-        lanes = pl.ds(pl.multiple_of(block * wide, wide), wide)
-        tile_blocks = [reply_ref[slot_ref[0, t * blocks + block]] for t in range(tiles)]
-        counts = [count_ref[block * tiles + t] for t in range(tiles)]
-        summed, total = tile_terms(
-            query_ref[:, lanes].astype(f32),
-            tile_blocks + list(more_blocks),
-            tile_rows(rows_ref, block) + list(more_rows),
-            counts + list(more_counts),
-        )
-        total = total + total_ref[:, lanes]
-        result = (summed + sum_ref[:, lanes]) * (1.0 / total)
-        inner = pl.ds(pl.multiple_of(lax.rem(block, share_blocks) * wide, wide), wide)
-        out_ref[lax.div(block, share_blocks), :, inner] = result.astype(bf16)
-
+    edge = edge_ref[0]
     near_tiles = edge_rows_ref.shape[1]
-    for end, halo_ref in enumerate((left_ref, right_ref)):
-        one(
-            jnp.int32(end * (blocks - 1)),
-            [halo_ref[0]] * near_tiles,
-            tile_rows(edge_rows_ref, end),
-            [edge_ref[end * near_tiles + t] for t in range(near_tiles)],
-        )
+    edge_sum, edge_total = tile_terms(
+        query_ref[:, pl.ds(pl.multiple_of(edge * wide, wide), wide)].astype(f32),
+        [outer_ref[0]] * near_tiles,
+        tile_rows(edge_rows_ref, edge),
+        [edge_count_ref[edge * near_tiles + t] for t in range(near_tiles)],
+    )
 
     def step(turn, _):
         for item in range(group):
-            one(1 + turn * group + item)
+            block = turn * group + item
+            lanes = pl.ds(pl.multiple_of(block * wide, wide), wide)
+            tile_blocks = [reply_ref[slot_ref[0, t * blocks + block]] for t in range(tiles)]
+            counts = [count_ref[block * tiles + t] for t in range(tiles)]
+            summed, total = tile_terms(
+                query_ref[:, lanes].astype(f32), tile_blocks, tile_rows(rows_ref, block), counts
+            )
+            here = (block == edge).astype(f32)
+            total = total + total_ref[:, lanes] + here * edge_total
+            result = (summed + sum_ref[:, lanes] + here * edge_sum) * (1.0 / total)
+            inner = pl.ds(pl.multiple_of(lax.rem(block, share_blocks) * wide, wide), wide)
+            out_ref[lax.div(block, share_blocks), :, inner] = result.astype(bf16)
         return 0
 
-    lax.fori_loop(0, (blocks - 2) // group, step, 0)
+    lax.fori_loop(0, blocks // group, step, 0)
+    copies = []
+    for ahead, out in enumerate(outs):
+        share = lax.rem(share_ref[0] + ahead, len(outs))
+        copies.append(pltpu.make_async_copy(out_ref.at[share], out, sem.at[ahead]))
+        copies[-1].start()
+    for copy in copies:
+        copy.wait()
 
 
 def far_terms(
-    slots, counts, edges, query, replies, rows, left, right, edge_rows, near_sum, near_total, shares,
-    group,
+    share, slots, counts, edge, edge_counts, query, replies, rows, outer, edge_rows, near_sum,
+    near_total, shares, group,
 ):
     head, total = query.shape
     return pl.pallas_call(
         functools.partial(far_kernel, group),
-        in_specs=[smem] * 3 + [vmem] * 8,
-        out_specs=vmem,
-        out_shape=jax.ShapeDtypeStruct((shares, head, total // shares), bf16),
+        in_specs=[smem] * 5 + [vmem] * 7,
+        out_specs=[pl.BlockSpec(memory_space=pl.ANY)] * shares,
+        out_shape=[jax.ShapeDtypeStruct((head, total // shares), bf16)] * shares,
+        scratch_shapes=[
+            pltpu.VMEM((shares, head, total // shares), bf16),
+            pltpu.SemaphoreType.DMA((shares,)),
+        ],
         compiler_params=params(TIGHT),
         name="far_terms",
-    )(slots, counts, edges, query, replies, rows, left, right, edge_rows, near_sum, near_total)
-
-
-def piece_kernel(core_ref, expand_ref, contract_ref, out_ref):
-    wide = out_ref.shape[0] // 2
-    for core in range(2):
-
-        @pl.when(core_ref[0] == core)
-        def _():
-            span = slice(core * wide, (core + 1) * wide)
-            out_ref[:wide] = expand_ref[:, span].T
-            out_ref[wide:] = contract_ref[span, :]
-
-
-def weight_piece(core, expand, contract):
-    features, width = expand.shape
-    return pl.pallas_call(
-        piece_kernel,
-        in_specs=[smem, vmem, vmem],
-        out_specs=vmem,
-        out_shape=jax.ShapeDtypeStruct((width, features), bf16),
-        compiler_params=params(16),
-        name="weight_piece",
-    )(core, expand, contract)
+    )(
+        share, slots, counts, edge, edge_counts, query, replies, rows, outer, edge_rows, near_sum,
+        near_total,
+    )
+
+
+def stage_kernel(share_ref, states_ref, *refs):
+    sources, (own_ref, *copies, sems) = refs[:3], refs[3:]
+    rows = own_ref.shape[0]
+    start = pl.multiple_of(share_ref[0] * rows, rows)
+    fetches = [pltpu.make_async_copy(states_ref.at[pl.ds(start, rows)], own_ref, sems.at[0])]
+    for item, (source, copy) in enumerate(zip(sources, copies)):
+        fetches.append(pltpu.make_async_copy(source, copy, sems.at[item + 1]))
+    for fetch in fetches:
+        fetch.start()
+    for fetch in fetches:
+        fetch.wait()
+
+
+def stage(share, states, rows, *others):
+    return pl.pallas_call(
+        stage_kernel,
+        in_specs=[smem] + [pl.BlockSpec(memory_space=pl.ANY)] * (1 + len(others)),
+        out_specs=[vmem] * (1 + len(others)),
+        out_shape=[jax.ShapeDtypeStruct((rows, states.shape[1]), bf16)]
+        + [jax.ShapeDtypeStruct(other.shape, bf16) for other in others],
+        scratch_shapes=[pltpu.SemaphoreType.DMA((1 + len(others),))],
+        compiler_params=params(STAGE),
+        name="stage",
+    )(share, states, *others)
 
 
 def tail_kernel(
-    offsets, place_ref, att_ref, own_ref, output_ref, mine_ref, theirs_ref, bias_ref, out_ref
+    offsets, place_ref, own_ref, output_ref, mine_ref, theirs_ref, bias_ref, *rest
 ):
-    heads, head, rows = att_ref.shape
-    features = heads * head
+    pieces, (out_ref, att_ref) = rest[:-2], rest[-2:]
+    features, rows = att_ref.shape
+    head, _ = pieces[0].shape
+    for behind, piece in enumerate(pieces):
+        owner = lax.rem(place_ref[0] + len(pieces) - behind, len(pieces))
+        att_ref[pl.ds(pl.multiple_of(owner * head, head), head), :] = piece[...]
     parts = len(offsets)
     wide = mine_ref.shape[1] // 2
-    attended = att_ref[...].reshape(features, rows).T
+    attended = att_ref[...].T
     residual = own_ref[...].astype(f32) + jnp.dot(
         attended, output_ref[...], preferred_element_type=f32
     )
@@ -343,15 +412,17 @@
     out_ref[...] = summed.astype(bf16)
 
 
-def tail(place, regrouped, own, output_weight, mine, theirs, bias, offsets):
+def tail(place, own, output_weight, mine, theirs, bias, pieces, offsets):
+    rows, features = own.shape
     return pl.pallas_call(
         functools.partial(tail_kernel, offsets),
-        in_specs=[smem] + [vmem] * 6,
+        in_specs=[smem] + [vmem] * (5 + len(pieces)),
         out_specs=vmem,
         out_shape=jax.ShapeDtypeStruct(own.shape, bf16),
+        scratch_shapes=[pltpu.VMEM((features, rows), bf16)],
         compiler_params=params(TAIL),
         name="tail",
-    )(place, regrouped, own, output_weight, mine, theirs, bias)
+    )(place, own, output_weight, mine, theirs, bias, *pieces)
 
 
 def local(
@@ -383,8 +454,19 @@
     message, slots = ask(expander_source.T, virtual_states, span)
     heard = lax.all_to_all(message, "nodes", split_axis=0, concat_axis=0, tiled=True)
     weight_t = project_weight.T
-    query, packed = project(node_states, weight_t, rows // 2, TIGHT)
+    query, packed, outer, inner, piece = project(
+        core.reshape(1), node_states, weight_t, rows // 2, TIGHT, expand_weight, contract_weight
+    )
+    outward = [(i, (i + (1 if i % 2 else -1)) % span) for i in range(span)]
+    inward = [(i, i ^ 1) for i in range(span)]
+
+    def turn(value, by):
+        return lax.ppermute(value, "heads", [(i, (i + by) % shares) for i in range(shares)])
+
+    half = expand_weight.shape[1] // 2
+    once = turn(piece, 1)
     chosen = select_blocks(me.reshape(1), heard, packed)
+    chosen, heard, outer, inner = barrier((chosen, heard, outer, inner))
     replies = lax.all_to_all(
         chosen.reshape(span, BCAP * block_rows, lanes),
         "nodes",
@@ -393,7 +475,8 @@
         tiled=True,
     ).reshape(span * BCAP, block_rows, lanes)
 
-    heard, chosen = barrier((heard, chosen))
+    inner = lax.ppermute(inner, "nodes", inward)
+    outer = lax.ppermute(outer, "nodes", outward)
     extra = jnp.concatenate(
         [
             heard[:, 8 : 8 + features // lanes].reshape(span, features),
@@ -401,75 +484,70 @@
         ],
         axis=0,
     )
-    _, virtual_packed = project(extra, weight_t, extra.shape[0], 16)
+    _, virtual_packed = project(core.reshape(1), extra, weight_t, block_rows, 16)
+    piece, once, virtual_packed = barrier((piece, once, virtual_packed))
     local_ids = jnp.arange(blocks, dtype=jnp.int32)[:, None]
     global_ids = me * blocks + local_ids
     place = jnp.mod(neigh_source - global_ids + 1, all_blocks) + local_ids - 1
-    inside = (place >= 0) & (place < blocks)
-    near_count = jnp.where(inside, neigh_count, 0)
-    edge_count = jnp.where(inside, 0, neigh_count)
+    edge = core * (blocks - 1)
+    beyond = jnp.where(core == 0, place < 0, place == blocks)
+    place = jnp.where(beyond, 0, jnp.where(place < 0, blocks, place))
+    near_count = jnp.where(beyond, 0, neigh_count)
+    edge_count = jnp.where(beyond, neigh_count, 0)
     near_sum, near_total = near_terms(
-        jnp.clip(place, 0, blocks - 1).reshape(-1),
+        place.reshape(-1),
         near_count.reshape(-1),
         query,
         packed,
+        inner,
         virtual_packed,
         neigh_rows,
         4,
     )
 
-    half = expand_weight.shape[1] // 2
-    piece = weight_piece(core.reshape(1), expand_weight, contract_weight)
-    piece, virtual_packed = barrier((piece, virtual_packed))
-    upward = [(i, (i + 1) % shares) for i in range(shares)]
-    downward = [((i + 1) % shares, i) for i in range(shares)]
-    pieces, offsets = [piece], [0]
-    above, below = piece, piece
-    for step in range(1, shares // 2 + 1):
-        below = lax.ppermute(below, "heads", upward)
-        if step == 1:
-            below, near_total = barrier((below, near_total))
-        pieces.append(below)
-        offsets.append(-step)
-        if step < shares // 2:
-            above = lax.ppermute(above, "heads", downward)
-            pieces.append(above)
-            offsets.append(step)
+    back = turn(piece, -1)
+    pieces = [piece, once, back]
+    for step in range(2, 4):
+        pieces += [turn(pieces[-2], 1), turn(pieces[-1], -1)]
+    pieces.append(turn(piece, 4))
+    offsets = (0, -1, 1, -2, 2, -3, 3, -4)
     mine = jnp.stack(pieces)
-    theirs = lax.ppermute(mine, "nodes", [(i, i ^ 1) for i in range(span)])
-
-    first_block, last_block, virtual_packed = barrier((packed[:1], packed[-1:], virtual_packed))
-    left = lax.ppermute(last_block, "nodes", [(i, (i + 1) % span) for i in range(span)])
-    right = lax.ppermute(first_block, "nodes", [((i + 1) % span, i) for i in range(span)])
-
-    edge_rows = jnp.concatenate([neigh_rows[:1], neigh_rows[-1:]], axis=0)
+    mine, near_total, outer = barrier((mine, near_total, outer))
+    theirs = lax.ppermute(mine, "nodes", inward)
+
     attended = far_terms(
+        share.reshape(1),
         slots,
         expander_count.reshape(-1),
-        jnp.concatenate([edge_count[0], edge_count[-1]]),
+        edge.reshape(1),
+        edge_count.reshape(-1),
         query,
         replies,
         expander_rows,
-        left,
-        right,
-        edge_rows,
+        outer,
+        neigh_rows,
         near_sum,
         near_total,
         shares,
-        10,
-    )
-    own = lax.dynamic_slice_in_dim(node_states, share * (rows // shares), rows // shares, 0)
-    attended, own, mine = barrier((attended, own, mine))
-    regrouped = lax.all_to_all(attended, "heads", split_axis=0, concat_axis=0, tiled=True)
+        16,
+    )
+    own, output_staged, mine, theirs = stage(
+        share.reshape(1), node_states, rows // shares, output_weight, mine, theirs
+    )
+    regrouped = [attended[0]] + [None] * (shares - 1)
+    for ahead in sorted(range(1, shares), key=lambda ahead: -min(ahead, shares - ahead)):
+        regrouped[ahead] = lax.ppermute(
+            attended[ahead], "heads", [(i, (i + ahead) % shares) for i in range(shares)]
+        )
     return tail(
         jnp.stack([share, core]),
-        regrouped,
         own,
-        output_weight,
+        output_staged,
         mine,
         theirs,
         expand_bias.reshape(2 * shares, 1, half),
-        tuple(offsets),
+        regrouped,
+        offsets,
     )
 
 

time: 120 us -> 119 us (level)
  waiting for transfers between devices: 42.9 us -> 25.1 us
  starting transfers between devices: 37 us -> 50.5 us
  local copies, waits for them, and re-layouts: 8.26 us -> 11.3 us
  other arithmetic: 1.31 us -> 0.1 us
    ppermute x10 -> x17, starting transfers between devices: 14.3 us -> 35.4 us  [the longest x7 17.7 us: local(): lax.ppermute(attended[ahead], 'heads', [(i, (i + ahead) % shares) for i i...]
    all_to_all x1 -> x0, waiting for transfers between devices: 17.2 us -> none  [local(): lax.all_to_all(attended, 'heads', split_axis=0, concat_axis=0, tiled=True)]
    all_to_all x1 -> x0, starting transfers between devices: 8.46 us -> none  [local(): lax.all_to_all(attended, 'heads', split_axis=0, concat_axis=0, tiled=True)]
    unnamed x33 -> x39, local copies, waits for them, and re-layouts: 2.56 us -> 7.6 us
    pallas_call x4, Pallas kernels: 12.4 us -> 15.1 us  [the longest x2 7.04 us: project(): pl.pallas_call(project_kernel, grid=(rows // step_rows,), in_specs=[smem,...]
    slice x3 -> x0, local copies, waits for them, and re-layouts: 1.65 us -> none  [the longest x1 0.78 us: local(): packed[-1:]]
    ppermute x10 -> x17, waiting for transfers between devices: 18.7 us -> 20.3 us  [the longest x7 16.5 us: turn(): lax.ppermute(value, 'heads', [(i, (i + by) % shares) for i in range(share...]
    all_to_all x1, waiting for transfers between devices: 6.2 us -> 4.8 us  [local(): lax.all_to_all(chosen.reshape(span, BCAP * block_rows, lanes), 'nodes', s...]
  transfers between devices with their start and end apart: 13 -> 19, of which waited for: 7 -> 7; matrix products, arithmetic and copies ran while one was open for 6% -> 8% of each run, Pallas kernels for 16% -> 21%
where the time goes in v3:
time: 119 us; the launch traced here: 118 us
  starting transfers between devices  50.5 us (42%)
  Pallas kernels  31 us (26%)
  waiting for transfers between devices  25.1 us (21%)
  local copies, waits for them, and re-layouts  11.3 us (9%)
    ppermute x7, starting transfers between devices, local(): lax.ppermute(attended[ahead], 'heads', [(i, (i + ahead) % shares) for i i...  17.7 us
    ppermute x7, starting transfers between devices, turn(): lax.ppermute(value, 'heads', [(i, (i + by) % shares) for i in range(share...  17.2 us
    ppermute x7, waiting for transfers between devices, turn(): lax.ppermute(value, 'heads', [(i, (i + by) % shares) for i in range(share...  16.5 us
    unnamed x39, local copies, waits for them, and re-layouts  7.6 us
    all_to_all x1, starting transfers between devices, local(): lax.all_to_all(chosen.reshape(span, BCAP * block_rows, lanes), 'nodes', s...  7.58 us
    all_to_all x1, starting transfers between devices, local(): lax.all_to_all(message, 'nodes', split_axis=0, concat_axis=0, tiled=True)  7.53 us
    pallas_call x2, Pallas kernels, project(): pl.pallas_call(project_kernel, grid=(rows // step_rows,), in_specs=[smem,...  7.04 us
    pallas_call x1, Pallas kernels, near_terms(): pl.pallas_call(functools.partial(near_kernel, group), in_specs=[smem, sme...  6.48 us
  transfers between devices with their start and end apart: 19, of which 7 were waited for; matrix products, arithmetic and copies ran while one was open for 8% of the time, Pallas kernels for 21%

profile of v3, /device:TPU:8, one launch (start us, length us, event | category | flops | bytes accessed | tf_op | source)
XLA Modules:
  0.0 118.2 jit_solution(2256217733254827537)
XLA Ops:
  1.7 7.5 %all-to-all-start = ((bf16[32,16,128]{2,1,0:T(8,128)(2,1)}), bf16[32,16,128]{2,1,0:T(8,128)(2,1)S(1)}, u32[]{:S(2)}, u32[]{:S(2)}) async-start(bf16[32,16,128]{2,1,0:T(8,128)(2,1)} %get-tuple-element.38), calls=%async_computation | async-start | bytes 262144 | tf_op jit(solution)/shard_map/all_to_all | solution.py:455
  9.3 6.1 %project.2 = (bf16[64,4096]{1,0:T(8,128)(2,1)}, bf16[32,128,128]{2,1,0:T(8,128)(2,1)}, bf16[1,128,128]{2,1,0:T(8,128)(2,1)}, bf16[1,128,128]{2,1,0:T(8,128)(2,1)}, bf16[256,512]{1,0:T(8,128)(2,1)}) custom-call(s32[1]{0:T(128)} %bitcast.1.core_ref, bf16[4096,512]{1,0:T(8,128)(2,1)} %states_ref.1, bf16[192,512]{1,0:T(8,128)(2,1)} %bitcast.29, ...), custom_call_target="tpu_custom_call" | custom-call | tf_op jit(solution)/shard_map/project/pallas_call | solution.py:137
  15.4 2.0 %collective-permute-start = (bf16[256,512]{1,0:T(8,128)(2,1)}, bf16[256,512]{1,0:T(8,128)(2,1)S(1)}, u32[]{:S(2)}, u32[]{:S(2)}) collective-permute-start(bf16[256,512]{1,0:T(8,128)(2,1)} %get-tuple-element.44), channel_id=1, source_target_pairs={{0,1},{1,2},{2,3},{3,4},{4,5},{5,6},{6,7},{7,0},{8,9},{9,10},{10,1... | collective-permute-start | bytes 786440 | tf_op jit(solution)/shard_map/ppermute | solution.py:464
  18.7 3.1 %select_blocks.1 = bf16[128,128,128]{2,1,0:T(8,128)(2,1)} custom-call(s32[1]{0:T(128)} %bitcast.3.me_ref, bf16[32,16,128]{2,1,0:T(8,128)(2,1)S(1)} %all-to-all-done.heard_ref, bf16[32,128,128]{2,1,0:T(8,128)(2,1)S(1)} %copy-done.1), custom_call_target="tpu_custom_call" | custom-call | tf_op jit(solution)/shard_map/select_blocks/pallas_call | solution.py:193
  21.8 7.6 %all-to-all-start.1 = ((bf16[32,512,128]{2,1,0:T(8,128)(2,1)}), bf16[32,512,128]{2,1,0:T(8,128)(2,1)}, u32[]{:S(2)}, u32[]{:S(2)}) async-start(bf16[32,512,128]{2,1,0:T(8,128)(2,1)} %bitcast.32), calls=%async_computation.1 | async-start | bytes 8388608 | tf_op jit(solution)/shard_map/all_to_all | solution.py:470
  33.0 6.3 %collective-permute-start.6 = (bf16[256,512]{1,0:T(8,128)(2,1)S(1)}, bf16[256,512]{1,0:T(8,128)(2,1)S(1)}, u32[]{:S(2)}, u32[]{:S(2)}) collective-permute-start(bf16[256,512]{1,0:T(8,128)(2,1)S(1)} %copy-done.7), channel_id=1, source_target_pairs={{0,4},{1,5},{2,6},{3,7},{4,0},{5,1},{6,2},{7,3},{8,12},{9,13},{10,... | collective-permute-start | bytes 786440 | tf_op jit(solution)/shard_map/ppermute | solution.py:464
  39.3 2.2 %collective-permute-start.1 = (bf16[256,512]{1,0:T(8,128)(2,1)S(1)}, bf16[256,512]{1,0:T(8,128)(2,1)S(1)}, u32[]{:S(2)}, u32[]{:S(2)}) collective-permute-start(bf16[256,512]{1,0:T(8,128)(2,1)S(1)} %copy-done.7), channel_id=1, source_target_pairs={{0,7},{1,0},{2,1},{3,2},{4,3},{5,4},{6,5},{7,6},{8,15},{9,8},{10,9... | collective-permute-start | bytes 786440 | tf_op jit(solution)/shard_map/ppermute | solution.py:464
  42.8 6.5 %near_terms.1 = (f32[64,4096]{1,0:T(8,128)}, f32[1,4096]{1,0:T(1,128)}) custom-call(s32[128]{0:T(128)} %reshape.41.place_ref, s32[128]{0:T(128)} %reshape.42.count_ref, bf16[64,4096]{1,0:T(8,128)(2,1)} %get-tuple-element.46.query_ref, bf16[32,128,128]{2,1,0:T(8,128)(2,1)} %get-tuple-element.39.pack_ref, bf16[1,128,128]{2,1,0:T(8,128)(2,1)} %copy-done.9, ...), custom_call_target="tpu_custom_call" | custom-call | flops 1 | bytes 1 | tf_op jit(solution)/shard_map/near_terms/pallas_call | solution.py:277
  50.0 7.7 %collective-permute-done.2 = bf16[256,512]{1,0:T(8,128)(2,1)S(1)} collective-permute-done((bf16[256,512]{1,0:T(8,128)(2,1)S(1)}, bf16[256,512]{1,0:T(8,128)(2,1)S(1)}, u32[]{:S(2)}, u32[]{:S(2)}) %collective-permute-start.2) | collective-permute-done | bytes 262176 | tf_op jit(solution)/shard_map/ppermute | solution.py:464
  57.7 1.8 %collective-permute-start.4 = (bf16[256,512]{1,0:T(8,128)(2,1)S(1)}, bf16[256,512]{1,0:T(8,128)(2,1)S(1)}, u32[]{:S(2)}, u32[]{:S(2)}) collective-permute-start(bf16[256,512]{1,0:T(8,128)(2,1)S(1)} %collective-permute-done.2), channel_id=1, source_target_pairs={{0,1},{1,2},{2,3},{3,4},{4,5},{5,6},{6,7},{7,0},{8,9},{9,10},{10,1... | collective-permute-start | bytes 786440 | tf_op jit(solution)/shard_map/ppermute | solution.py:464
  59.4 1.9 %collective-permute-start.3 = (bf16[256,512]{1,0:T(8,128)(2,1)S(1)}, bf16[256,512]{1,0:T(8,128)(2,1)S(1)}, u32[]{:S(2)}, u32[]{:S(2)}) collective-permute-start(bf16[256,512]{1,0:T(8,128)(2,1)S(1)} %collective-permute-done.1), channel_id=1, source_target_pairs={{0,7},{1,0},{2,1},{3,2},{4,3},{5,4},{6,5},{7,6},{8,15},{9,8},{10,9... | collective-permute-start | bytes 786440 | tf_op jit(solution)/shard_map/ppermute | solution.py:464
  62.7 5.2 %collective-permute-done.3 = bf16[256,512]{1,0:T(8,128)(2,1)S(1)} collective-permute-done((bf16[256,512]{1,0:T(8,128)(2,1)S(1)}, bf16[256,512]{1,0:T(8,128)(2,1)S(1)}, u32[]{:S(2)}, u32[]{:S(2)}) %collective-permute-start.3) | collective-permute-done | bytes 262176 | tf_op jit(solution)/shard_map/ppermute | solution.py:464
  67.9 3.1 %collective-permute-start.5 = (bf16[256,512]{1,0:T(8,128)(2,1)S(1)}, bf16[256,512]{1,0:T(8,128)(2,1)S(1)}, u32[]{:S(2)}, u32[]{:S(2)}) collective-permute-start(bf16[256,512]{1,0:T(8,128)(2,1)S(1)} %collective-permute-done.3), channel_id=1, source_target_pairs={{0,7},{1,0},{2,1},{3,2},{4,3},{5,4},{6,5},{7,6},{8,15},{9,8},{10,9... | collective-permute-start | bytes 786440 | tf_op jit(solution)/shard_map/ppermute | solution.py:464
  72.4 3.7 %collective-permute-done.5 = bf16[256,512]{1,0:T(8,128)(2,1)S(1)} collective-permute-done((bf16[256,512]{1,0:T(8,128)(2,1)S(1)}, bf16[256,512]{1,0:T(8,128)(2,1)S(1)}, u32[]{:S(2)}, u32[]{:S(2)}) %collective-permute-start.5) | collective-permute-done | bytes 262176 | tf_op jit(solution)/shard_map/ppermute | solution.py:464
  79.1 4.8 %all-to-all-done.1 = bf16[32,512,128]{2,1,0:T(8,128)(2,1)} async-done(((bf16[32,512,128]{2,1,0:T(8,128)(2,1)}), bf16[32,512,128]{2,1,0:T(8,128)(2,1)}, u32[]{:S(2)}, u32[]{:S(2)}) %all-to-all-start.1) | async-done | bytes 4194336 | tf_op jit(solution)/shard_map/all_to_all | solution.py:470
  83.9 5.7 %far_terms.1 = (bf16[64,512]{1,0:T(8,128)(2,1)}, bf16[64,512]{1,0:T(8,128)(2,1)}, bf16[64,512]{1,0:T(8,128)(2,1)}, bf16[64,512]{1,0:T(8,128)(2,1)}, bf16[64,512]...) custom-call(s32[1]{0:T(128)} %bitcast.share_ref, ...), custom_call_target="tpu_custom_call" | custom-call | tf_op jit(solution)/shard_map/far_terms/pallas_call | solution.py:339
  89.7 2.2 %collective-permute-start.10 = (bf16[64,512]{1,0:T(8,128)(2,1)}, bf16[64,512]{1,0:T(8,128)(2,1)S(1)}, u32[]{:S(2)}, u32[]{:S(2)}) collective-permute-start(bf16[64,512]{1,0:T(8,128)(2,1)} %get-tuple-element.62), channel_id=1, source_target_pairs={{0,1},{1,2},{2,3},{3,4},{4,5},{5,6},{6,7},{7,0},{8,9},{9,10},{10,1... | collective-permute-start | bytes 196616 | tf_op jit(solution)/shard_map/ppermute | solution.py:539
  91.8 4.5 %collective-permute-start.11 = (bf16[64,512]{1,0:T(8,128)(2,1)}, bf16[64,512]{1,0:T(8,128)(2,1)S(1)}, u32[]{:S(2)}, u32[]{:S(2)}) collective-permute-start(bf16[64,512]{1,0:T(8,128)(2,1)} %get-tuple-element.63), channel_id=1, source_target_pairs={{0,2},{1,3},{2,4},{3,5},{4,6},{5,7},{6,0},{7,1},{8,10},{9,11},{10,... | collective-permute-start | bytes 196616 | tf_op jit(solution)/shard_map/ppermute | solution.py:539
  96.3 1.9 %collective-permute-start.12 = (bf16[64,512]{1,0:T(8,128)(2,1)}, bf16[64,512]{1,0:T(8,128)(2,1)S(1)}, u32[]{:S(2)}, u32[]{:S(2)}) collective-permute-start(bf16[64,512]{1,0:T(8,128)(2,1)} %get-tuple-element.64), channel_id=1, source_target_pairs={{0,3},{1,4},{2,5},{3,6},{4,7},{5,0},{6,1},{7,2},{8,11},{9,12},{10,... | collective-permute-start | bytes 196616 | tf_op jit(solution)/shard_map/ppermute | solution.py:539
  99.7 3.1 %collective-permute-start.14 = (bf16[64,512]{1,0:T(8,128)(2,1)}, bf16[64,512]{1,0:T(8,128)(2,1)S(1)}, u32[]{:S(2)}, u32[]{:S(2)}) collective-permute-start(bf16[64,512]{1,0:T(8,128)(2,1)} %get-tuple-element.66), channel_id=1, source_target_pairs={{0,5},{1,6},{2,7},{3,0},{4,1},{5,2},{6,3},{7,4},{8,13},{9,14},{10,... | collective-permute-start | bytes 196616 | tf_op jit(solution)/shard_map/ppermute | solution.py:539
  102.8 3.6 %collective-permute-start.15 = (bf16[64,512]{1,0:T(8,128)(2,1)}, bf16[64,512]{1,0:T(8,128)(2,1)S(1)}, u32[]{:S(2)}, u32[]{:S(2)}) collective-permute-start(bf16[64,512]{1,0:T(8,128)(2,1)} %get-tuple-element.67), channel_id=1, source_target_pairs={{0,6},{1,7},{2,0},{3,1},{4,2},{5,3},{6,4},{7,5},{8,14},{9,15},{10,... | collective-permute-start | bytes 196616 | tf_op jit(solution)/shard_map/ppermute | solution.py:539
  107.5 2.3 %stage.1 = (bf16[512,512]{1,0:T(8,128)(2,1)S(1)}, bf16[512,512]{1,0:T(8,128)(2,1)S(1)}, bf16[8,256,512]{2,1,0:T(8,128)(2,1)S(1)}, bf16[8,256,512]{2,1,0:T(8,128)(2,1)S(1)}) custom-call(s32[1]{0:T(128)} %bitcast.share_ref, bf16[4096,512]{1,0:T(8,128)(2,1)S(1)} %copy-done, bf16[512,512]{1,0:T(8,128)(2,1)S(1)} %copy-done.3, ...), custom_call_target="tpu_custom_call" | custom-call | tf_op jit(solution)/shard_map/stage/pallas_call | solution.py:370
  109.9 2.4 %collective-permute-done.14.rest_5_ = bf16[64,512]{1,0:T(8,128)(2,1)S(1)} collective-permute-done((bf16[64,512]{1,0:T(8,128)(2,1)}, bf16[64,512]{1,0:T(8,128)(2,1)S(1)}, u32[]{:S(2)}, u32[]{:S(2)}) %collective-permute-start.14) | collective-permute-done | bytes 65568 | tf_op jit(solution)/shard_map/ppermute | solution.py:539
  113.6 4.6 %tail.1 = bf16[512,512]{1,0:T(8,128)(2,1)} custom-call(s32[2]{0:T(128)S(1)} %pad_add_fusion.place_ref, bf16[512,512]{1,0:T(8,128)(2,1)S(1)} %get-tuple-element.52.own_ref, bf16[512,512]{1,0:T(8,128)(2,1)S(1)} %get-tuple-element.53.output_ref, bf16[8,256,512]{2,1,0:T(8,128)(2,1)S(1)} %get-tuple-element.54.mine_ref, ...), custom_call_target="tpu_custom_call" | custom-call | tf_op jit(solution)/shard_map/tail/pallas_call | solution.py:417
  (75 shorter events, 18.3 us)
Async XLA Ops:
  1.7 15.7 %all-to-all-start = ((bf16[32,16,128]{2,1,0:T(8,128)(2,1)}), bf16[32,16,128]{2,1,0:T(8,128)(2,1)S(1)}, u32[]{:S(2)}, u32[]{:S(2)}) async-start(bf16[32,16,128]{2,1,0:T(8,128)(2,1)} %get-tuple-element.38), calls=%async_computation | async-start | bytes 262144 | tf_op jit(solution)/shard_map/all_to_all | solution.py:455
  15.4 17.6 %collective-permute-start = (bf16[256,512]{1,0:T(8,128)(2,1)}, bf16[256,512]{1,0:T(8,128)(2,1)S(1)}, u32[]{:S(2)}, u32[]{:S(2)}) collective-permute-start(bf16[256,512]{1,0:T(8,128)(2,1)} %get-tuple-element.44), channel_id=1, source_target_pairs={{0,1},{1,2},{2,3},{3,4},{4,5},{5,6},{6,7},{7,0},{8,9},{9,10},{10,1... | collective-permute-start | bytes 786440 | tf_op jit(solution)/shard_map/ppermute | solution.py:464
  21.8 9.6 %copy-start.2 = (bf16[512,192]{0,1:T(8,128)(2,1)S(1)}, bf16[512,192]{0,1:T(8,128)(2,1)}, u32[]{:S(2)}) copy-start(bf16[512,192]{0,1:T(8,128)(2,1)} %param.15) | copy-start | bytes 589828
  21.8 11.2 %copy-start.7 = (bf16[256,512]{1,0:T(8,128)(2,1)S(1)}, bf16[256,512]{1,0:T(8,128)(2,1)}, u32[]{:S(2)}) copy-start(bf16[256,512]{1,0:T(8,128)(2,1)} %get-tuple-element.44) | copy-start | bytes 786436
  21.8 62.1 %all-to-all-start.1 = ((bf16[32,512,128]{2,1,0:T(8,128)(2,1)}), bf16[32,512,128]{2,1,0:T(8,128)(2,1)}, u32[]{:S(2)}, u32[]{:S(2)}) async-start(bf16[32,512,128]{2,1,0:T(8,128)(2,1)} %bitcast.32), calls=%async_computation.1 | async-start | bytes 8388608 | tf_op jit(solution)/shard_map/all_to_all | solution.py:470
  30.9 11.3 %collective-permute-start.7 = (bf16[1,128,128]{2,1,0:T(8,128)(2,1)S(1)}, bf16[1,128,128]{2,1,0:T(8,128)(2,1)S(1)}, u32[]{:S(2)}, u32[]{:S(2)}) collective-permute-start(bf16[1,128,128]{2,1,0:T(8,128)(2,1)S(1)} %copy-done.14), channel_id=1, source_target_pairs={{0,8},{8,0},{16,24},{24,16},{32,40},{40,32},{48,56},{56,48},{64,72... | collective-permute-start | bytes 98312 | tf_op jit(solution)/shard_map/ppermute | solution.py:478
  31.1 46.4 %collective-permute-start.8 = (bf16[1,128,128]{2,1,0:T(8,128)(2,1)S(1)}, bf16[1,128,128]{2,1,0:T(8,128)(2,1)S(1)}, u32[]{:S(2)}, u32[]{:S(2)}) collective-permute-start(bf16[1,128,128]{2,1,0:T(8,128)(2,1)S(1)} %copy-done.13), channel_id=1, source_target_pairs={{0,248},{8,16},{16,8},{24,32},{32,24},{40,48},{48,40},{56,64},{64,... | collective-permute-start | bytes 98312 | tf_op jit(solution)/shard_map/ppermute | solution.py:479
  33.0 43.8 %collective-permute-start.6 = (bf16[256,512]{1,0:T(8,128)(2,1)S(1)}, bf16[256,512]{1,0:T(8,128)(2,1)S(1)}, u32[]{:S(2)}, u32[]{:S(2)}) collective-permute-start(bf16[256,512]{1,0:T(8,128)(2,1)S(1)} %copy-done.7), channel_id=1, source_target_pairs={{0,4},{1,5},{2,6},{3,7},{4,0},{5,1},{6,2},{7,3},{8,12},{9,13},{10,... | collective-permute-start | bytes 786440 | tf_op jit(solution)/shard_map/ppermute | solution.py:464
  39.3 20.2 %collective-permute-start.1 = (bf16[256,512]{1,0:T(8,128)(2,1)S(1)}, bf16[256,512]{1,0:T(8,128)(2,1)S(1)}, u32[]{:S(2)}, u32[]{:S(2)}) collective-permute-start(bf16[256,512]{1,0:T(8,128)(2,1)S(1)} %copy-done.7), channel_id=1, source_target_pairs={{0,7},{1,0},{2,1},{3,2},{4,3},{5,4},{6,5},{7,6},{8,15},{9,8},{10,9... | collective-permute-start | bytes 786440 | tf_op jit(solution)/shard_map/ppermute | solution.py:464
  41.5 16.2 %collective-permute-start.2 = (bf16[256,512]{1,0:T(8,128)(2,1)S(1)}, bf16[256,512]{1,0:T(8,128)(2,1)S(1)}, u32[]{:S(2)}, u32[]{:S(2)}) collective-permute-start(bf16[256,512]{1,0:T(8,128)(2,1)S(1)} %collective-permute-done), channel_id=1, source_target_pairs={{0,1},{1,2},{2,3},{3,4},{4,5},{5,6},{6,7},{7,0},{8,9},{9,10},{10,1... | collective-permute-start | bytes 786440 | tf_op jit(solution)/shard_map/ppermute | solution.py:464
  49.3 29.0 %copy-start.12 = (s32[32,4]{0,1:T(4,128)S(1)}, s32[32,4]{0,1:T(4,128)}, u32[]{:S(2)}) copy-start(s32[32,4]{0,1:T(4,128)} %param.25) | copy-start | bytes 1540
  57.7 14.0 %collective-permute-start.4 = (bf16[256,512]{1,0:T(8,128)(2,1)S(1)}, bf16[256,512]{1,0:T(8,128)(2,1)S(1)}, u32[]{:S(2)}, u32[]{:S(2)}) collective-permute-start(bf16[256,512]{1,0:T(8,128)(2,1)S(1)} %collective-permute-done.2), channel_id=1, source_target_pairs={{0,1},{1,2},{2,3},{3,4},{4,5},{5,6},{6,7},{7,0},{8,9},{9,10},{10,1... | collective-permute-start | bytes 786440 | tf_op jit(solution)/shard_map/ppermute | solution.py:464
  59.4 8.5 %collective-permute-start.3 = (bf16[256,512]{1,0:T(8,128)(2,1)S(1)}, bf16[256,512]{1,0:T(8,128)(2,1)S(1)}, u32[]{:S(2)}, u32[]{:S(2)}) collective-permute-start(bf16[256,512]{1,0:T(8,128)(2,1)S(1)} %collective-permute-done.1), channel_id=1, source_target_pairs={{0,7},{1,0},{2,1},{3,2},{4,3},{5,4},{6,5},{7,6},{8,15},{9,8},{10,9... | collective-permute-start | bytes 786440 | tf_op jit(solution)/shard_map/ppermute | solution.py:464
  67.9 8.2 %collective-permute-start.5 = (bf16[256,512]{1,0:T(8,128)(2,1)S(1)}, bf16[256,512]{1,0:T(8,128)(2,1)S(1)}, u32[]{:S(2)}, u32[]{:S(2)}) collective-permute-start(bf16[256,512]{1,0:T(8,128)(2,1)S(1)} %collective-permute-done.3), channel_id=1, source_target_pairs={{0,7},{1,0},{2,1},{3,2},{4,3},{5,4},{6,5},{7,6},{8,15},{9,8},{10,9... | collective-permute-start | bytes 786440 | tf_op jit(solution)/shard_map/ppermute | solution.py:464
  77.6 22.1 %collective-permute-start.9 = (bf16[8,256,512]{2,1,0:T(8,128)(2,1)}, bf16[8,256,512]{2,1,0:T(8,128)(2,1)}, u32[]{:S(2)}, u32[]{:S(2)}) collective-permute-start(bf16[8,256,512]{2,1,0:T(8,128)(2,1)} %bitcast_dynamic-update-slice_fusion.refs_1_), channel_id=1, source_target_pairs={{0,8},{8,0},{16,24},{24,16},{32,40},{40,32},{48,56},{56,48},{64,72... | collective-permute-start | bytes 6291464 | tf_op jit(solution)/shard_map/ppermute | solution.py:516
  83.9 23.6 %copy-start = (bf16[4096,512]{1,0:T(8,128)(2,1)S(1)}, bf16[4096,512]{1,0:T(8,128)(2,1)}, u32[]{:S(2)}) copy-start(bf16[4096,512]{1,0:T(8,128)(2,1)} %states_ref.1) | copy-start | bytes 12582916
  83.9 23.6 %copy-start.3 = (bf16[512,512]{1,0:T(8,128)(2,1)S(1)}, bf16[512,512]{1,0:T(8,128)(2,1)}, u32[]{:S(2)}) copy-start(bf16[512,512]{1,0:T(8,128)(2,1)} %refs_0_.3) | copy-start | bytes 1572868
  89.7 13.2 %collective-permute-start.10 = (bf16[64,512]{1,0:T(8,128)(2,1)}, bf16[64,512]{1,0:T(8,128)(2,1)S(1)}, u32[]{:S(2)}, u32[]{:S(2)}) collective-permute-start(bf16[64,512]{1,0:T(8,128)(2,1)} %get-tuple-element.62), channel_id=1, source_target_pairs={{0,1},{1,2},{2,3},{3,4},{4,5},{5,6},{6,7},{7,0},{8,9},{9,10},{10,1... | collective-permute-start | bytes 196616 | tf_op jit(solution)/shard_map/ppermute | solution.py:539
  91.8 14.6 %collective-permute-start.11 = (bf16[64,512]{1,0:T(8,128)(2,1)}, bf16[64,512]{1,0:T(8,128)(2,1)S(1)}, u32[]{:S(2)}, u32[]{:S(2)}) collective-permute-start(bf16[64,512]{1,0:T(8,128)(2,1)} %get-tuple-element.63), channel_id=1, source_target_pairs={{0,2},{1,3},{2,4},{3,5},{4,6},{5,7},{6,0},{7,1},{8,10},{9,11},{10,... | collective-permute-start | bytes 196616 | tf_op jit(solution)/shard_map/ppermute | solution.py:539
  96.3 13.5 %collective-permute-start.12 = (bf16[64,512]{1,0:T(8,128)(2,1)}, bf16[64,512]{1,0:T(8,128)(2,1)S(1)}, u32[]{:S(2)}, u32[]{:S(2)}) collective-permute-start(bf16[64,512]{1,0:T(8,128)(2,1)} %get-tuple-element.64), channel_id=1, source_target_pairs={{0,3},{1,4},{2,5},{3,6},{4,7},{5,0},{6,1},{7,2},{8,11},{9,12},{10,... | collective-permute-start | bytes 196616 | tf_op jit(solution)/shard_map/ppermute | solution.py:539
  98.2 11.6 %collective-permute-start.13 = (bf16[64,512]{1,0:T(8,128)(2,1)}, bf16[64,512]{1,0:T(8,128)(2,1)S(1)}, u32[]{:S(2)}, u32[]{:S(2)}) collective-permute-start(bf16[64,512]{1,0:T(8,128)(2,1)} %get-tuple-element.65), channel_id=1, source_target_pairs={{0,4},{1,5},{2,6},{3,7},{4,0},{5,1},{6,2},{7,3},{8,12},{9,13},{10,... | collective-permute-start | bytes 196616 | tf_op jit(solution)/shard_map/ppermute | solution.py:539
  99.7 12.6 %collective-permute-start.14 = (bf16[64,512]{1,0:T(8,128)(2,1)}, bf16[64,512]{1,0:T(8,128)(2,1)S(1)}, u32[]{:S(2)}, u32[]{:S(2)}) collective-permute-start(bf16[64,512]{1,0:T(8,128)(2,1)} %get-tuple-element.66), channel_id=1, source_target_pairs={{0,5},{1,6},{2,7},{3,0},{4,1},{5,2},{6,3},{7,4},{8,13},{9,14},{10,... | collective-permute-start | bytes 196616 | tf_op jit(solution)/shard_map/ppermute | solution.py:539
  102.8 10.4 %collective-permute-start.15 = (bf16[64,512]{1,0:T(8,128)(2,1)}, bf16[64,512]{1,0:T(8,128)(2,1)S(1)}, u32[]{:S(2)}, u32[]{:S(2)}) collective-permute-start(bf16[64,512]{1,0:T(8,128)(2,1)} %get-tuple-element.67), channel_id=1, source_target_pairs={{0,6},{1,7},{2,0},{3,1},{4,2},{5,3},{6,4},{7,5},{8,14},{9,15},{10,... | collective-permute-start | bytes 196616 | tf_op jit(solution)/shard_map/ppermute | solution.py:539
  106.4 7.2 %collective-permute-start.16 = (bf16[64,512]{1,0:T(8,128)(2,1)}, bf16[64,512]{1,0:T(8,128)(2,1)S(1)}, u32[]{:S(2)}, u32[]{:S(2)}) collective-permute-start(bf16[64,512]{1,0:T(8,128)(2,1)} %get-tuple-element.68), channel_id=1, source_target_pairs={{0,7},{1,0},{2,1},{3,2},{4,3},{5,4},{6,5},{7,6},{8,15},{9,8},{10,9... | collective-permute-start | bytes 196616 | tf_op jit(solution)/shard_map/ppermute | solution.py:539
  (10 other events, 55.7 us)

commit v4 on v3

--- a/solution.py
+++ b/solution.py
@@ -14,7 +14,7 @@
 clip_level = 5.0
 TAIL = 10
 STAGE = 16
-SELECT = 52
+SELECT = 53
 TIGHT = 58
 
 f32 = jnp.float32
@@ -154,6 +154,7 @@
         ]
         + more_shapes,
         compiler_params=params(mib),
+        cost_estimate=pl.CostEstimate(flops=1, bytes_accessed=1, transcendentals=0),
         name="project",
     )(core, states, weight_t, *feed)
 
@@ -253,8 +254,8 @@
             block = turn * group + item
             lanes = pl.ds(pl.multiple_of(block * wide, wide), wide)
             query = query_ref[:, lanes]
-            tile_blocks = [window_ref[place_ref[block * tiles + t]] for t in range(tiles)]
-            counts = [count_ref[block * tiles + t] for t in range(tiles)]
+            tile_blocks = [window_ref[place_ref[block, t]] for t in range(tiles)]
+            counts = [count_ref[block, t] for t in range(tiles)]
             summed, total = tile_terms(
                 query.astype(f32), tile_blocks, tile_rows(rows_ref, block), counts
             )
@@ -302,7 +303,7 @@
         query_ref[:, pl.ds(pl.multiple_of(edge * wide, wide), wide)].astype(f32),
         [outer_ref[0]] * near_tiles,
         tile_rows(edge_rows_ref, edge),
-        [edge_count_ref[edge * near_tiles + t] for t in range(near_tiles)],
+        [edge_count_ref[edge, t] for t in range(near_tiles)],
     )
 
     def step(turn, _):
@@ -310,7 +311,7 @@
             block = turn * group + item
             lanes = pl.ds(pl.multiple_of(block * wide, wide), wide)
             tile_blocks = [reply_ref[slot_ref[0, t * blocks + block]] for t in range(tiles)]
-            counts = [count_ref[block * tiles + t] for t in range(tiles)]
+            counts = [count_ref[block, t] for t in range(tiles)]
             summed, total = tile_terms(
                 query_ref[:, lanes].astype(f32), tile_blocks, tile_rows(rows_ref, block), counts
             )
@@ -464,7 +465,6 @@
         return lax.ppermute(value, "heads", [(i, (i + by) % shares) for i in range(shares)])
 
     half = expand_weight.shape[1] // 2
-    once = turn(piece, 1)
     chosen = select_blocks(me.reshape(1), heard, packed)
     chosen, heard, outer, inner = barrier((chosen, heard, outer, inner))
     replies = lax.all_to_all(
@@ -485,7 +485,7 @@
         axis=0,
     )
     _, virtual_packed = project(core.reshape(1), extra, weight_t, block_rows, 16)
-    piece, once, virtual_packed = barrier((piece, once, virtual_packed))
+    piece, virtual_packed = barrier((piece, virtual_packed))
     local_ids = jnp.arange(blocks, dtype=jnp.int32)[:, None]
     global_ids = me * blocks + local_ids
     place = jnp.mod(neigh_source - global_ids + 1, all_blocks) + local_ids - 1
@@ -495,8 +495,8 @@
     near_count = jnp.where(beyond, 0, neigh_count)
     edge_count = jnp.where(beyond, neigh_count, 0)
     near_sum, near_total = near_terms(
-        place.reshape(-1),
-        near_count.reshape(-1),
+        place,
+        near_count,
         query,
         packed,
         inner,
@@ -505,22 +505,21 @@
         4,
     )
 
-    back = turn(piece, -1)
+    once, back = turn(piece, 1), turn(piece, -1)
     pieces = [piece, once, back]
     for step in range(2, 4):
         pieces += [turn(pieces[-2], 1), turn(pieces[-1], -1)]
     pieces.append(turn(piece, 4))
     offsets = (0, -1, 1, -2, 2, -3, 3, -4)
     mine = jnp.stack(pieces)
-    mine, near_total, outer = barrier((mine, near_total, outer))
     theirs = lax.ppermute(mine, "nodes", inward)
 
     attended = far_terms(
         share.reshape(1),
         slots,
-        expander_count.reshape(-1),
+        expander_count,
         edge.reshape(1),
-        edge_count.reshape(-1),
+        edge_count,
         query,
         replies,
         expander_rows,

time: 119 us -> 116 us (0.975)
  local copies, waits for them, and re-layouts: 11.3 us -> 7.69 us
    all_to_all x1, waiting for transfers between devices: 4.8 us -> 0.19 us  [local(): lax.all_to_all(chosen.reshape(span, BCAP * block_rows, lanes), 'nodes', s...]
    reshape x4 -> x0, local copies, waits for them, and re-layouts: 2.64 us -> none  [the longest x1 0.69 us: local(): expander_count.reshape(-1)]
    ppermute x7, waiting for transfers between devices: 16.5 us -> 19.1 us  [turn(): lax.ppermute(value, 'heads', [(i, (i + by) % shares) for i in range(share...]
    ppermute x1, waiting for transfers between devices: 0.01 us -> 1.71 us  [local(): inner = lax.ppermute(inner, 'nodes', inward)]
    unnamed x39 -> x38, local copies, waits for them, and re-layouts: 7.6 us -> 6.84 us
  transfers between devices with their start and end apart: 19 -> 19, of which waited for: 7 -> 9; matrix products, arithmetic and copies ran while one was open for 8% -> 6% of each run, Pallas kernels for 21% -> 19%
where the time goes in v4:
time: 116 us
  starting transfers between devices  51 us (44%)
  Pallas kernels  31.4 us (27%)
  waiting for transfers between devices  24.8 us (21%)
  local copies, waits for them, and re-layouts  7.69 us (7%)
    ppermute x7, waiting for transfers between devices, turn(): lax.ppermute(value, 'heads', [(i, (i + by) % shares) for i in range(share...  19.1 us
    ppermute x7, starting transfers between devices, local(): lax.ppermute(attended[ahead], 'heads', [(i, (i + ahead) % shares) for i i...  18.2 us
    ppermute x7, starting transfers between devices, turn(): lax.ppermute(value, 'heads', [(i, (i + by) % shares) for i in range(share...  17.5 us
    all_to_all x1, starting transfers between devices, local(): lax.all_to_all(message, 'nodes', split_axis=0, concat_axis=0, tiled=True)  7.53 us
    all_to_all x1, starting transfers between devices, local(): lax.all_to_all(chosen.reshape(span, BCAP * block_rows, lanes), 'nodes', s...  7.13 us
    pallas_call x2, Pallas kernels, project(): pl.pallas_call(project_kernel, grid=(rows // step_rows,), in_specs=[smem,...  7.05 us
    unnamed x38, local copies, waits for them, and re-layouts  6.84 us
    pallas_call x1, Pallas kernels, near_terms(): pl.pallas_call(functools.partial(near_kernel, group), in_specs=[smem, sme...  6.52 us
  transfers between devices with their start and end apart: 19, of which 9 were waited for; matrix products, arithmetic and copies ran while one was open for 6% of the time, Pallas kernels for 19%

profile of v4, /device:TPU:8, one launch (start us, length us, event | category | flops | bytes accessed | tf_op | source)
XLA Modules:
  0.0 115.7 jit_solution(10838887693440302294)
XLA Ops:
  0.0 1.7 %ask.1 = (bf16[32,16,128]{2,1,0:T(8,128)(2,1)}, s32[1,128]{1,0:T(1,128)}) custom-call(s32[4,32]{1,0:T(4,128)} %bitcast.35, bf16[1,512]{1,0:T(2,128)(2,1)} %virtual_ref.1), custom_call_target="tpu_custom_call" | custom-call | tf_op jit(solution)/shard_map/ask/pallas_call | solution.py:68
  1.7 7.5 %all-to-all-start = ((bf16[32,16,128]{2,1,0:T(8,128)(2,1)}), bf16[32,16,128]{2,1,0:T(8,128)(2,1)S(1)}, u32[]{:S(2)}, u32[]{:S(2)}) async-start(bf16[32,16,128]{2,1,0:T(8,128)(2,1)} %get-tuple-element.34), calls=%async_computation | async-start | bytes 262144 | tf_op jit(solution)/shard_map/all_to_all | solution.py:456
  9.3 6.1 %project.2 = (bf16[64,4096]{1,0:T(8,128)(2,1)}, bf16[32,128,128]{2,1,0:T(8,128)(2,1)}, bf16[1,128,128]{2,1,0:T(8,128)(2,1)}, bf16[1,128,128]{2,1,0:T(8,128)(2,1)}, bf16[256,512]{1,0:T(8,128)(2,1)}) custom-call(s32[1]{0:T(128)} %bitcast.1.core_ref, bf16[4096,512]{1,0:T(8,128)(2,1)} %states_ref.1, bf16[192,512]{1,0:T(8,128)(2,1)} %bitcast.29, ...), custom_call_target="tpu_custom_call" | custom-call | flops 1 | bytes 1 | tf_op jit(solution)/shard_map/project/pallas_call | solution.py:137
  15.9 3.4 %select_blocks.1 = bf16[128,128,128]{2,1,0:T(8,128)(2,1)} custom-call(s32[1]{0:T(128)} %bitcast.3.me_ref, bf16[32,16,128]{2,1,0:T(8,128)(2,1)S(1)} %all-to-all-done.heard_ref, bf16[32,128,128]{2,1,0:T(8,128)(2,1)} %get-tuple-element.35.pack_ref), custom_call_target="tpu_custom_call" | custom-call | tf_op jit(solution)/shard_map/select_blocks/pallas_call | solution.py:194
  19.3 7.1 %all-to-all-start.1 = ((bf16[32,512,128]{2,1,0:T(8,128)(2,1)}), bf16[32,512,128]{2,1,0:T(8,128)(2,1)}, u32[]{:S(2)}, u32[]{:S(2)}) async-start(bf16[32,512,128]{2,1,0:T(8,128)(2,1)} %bitcast.32), calls=%async_computation.1 | async-start | bytes 8388608 | tf_op jit(solution)/shard_map/all_to_all | solution.py:470
  27.5 2.0 %collective-permute-start = (bf16[256,512]{1,0:T(8,128)(2,1)S(1)}, bf16[256,512]{1,0:T(8,128)(2,1)S(1)}, u32[]{:S(2)}, u32[]{:S(2)}) collective-permute-start(bf16[256,512]{1,0:T(8,128)(2,1)S(1)} %copy-done.6), channel_id=1, source_target_pairs={{0,1},{1,2},{2,3},{3,4},{4,5},{5,6},{6,7},{7,0},{8,9},{9,10},{10,1... | collective-permute-start | bytes 786440 | tf_op jit(solution)/shard_map/ppermute | solution.py:465
  29.5 4.0 %collective-permute-start.1 = (bf16[256,512]{1,0:T(8,128)(2,1)S(1)}, bf16[256,512]{1,0:T(8,128)(2,1)S(1)}, u32[]{:S(2)}, u32[]{:S(2)}) collective-permute-start(bf16[256,512]{1,0:T(8,128)(2,1)S(1)} %copy-done.6), channel_id=1, source_target_pairs={{0,7},{1,0},{2,1},{3,2},{4,3},{5,4},{6,5},{7,6},{8,15},{9,8},{10,9... | collective-permute-start | bytes 786440 | tf_op jit(solution)/shard_map/ppermute | solution.py:465
  34.3 4.5 %collective-permute-start.6 = (bf16[256,512]{1,0:T(8,128)(2,1)S(1)}, bf16[256,512]{1,0:T(8,128)(2,1)S(1)}, u32[]{:S(2)}, u32[]{:S(2)}) collective-permute-start(bf16[256,512]{1,0:T(8,128)(2,1)S(1)} %copy-done.6), channel_id=1, source_target_pairs={{0,4},{1,5},{2,6},{3,7},{4,0},{5,1},{6,2},{7,3},{8,12},{9,13},{10,... | collective-permute-start | bytes 786440 | tf_op jit(solution)/shard_map/ppermute | solution.py:465
  40.8 6.9 %collective-permute-done.1 = bf16[256,512]{1,0:T(8,128)(2,1)S(1)} collective-permute-done((bf16[256,512]{1,0:T(8,128)(2,1)S(1)}, bf16[256,512]{1,0:T(8,128)(2,1)S(1)}, u32[]{:S(2)}, u32[]{:S(2)}) %collective-permute-start.1) | collective-permute-done | bytes 262176 | tf_op jit(solution)/shard_map/ppermute | solution.py:465
  47.7 3.7 %collective-permute-start.3 = (bf16[256,512]{1,0:T(8,128)(2,1)S(1)}, bf16[256,512]{1,0:T(8,128)(2,1)S(1)}, u32[]{:S(2)}, u32[]{:S(2)}) collective-permute-start(bf16[256,512]{1,0:T(8,128)(2,1)S(1)} %collective-permute-done.1), channel_id=1, source_target_pairs={{0,7},{1,0},{2,1},{3,2},{4,3},{5,4},{6,5},{7,6},{8,15},{9,8},{10,9... | collective-permute-start | bytes 786440 | tf_op jit(solution)/shard_map/ppermute | solution.py:465
  52.1 6.0 %collective-permute-done.2 = bf16[256,512]{1,0:T(8,128)(2,1)S(1)} collective-permute-done((bf16[256,512]{1,0:T(8,128)(2,1)S(1)}, bf16[256,512]{1,0:T(8,128)(2,1)S(1)}, u32[]{:S(2)}, u32[]{:S(2)}) %collective-permute-start.2) | collective-permute-done | bytes 262176 | tf_op jit(solution)/shard_map/ppermute | solution.py:465
  58.8 3.2 %collective-permute-start.5 = (bf16[256,512]{1,0:T(8,128)(2,1)S(1)}, bf16[256,512]{1,0:T(8,128)(2,1)S(1)}, u32[]{:S(2)}, u32[]{:S(2)}) collective-permute-start(bf16[256,512]{1,0:T(8,128)(2,1)S(1)} %collective-permute-done.3), channel_id=1, source_target_pairs={{0,7},{1,0},{2,1},{3,2},{4,3},{5,4},{6,5},{7,6},{8,15},{9,8},{10,9... | collective-permute-start | bytes 786440 | tf_op jit(solution)/shard_map/ppermute | solution.py:465
  62.8 4.9 %collective-permute-done.4 = bf16[256,512]{1,0:T(8,128)(2,1)S(1)} collective-permute-done((bf16[256,512]{1,0:T(8,128)(2,1)S(1)}, bf16[256,512]{1,0:T(8,128)(2,1)S(1)}, u32[]{:S(2)}, u32[]{:S(2)}) %collective-permute-start.4) | collective-permute-done | bytes 262176 | tf_op jit(solution)/shard_map/ppermute | solution.py:465
  72.0 1.7 %collective-permute-done.9.inner_ref = bf16[1,128,128]{2,1,0:T(8,128)(2,1)S(1)} collective-permute-done((bf16[1,128,128]{2,1,0:T(8,128)(2,1)S(1)}, bf16[1,128,128]{2,1,0:T(8,128)(2,1)S(1)}, u32[]{:S(2)}, u32[]{:S(2)}) %collective-permute-start.9) | collective-permute-done | bytes 32800 | tf_op jit(solution)/shard_map/ppermute | solution.py:478
  74.3 6.5 %near_terms.1 = (f32[64,4096]{1,0:T(8,128)}, f32[1,4096]{1,0:T(1,128)}) custom-call(s32[32,4]{1,0:T(8,128)} %get-tuple-element.63.place_ref, s32[32,4]{1,0:T(8,128)} %get-tuple-element.61.count_ref, bf16[64,4096]{1,0:T(8,128)(2,1)} %get-tuple-element.46.query_ref, bf16[32,128,128]{2,1,0:T(8,128)(2,1)} %get-tuple-element.35.pack_ref, ...), custom_call_target="tpu_custom_call" | custom-call | flops 1 | bytes 1 | tf_op jit(solution)/shard_map/near_terms/pallas_call | solution.py:278
  81.4 5.7 %far_terms.1 = (bf16[64,512]{1,0:T(8,128)(2,1)}, bf16[64,512]{1,0:T(8,128)(2,1)}, bf16[64,512]{1,0:T(8,128)(2,1)}, bf16[64,512]{1,0:T(8,128)(2,1)}, bf16[64,512]...) custom-call(s32[1]{0:T(128)} %bitcast.share_ref, ...), custom_call_target="tpu_custom_call" | custom-call | tf_op jit(solution)/shard_map/far_terms/pallas_call | solution.py:340
  87.2 1.8 %collective-permute-start.10 = (bf16[64,512]{1,0:T(8,128)(2,1)}, bf16[64,512]{1,0:T(8,128)(2,1)S(1)}, u32[]{:S(2)}, u32[]{:S(2)}) collective-permute-start(bf16[64,512]{1,0:T(8,128)(2,1)} %get-tuple-element.54), channel_id=1, source_target_pairs={{0,1},{1,2},{2,3},{3,4},{4,5},{5,6},{6,7},{7,0},{8,9},{9,10},{10,1... | collective-permute-start | bytes 196616 | tf_op jit(solution)/shard_map/ppermute | solution.py:538
  88.9 3.3 %collective-permute-start.11 = (bf16[64,512]{1,0:T(8,128)(2,1)}, bf16[64,512]{1,0:T(8,128)(2,1)S(1)}, u32[]{:S(2)}, u32[]{:S(2)}) collective-permute-start(bf16[64,512]{1,0:T(8,128)(2,1)} %get-tuple-element.55), channel_id=1, source_target_pairs={{0,2},{1,3},{2,4},{3,5},{4,6},{5,7},{6,0},{7,1},{8,10},{9,11},{10,... | collective-permute-start | bytes 196616 | tf_op jit(solution)/shard_map/ppermute | solution.py:538
  92.2 4.0 %collective-permute-start.12 = (bf16[64,512]{1,0:T(8,128)(2,1)}, bf16[64,512]{1,0:T(8,128)(2,1)S(1)}, u32[]{:S(2)}, u32[]{:S(2)}) collective-permute-start(bf16[64,512]{1,0:T(8,128)(2,1)} %get-tuple-element.56), channel_id=1, source_target_pairs={{0,3},{1,4},{2,5},{3,6},{4,7},{5,0},{6,1},{7,2},{8,11},{9,12},{10,... | collective-permute-start | bytes 196616 | tf_op jit(solution)/shard_map/ppermute | solution.py:538
  96.8 5.0 %collective-permute-start.14 = (bf16[64,512]{1,0:T(8,128)(2,1)}, bf16[64,512]{1,0:T(8,128)(2,1)S(1)}, u32[]{:S(2)}, u32[]{:S(2)}) collective-permute-start(bf16[64,512]{1,0:T(8,128)(2,1)} %get-tuple-element.58), channel_id=1, source_target_pairs={{0,5},{1,6},{2,7},{3,0},{4,1},{5,2},{6,3},{7,4},{8,13},{9,14},{10,... | collective-permute-start | bytes 196616 | tf_op jit(solution)/shard_map/ppermute | solution.py:538
  101.7 2.7 %collective-permute-start.15 = (bf16[64,512]{1,0:T(8,128)(2,1)}, bf16[64,512]{1,0:T(8,128)(2,1)S(1)}, u32[]{:S(2)}, u32[]{:S(2)}) collective-permute-start(bf16[64,512]{1,0:T(8,128)(2,1)} %get-tuple-element.59), channel_id=1, source_target_pairs={{0,6},{1,7},{2,0},{3,1},{4,2},{5,3},{6,4},{7,5},{8,14},{9,15},{10,... | collective-permute-start | bytes 196616 | tf_op jit(solution)/shard_map/ppermute | solution.py:538
  105.5 2.3 %stage.1 = (bf16[512,512]{1,0:T(8,128)(2,1)S(1)}, bf16[512,512]{1,0:T(8,128)(2,1)S(1)}, bf16[8,256,512]{2,1,0:T(8,128)(2,1)S(1)}, bf16[8,256,512]{2,1,0:T(8,128)(2,1)S(1)}) custom-call(s32[1]{0:T(128)} %bitcast.share_ref, bf16[4096,512]{1,0:T(8,128)(2,1)S(1)} %copy-done, bf16[512,512]{1,0:T(8,128)(2,1)S(1)} %copy-done.2, ...), custom_call_target="tpu_custom_call" | custom-call | tf_op jit(solution)/shard_map/stage/pallas_call | solution.py:371
  107.9 2.7 %collective-permute-done.14.rest_5_ = bf16[64,512]{1,0:T(8,128)(2,1)S(1)} collective-permute-done((bf16[64,512]{1,0:T(8,128)(2,1)}, bf16[64,512]{1,0:T(8,128)(2,1)S(1)}, u32[]{:S(2)}, u32[]{:S(2)}) %collective-permute-start.14) | collective-permute-done | bytes 65568 | tf_op jit(solution)/shard_map/ppermute | solution.py:538
  111.1 4.6 %tail.1 = bf16[512,512]{1,0:T(8,128)(2,1)} custom-call(s32[2]{0:T(128)S(1)} %pad_add_fusion.place_ref, bf16[512,512]{1,0:T(8,128)(2,1)S(1)} %get-tuple-element.41.own_ref, bf16[512,512]{1,0:T(8,128)(2,1)S(1)} %get-tuple-element.42.output_ref, bf16[8,256,512]{2,1,0:T(8,128)(2,1)S(1)} %get-tuple-element.43.mine_ref, ...), custom_call_target="tpu_custom_call" | custom-call | tf_op jit(solution)/shard_map/tail/pallas_call | solution.py:418
  (68 shorter events, 14.1 us)
Async XLA Ops:
  1.7 14.1 %all-to-all-start = ((bf16[32,16,128]{2,1,0:T(8,128)(2,1)}), bf16[32,16,128]{2,1,0:T(8,128)(2,1)S(1)}, u32[]{:S(2)}, u32[]{:S(2)}) async-start(bf16[32,16,128]{2,1,0:T(8,128)(2,1)} %get-tuple-element.34), calls=%async_computation | async-start | bytes 262144 | tf_op jit(solution)/shard_map/all_to_all | solution.py:456
  19.3 61.7 %all-to-all-start.1 = ((bf16[32,512,128]{2,1,0:T(8,128)(2,1)}), bf16[32,512,128]{2,1,0:T(8,128)(2,1)}, u32[]{:S(2)}, u32[]{:S(2)}) async-start(bf16[32,512,128]{2,1,0:T(8,128)(2,1)} %bitcast.32), calls=%async_computation.1 | async-start | bytes 8388608 | tf_op jit(solution)/shard_map/all_to_all | solution.py:470
  27.5 42.4 %copy-start.11 = (s32[32,4]{0,1:T(4,128)S(1)}, s32[32,4]{0,1:T(4,128)}, u32[]{:S(2)}) copy-start(s32[32,4]{0,1:T(4,128)} %param.20) | copy-start | bytes 1540
  27.5 42.5 %copy-start.9 = (s32[32,4]{0,1:T(4,128)S(1)}, s32[32,4]{0,1:T(4,128)}, u32[]{:S(2)}) copy-start(s32[32,4]{0,1:T(4,128)} %param.22) | copy-start | bytes 1540
  27.5 42.6 %copy-start.13 = (bf16[1,128,128]{2,1,0:T(8,128)(2,1)S(1)}, bf16[1,128,128]{2,1,0:T(8,128)(2,1)}, u32[]{:S(2)}) copy-start(bf16[1,128,128]{2,1,0:T(8,128)(2,1)} %get-tuple-element.49) | copy-start | bytes 98308
  27.5 43.1 %copy-start.12 = (bf16[1,128,128]{2,1,0:T(8,128)(2,1)S(1)}, bf16[1,128,128]{2,1,0:T(8,128)(2,1)}, u32[]{:S(2)}) copy-start(bf16[1,128,128]{2,1,0:T(8,128)(2,1)} %get-tuple-element.48) | copy-start | bytes 98308
  27.5 43.8 %copy-start.10 = (s32[32,4]{0,1:T(4,128)S(1)}, s32[32,4]{0,1:T(4,128)}, u32[]{:S(2)}) copy-start(s32[32,4]{0,1:T(4,128)} %param.25) | copy-start | bytes 1540
  27.5 12.6 %collective-permute-start = (bf16[256,512]{1,0:T(8,128)(2,1)S(1)}, bf16[256,512]{1,0:T(8,128)(2,1)S(1)}, u32[]{:S(2)}, u32[]{:S(2)}) collective-permute-start(bf16[256,512]{1,0:T(8,128)(2,1)S(1)} %copy-done.6), channel_id=1, source_target_pairs={{0,1},{1,2},{2,3},{3,4},{4,5},{5,6},{6,7},{7,0},{8,9},{9,10},{10,1... | collective-permute-start | bytes 786440 | tf_op jit(solution)/shard_map/ppermute | solution.py:465
  29.5 18.2 %collective-permute-start.1 = (bf16[256,512]{1,0:T(8,128)(2,1)S(1)}, bf16[256,512]{1,0:T(8,128)(2,1)S(1)}, u32[]{:S(2)}, u32[]{:S(2)}) collective-permute-start(bf16[256,512]{1,0:T(8,128)(2,1)S(1)} %copy-done.6), channel_id=1, source_target_pairs={{0,7},{1,0},{2,1},{3,2},{4,3},{5,4},{6,5},{7,6},{8,15},{9,8},{10,9... | collective-permute-start | bytes 786440 | tf_op jit(solution)/shard_map/ppermute | solution.py:465
  34.3 34.8 %collective-permute-start.6 = (bf16[256,512]{1,0:T(8,128)(2,1)S(1)}, bf16[256,512]{1,0:T(8,128)(2,1)S(1)}, u32[]{:S(2)}, u32[]{:S(2)}) collective-permute-start(bf16[256,512]{1,0:T(8,128)(2,1)S(1)} %copy-done.6), channel_id=1, source_target_pairs={{0,4},{1,5},{2,6},{3,7},{4,0},{5,1},{6,2},{7,3},{8,12},{9,13},{10,... | collective-permute-start | bytes 786440 | tf_op jit(solution)/shard_map/ppermute | solution.py:465
  40.1 18.0 %collective-permute-start.2 = (bf16[256,512]{1,0:T(8,128)(2,1)S(1)}, bf16[256,512]{1,0:T(8,128)(2,1)S(1)}, u32[]{:S(2)}, u32[]{:S(2)}) collective-permute-start(bf16[256,512]{1,0:T(8,128)(2,1)S(1)} %collective-permute-done), channel_id=1, source_target_pairs={{0,1},{1,2},{2,3},{3,4},{4,5},{5,6},{6,7},{7,0},{8,9},{9,10},{10,1... | collective-permute-start | bytes 786440 | tf_op jit(solution)/shard_map/ppermute | solution.py:465
  47.7 11.2 %collective-permute-start.3 = (bf16[256,512]{1,0:T(8,128)(2,1)S(1)}, bf16[256,512]{1,0:T(8,128)(2,1)S(1)}, u32[]{:S(2)}, u32[]{:S(2)}) collective-permute-start(bf16[256,512]{1,0:T(8,128)(2,1)S(1)} %collective-permute-done.1), channel_id=1, source_target_pairs={{0,7},{1,0},{2,1},{3,2},{4,3},{5,4},{6,5},{7,6},{8,15},{9,8},{10,9... | collective-permute-start | bytes 786440 | tf_op jit(solution)/shard_map/ppermute | solution.py:465
  58.1 9.5 %collective-permute-start.4 = (bf16[256,512]{1,0:T(8,128)(2,1)S(1)}, bf16[256,512]{1,0:T(8,128)(2,1)S(1)}, u32[]{:S(2)}, u32[]{:S(2)}) collective-permute-start(bf16[256,512]{1,0:T(8,128)(2,1)S(1)} %collective-permute-done.2), channel_id=1, source_target_pairs={{0,1},{1,2},{2,3},{3,4},{4,5},{5,6},{6,7},{7,0},{8,9},{9,10},{10,1... | collective-permute-start | bytes 786440 | tf_op jit(solution)/shard_map/ppermute | solution.py:465
  58.8 9.6 %collective-permute-start.5 = (bf16[256,512]{1,0:T(8,128)(2,1)S(1)}, bf16[256,512]{1,0:T(8,128)(2,1)S(1)}, u32[]{:S(2)}, u32[]{:S(2)}) collective-permute-start(bf16[256,512]{1,0:T(8,128)(2,1)S(1)} %collective-permute-done.3), channel_id=1, source_target_pairs={{0,7},{1,0},{2,1},{3,2},{4,3},{5,4},{6,5},{7,6},{8,15},{9,8},{10,9... | collective-permute-start | bytes 786440 | tf_op jit(solution)/shard_map/ppermute | solution.py:465
  69.9 26.9 %collective-permute-start.7 = (bf16[8,256,512]{2,1,0:T(8,128)(2,1)}, bf16[8,256,512]{2,1,0:T(8,128)(2,1)}, u32[]{:S(2)}, u32[]{:S(2)}) collective-permute-start(bf16[8,256,512]{2,1,0:T(8,128)(2,1)} %bitcast_dynamic-update-slice_fusion.refs_1_), channel_id=1, source_target_pairs={{0,8},{8,0},{16,24},{24,16},{32,40},{40,32},{48,56},{56,48},{64,72... | collective-permute-start | bytes 6291464 | tf_op jit(solution)/shard_map/ppermute | solution.py:515
  70.1 3.6 %collective-permute-start.9 = (bf16[1,128,128]{2,1,0:T(8,128)(2,1)S(1)}, bf16[1,128,128]{2,1,0:T(8,128)(2,1)S(1)}, u32[]{:S(2)}, u32[]{:S(2)}) collective-permute-start(bf16[1,128,128]{2,1,0:T(8,128)(2,1)S(1)} %copy-done.13), channel_id=1, source_target_pairs={{0,8},{8,0},{16,24},{24,16},{32,40},{40,32},{48,56},{56,48},{64,72... | collective-permute-start | bytes 98312 | tf_op jit(solution)/shard_map/ppermute | solution.py:478
  70.6 10.2 %collective-permute-start.8 = (bf16[1,128,128]{2,1,0:T(8,128)(2,1)S(1)}, bf16[1,128,128]{2,1,0:T(8,128)(2,1)S(1)}, u32[]{:S(2)}, u32[]{:S(2)}) collective-permute-start(bf16[1,128,128]{2,1,0:T(8,128)(2,1)S(1)} %copy-done.12), channel_id=1, source_target_pairs={{0,248},{8,16},{16,8},{24,32},{32,24},{40,48},{48,40},{56,64},{64,... | collective-permute-start | bytes 98312 | tf_op jit(solution)/shard_map/ppermute | solution.py:479
  87.2 14.6 %collective-permute-start.10 = (bf16[64,512]{1,0:T(8,128)(2,1)}, bf16[64,512]{1,0:T(8,128)(2,1)S(1)}, u32[]{:S(2)}, u32[]{:S(2)}) collective-permute-start(bf16[64,512]{1,0:T(8,128)(2,1)} %get-tuple-element.54), channel_id=1, source_target_pairs={{0,1},{1,2},{2,3},{3,4},{4,5},{5,6},{6,7},{7,0},{8,9},{9,10},{10,1... | collective-permute-start | bytes 196616 | tf_op jit(solution)/shard_map/ppermute | solution.py:538
  88.9 15.5 %collective-permute-start.11 = (bf16[64,512]{1,0:T(8,128)(2,1)}, bf16[64,512]{1,0:T(8,128)(2,1)S(1)}, u32[]{:S(2)}, u32[]{:S(2)}) collective-permute-start(bf16[64,512]{1,0:T(8,128)(2,1)} %get-tuple-element.55), channel_id=1, source_target_pairs={{0,2},{1,3},{2,4},{3,5},{4,6},{5,7},{6,0},{7,1},{8,10},{9,11},{10,... | collective-permute-start | bytes 196616 | tf_op jit(solution)/shard_map/ppermute | solution.py:538
  92.2 15.6 %collective-permute-start.12 = (bf16[64,512]{1,0:T(8,128)(2,1)}, bf16[64,512]{1,0:T(8,128)(2,1)S(1)}, u32[]{:S(2)}, u32[]{:S(2)}) collective-permute-start(bf16[64,512]{1,0:T(8,128)(2,1)} %get-tuple-element.56), channel_id=1, source_target_pairs={{0,3},{1,4},{2,5},{3,6},{4,7},{5,0},{6,1},{7,2},{8,11},{9,12},{10,... | collective-permute-start | bytes 196616 | tf_op jit(solution)/shard_map/ppermute | solution.py:538
  96.2 11.6 %collective-permute-start.13 = (bf16[64,512]{1,0:T(8,128)(2,1)}, bf16[64,512]{1,0:T(8,128)(2,1)S(1)}, u32[]{:S(2)}, u32[]{:S(2)}) collective-permute-start(bf16[64,512]{1,0:T(8,128)(2,1)} %get-tuple-element.57), channel_id=1, source_target_pairs={{0,4},{1,5},{2,6},{3,7},{4,0},{5,1},{6,2},{7,3},{8,12},{9,13},{10,... | collective-permute-start | bytes 196616 | tf_op jit(solution)/shard_map/ppermute | solution.py:538
  96.8 13.8 %collective-permute-start.14 = (bf16[64,512]{1,0:T(8,128)(2,1)}, bf16[64,512]{1,0:T(8,128)(2,1)S(1)}, u32[]{:S(2)}, u32[]{:S(2)}) collective-permute-start(bf16[64,512]{1,0:T(8,128)(2,1)} %get-tuple-element.58), channel_id=1, source_target_pairs={{0,5},{1,6},{2,7},{3,0},{4,1},{5,2},{6,3},{7,4},{8,13},{9,14},{10,... | collective-permute-start | bytes 196616 | tf_op jit(solution)/shard_map/ppermute | solution.py:538
  101.7 8.9 %collective-permute-start.15 = (bf16[64,512]{1,0:T(8,128)(2,1)}, bf16[64,512]{1,0:T(8,128)(2,1)S(1)}, u32[]{:S(2)}, u32[]{:S(2)}) collective-permute-start(bf16[64,512]{1,0:T(8,128)(2,1)} %get-tuple-element.59), channel_id=1, source_target_pairs={{0,6},{1,7},{2,0},{3,1},{4,2},{5,3},{6,4},{7,5},{8,14},{9,15},{10,... | collective-permute-start | bytes 196616 | tf_op jit(solution)/shard_map/ppermute | solution.py:538
  104.4 6.7 %collective-permute-start.16 = (bf16[64,512]{1,0:T(8,128)(2,1)}, bf16[64,512]{1,0:T(8,128)(2,1)S(1)}, u32[]{:S(2)}, u32[]{:S(2)}) collective-permute-start(bf16[64,512]{1,0:T(8,128)(2,1)} %get-tuple-element.60), channel_id=1, source_target_pairs={{0,7},{1,0},{2,1},{3,2},{4,3},{5,4},{6,5},{7,6},{8,15},{9,8},{10,9... | collective-permute-start | bytes 196616 | tf_op jit(solution)/shard_map/ppermute | solution.py:538
  (9 other events, 118.4 us)

commit v5 on v4

--- a/solution.py
+++ b/solution.py
@@ -381,12 +381,12 @@
 
 
 def tail_kernel(
-    offsets, place_ref, own_ref, output_ref, mine_ref, theirs_ref, bias_ref, *rest
+    behinds, offsets, place_ref, own_ref, output_ref, mine_ref, theirs_ref, bias_ref, *rest
 ):
     pieces, (out_ref, att_ref) = rest[:-2], rest[-2:]
     features, rows = att_ref.shape
     head, _ = pieces[0].shape
-    for behind, piece in enumerate(pieces):
+    for behind, piece in zip(behinds, pieces):
         owner = lax.rem(place_ref[0] + len(pieces) - behind, len(pieces))
         att_ref[pl.ds(pl.multiple_of(owner * head, head), head), :] = piece[...]
     parts = len(offsets)
@@ -413,10 +413,10 @@
     out_ref[...] = summed.astype(bf16)
 
 
-def tail(place, own, output_weight, mine, theirs, bias, pieces, offsets):
+def tail(place, own, output_weight, mine, theirs, bias, pieces, behinds, offsets):
     rows, features = own.shape
     return pl.pallas_call(
-        functools.partial(tail_kernel, offsets),
+        functools.partial(tail_kernel, behinds, offsets),
         in_specs=[smem] + [vmem] * (5 + len(pieces)),
         out_specs=vmem,
         out_shape=jax.ShapeDtypeStruct(own.shape, bf16),
@@ -533,11 +533,8 @@
     own, output_staged, mine, theirs = stage(
         share.reshape(1), node_states, rows // shares, output_weight, mine, theirs
     )
-    regrouped = [attended[0]] + [None] * (shares - 1)
-    for ahead in sorted(range(1, shares), key=lambda ahead: -min(ahead, shares - ahead)):
-        regrouped[ahead] = lax.ppermute(
-            attended[ahead], "heads", [(i, (i + ahead) % shares) for i in range(shares)]
-        )
+    aheads = [0] + sorted(range(1, shares), key=lambda ahead: -min(ahead, shares - ahead))
+    regrouped = [attended[0]] + [turn(attended[ahead], ahead) for ahead in aheads[1:]]
     return tail(
         jnp.stack([share, core]),
         own,
@@ -546,6 +543,7 @@
         theirs,
         expand_bias.reshape(2 * shares, 1, half),
         regrouped,
+        tuple(aheads),
         offsets,
     )
 

time: 116 us -> 114 us (0.983)
  waiting for transfers between devices: 24.8 us -> 21.9 us
    ppermute x7 -> x14, starting transfers between devices: 17.5 us -> 36.6 us  [turn(): lax.ppermute(value, 'heads', [(i, (i + by) % shares) for i in range(share...]
    ppermute x7 -> x0, starting transfers between devices: 18.2 us -> none  [local(): lax.ppermute(attended[ahead], 'heads', [(i, (i + ahead) % shares) for i i...]
    ppermute x7 -> x0, waiting for transfers between devices: 3.27 us -> none  [local(): lax.ppermute(attended[ahead], 'heads', [(i, (i + ahead) % shares) for i i...]
    ppermute x7 -> x14, waiting for transfers between devices: 19.1 us -> 19.5 us  [turn(): lax.ppermute(value, 'heads', [(i, (i + by) % shares) for i in range(share...]
where the time goes in v5:
time: 114 us
  starting transfers between devices  51.9 us (46%)
  Pallas kernels  31.4 us (28%)
  waiting for transfers between devices  21.9 us (19%)
  local copies, waits for them, and re-layouts  7.69 us (7%)
    ppermute x14, starting transfers between devices, turn(): lax.ppermute(value, 'heads', [(i, (i + by) % shares) for i in range(share...  36.6 us
    ppermute x14, waiting for transfers between devices, turn(): lax.ppermute(value, 'heads', [(i, (i + by) % shares) for i in range(share...  19.5 us
    all_to_all x1, starting transfers between devices, local(): lax.all_to_all(message, 'nodes', split_axis=0, concat_axis=0, tiled=True)  7.53 us
    all_to_all x1, starting transfers between devices, local(): lax.all_to_all(chosen.reshape(span, BCAP * block_rows, lanes), 'nodes', s...  7.13 us
    pallas_call x2, Pallas kernels, project(): pl.pallas_call(project_kernel, grid=(rows // step_rows,), in_specs=[smem,...  7.05 us
    unnamed x38, local copies, waits for them, and re-layouts  6.84 us
    pallas_call x1, Pallas kernels, near_terms(): pl.pallas_call(functools.partial(near_kernel, group), in_specs=[smem, sme...  6.52 us
    pallas_call x1, Pallas kernels, far_terms(): pl.pallas_call(functools.partial(far_kernel, group), in_specs=[smem] * 5...  5.74 us
  transfers between devices with their start and end apart: 19, of which 9 were waited for; matrix products, arithmetic and copies ran while one was open for 6% of the time, Pallas kernels for 19%

profile of v5, /device:TPU:8, one launch (start us, length us, event | category | flops | bytes accessed | tf_op | source)
XLA Modules:
  0.0 113.8 jit_solution(1928086551750319620)
XLA Ops:
  0.0 1.7 %ask.1 = (bf16[32,16,128]{2,1,0:T(8,128)(2,1)}, s32[1,128]{1,0:T(1,128)}) custom-call(s32[4,32]{1,0:T(4,128)} %bitcast.35, bf16[1,512]{1,0:T(2,128)(2,1)} %virtual_ref.1), custom_call_target="tpu_custom_call" | custom-call | tf_op jit(solution)/shard_map/ask/pallas_call | solution.py:68
  1.7 7.5 %all-to-all-start = ((bf16[32,16,128]{2,1,0:T(8,128)(2,1)}), bf16[32,16,128]{2,1,0:T(8,128)(2,1)S(1)}, u32[]{:S(2)}, u32[]{:S(2)}) async-start(bf16[32,16,128]{2,1,0:T(8,128)(2,1)} %get-tuple-element.34), calls=%async_computation | async-start | bytes 262144 | tf_op jit(solution)/shard_map/all_to_all | solution.py:456
  9.3 6.1 %project.2 = (bf16[64,4096]{1,0:T(8,128)(2,1)}, bf16[32,128,128]{2,1,0:T(8,128)(2,1)}, bf16[1,128,128]{2,1,0:T(8,128)(2,1)}, bf16[1,128,128]{2,1,0:T(8,128)(2,1)}, bf16[256,512]{1,0:T(8,128)(2,1)}) custom-call(s32[1]{0:T(128)} %bitcast.1.core_ref, bf16[4096,512]{1,0:T(8,128)(2,1)} %states_ref.1, bf16[192,512]{1,0:T(8,128)(2,1)} %bitcast.29, ...), custom_call_target="tpu_custom_call" | custom-call | flops 1 | bytes 1 | tf_op jit(solution)/shard_map/project/pallas_call | solution.py:137
  15.9 3.4 %select_blocks.1 = bf16[128,128,128]{2,1,0:T(8,128)(2,1)} custom-call(s32[1]{0:T(128)} %bitcast.3.me_ref, bf16[32,16,128]{2,1,0:T(8,128)(2,1)S(1)} %all-to-all-done.heard_ref, bf16[32,128,128]{2,1,0:T(8,128)(2,1)} %get-tuple-element.35.pack_ref), custom_call_target="tpu_custom_call" | custom-call | tf_op jit(solution)/shard_map/select_blocks/pallas_call | solution.py:194
  19.3 7.1 %all-to-all-start.1 = ((bf16[32,512,128]{2,1,0:T(8,128)(2,1)}), bf16[32,512,128]{2,1,0:T(8,128)(2,1)}, u32[]{:S(2)}, u32[]{:S(2)}) async-start(bf16[32,512,128]{2,1,0:T(8,128)(2,1)} %bitcast.32), calls=%async_computation.1 | async-start | bytes 8388608 | tf_op jit(solution)/shard_map/all_to_all | solution.py:470
  27.5 2.0 %collective-permute-start = (bf16[256,512]{1,0:T(8,128)(2,1)S(1)}, bf16[256,512]{1,0:T(8,128)(2,1)S(1)}, u32[]{:S(2)}, u32[]{:S(2)}) collective-permute-start(bf16[256,512]{1,0:T(8,128)(2,1)S(1)} %copy-done.6), channel_id=1, source_target_pairs={{0,1},{1,2},{2,3},{3,4},{4,5},{5,6},{6,7},{7,0},{8,9},{9,10},{10,1... | collective-permute-start | bytes 786440 | tf_op jit(solution)/shard_map/ppermute | solution.py:465
  29.5 4.0 %collective-permute-start.1 = (bf16[256,512]{1,0:T(8,128)(2,1)S(1)}, bf16[256,512]{1,0:T(8,128)(2,1)S(1)}, u32[]{:S(2)}, u32[]{:S(2)}) collective-permute-start(bf16[256,512]{1,0:T(8,128)(2,1)S(1)} %copy-done.6), channel_id=1, source_target_pairs={{0,7},{1,0},{2,1},{3,2},{4,3},{5,4},{6,5},{7,6},{8,15},{9,8},{10,9... | collective-permute-start | bytes 786440 | tf_op jit(solution)/shard_map/ppermute | solution.py:465
  34.3 4.5 %collective-permute-start.6 = (bf16[256,512]{1,0:T(8,128)(2,1)S(1)}, bf16[256,512]{1,0:T(8,128)(2,1)S(1)}, u32[]{:S(2)}, u32[]{:S(2)}) collective-permute-start(bf16[256,512]{1,0:T(8,128)(2,1)S(1)} %copy-done.6), channel_id=1, source_target_pairs={{0,4},{1,5},{2,6},{3,7},{4,0},{5,1},{6,2},{7,3},{8,12},{9,13},{10,... | collective-permute-start | bytes 786440 | tf_op jit(solution)/shard_map/ppermute | solution.py:465
  40.8 6.9 %collective-permute-done.1 = bf16[256,512]{1,0:T(8,128)(2,1)S(1)} collective-permute-done((bf16[256,512]{1,0:T(8,128)(2,1)S(1)}, bf16[256,512]{1,0:T(8,128)(2,1)S(1)}, u32[]{:S(2)}, u32[]{:S(2)}) %collective-permute-start.1) | collective-permute-done | bytes 262176 | tf_op jit(solution)/shard_map/ppermute | solution.py:465
  47.7 3.7 %collective-permute-start.3 = (bf16[256,512]{1,0:T(8,128)(2,1)S(1)}, bf16[256,512]{1,0:T(8,128)(2,1)S(1)}, u32[]{:S(2)}, u32[]{:S(2)}) collective-permute-start(bf16[256,512]{1,0:T(8,128)(2,1)S(1)} %collective-permute-done.1), channel_id=1, source_target_pairs={{0,7},{1,0},{2,1},{3,2},{4,3},{5,4},{6,5},{7,6},{8,15},{9,8},{10,9... | collective-permute-start | bytes 786440 | tf_op jit(solution)/shard_map/ppermute | solution.py:465
  52.1 6.0 %collective-permute-done.2 = bf16[256,512]{1,0:T(8,128)(2,1)S(1)} collective-permute-done((bf16[256,512]{1,0:T(8,128)(2,1)S(1)}, bf16[256,512]{1,0:T(8,128)(2,1)S(1)}, u32[]{:S(2)}, u32[]{:S(2)}) %collective-permute-start.2) | collective-permute-done | bytes 262176 | tf_op jit(solution)/shard_map/ppermute | solution.py:465
  58.8 3.2 %collective-permute-start.5 = (bf16[256,512]{1,0:T(8,128)(2,1)S(1)}, bf16[256,512]{1,0:T(8,128)(2,1)S(1)}, u32[]{:S(2)}, u32[]{:S(2)}) collective-permute-start(bf16[256,512]{1,0:T(8,128)(2,1)S(1)} %collective-permute-done.3), channel_id=1, source_target_pairs={{0,7},{1,0},{2,1},{3,2},{4,3},{5,4},{6,5},{7,6},{8,15},{9,8},{10,9... | collective-permute-start | bytes 786440 | tf_op jit(solution)/shard_map/ppermute | solution.py:465
  62.8 4.9 %collective-permute-done.4 = bf16[256,512]{1,0:T(8,128)(2,1)S(1)} collective-permute-done((bf16[256,512]{1,0:T(8,128)(2,1)S(1)}, bf16[256,512]{1,0:T(8,128)(2,1)S(1)}, u32[]{:S(2)}, u32[]{:S(2)}) %collective-permute-start.4) | collective-permute-done | bytes 262176 | tf_op jit(solution)/shard_map/ppermute | solution.py:465
  72.0 1.7 %collective-permute-done.9.inner_ref = bf16[1,128,128]{2,1,0:T(8,128)(2,1)S(1)} collective-permute-done((bf16[1,128,128]{2,1,0:T(8,128)(2,1)S(1)}, bf16[1,128,128]{2,1,0:T(8,128)(2,1)S(1)}, u32[]{:S(2)}, u32[]{:S(2)}) %collective-permute-start.9) | collective-permute-done | bytes 32800 | tf_op jit(solution)/shard_map/ppermute | solution.py:478
  74.3 6.5 %near_terms.1 = (f32[64,4096]{1,0:T(8,128)}, f32[1,4096]{1,0:T(1,128)}) custom-call(s32[32,4]{1,0:T(8,128)} %get-tuple-element.63.place_ref, s32[32,4]{1,0:T(8,128)} %get-tuple-element.61.count_ref, bf16[64,4096]{1,0:T(8,128)(2,1)} %get-tuple-element.46.query_ref, bf16[32,128,128]{2,1,0:T(8,128)(2,1)} %get-tuple-element.35.pack_ref, ...), custom_call_target="tpu_custom_call" | custom-call | flops 1 | bytes 1 | tf_op jit(solution)/shard_map/near_terms/pallas_call | solution.py:278
  81.4 5.7 %far_terms.1 = (bf16[64,512]{1,0:T(8,128)(2,1)}, bf16[64,512]{1,0:T(8,128)(2,1)}, bf16[64,512]{1,0:T(8,128)(2,1)}, bf16[64,512]{1,0:T(8,128)(2,1)}, bf16[64,512]...) custom-call(s32[1]{0:T(128)} %bitcast.share_ref, ...), custom_call_target="tpu_custom_call" | custom-call | tf_op jit(solution)/shard_map/far_terms/pallas_call | solution.py:340
  87.2 7.0 %collective-permute-start.10 = (bf16[64,512]{1,0:T(8,128)(2,1)}, bf16[64,512]{1,0:T(8,128)(2,1)S(1)}, u32[]{:S(2)}, u32[]{:S(2)}) collective-permute-start(bf16[64,512]{1,0:T(8,128)(2,1)} %get-tuple-element.54), channel_id=1, source_target_pairs={{0,4},{1,5},{2,6},{3,7},{4,0},{5,1},{6,2},{7,3},{8,12},{9,13},{10,... | collective-permute-start | bytes 196616 | tf_op jit(solution)/shard_map/ppermute | solution.py:465
  94.2 1.9 %collective-permute-start.11 = (bf16[64,512]{1,0:T(8,128)(2,1)}, bf16[64,512]{1,0:T(8,128)(2,1)S(1)}, u32[]{:S(2)}, u32[]{:S(2)}) collective-permute-start(bf16[64,512]{1,0:T(8,128)(2,1)} %get-tuple-element.55), channel_id=1, source_target_pairs={{0,3},{1,4},{2,5},{3,6},{4,7},{5,0},{6,1},{7,2},{8,11},{9,12},{10,... | collective-permute-start | bytes 196616 | tf_op jit(solution)/shard_map/ppermute | solution.py:465
  96.2 3.1 %collective-permute-start.12 = (bf16[64,512]{1,0:T(8,128)(2,1)}, bf16[64,512]{1,0:T(8,128)(2,1)S(1)}, u32[]{:S(2)}, u32[]{:S(2)}) collective-permute-start(bf16[64,512]{1,0:T(8,128)(2,1)} %get-tuple-element.56), channel_id=1, source_target_pairs={{0,5},{1,6},{2,7},{3,0},{4,1},{5,2},{6,3},{7,4},{8,13},{9,14},{10,... | collective-permute-start | bytes 196616 | tf_op jit(solution)/shard_map/ppermute | solution.py:465
  99.3 1.5 %collective-permute-start.13 = (bf16[64,512]{1,0:T(8,128)(2,1)}, bf16[64,512]{1,0:T(8,128)(2,1)S(1)}, u32[]{:S(2)}, u32[]{:S(2)}) collective-permute-start(bf16[64,512]{1,0:T(8,128)(2,1)} %get-tuple-element.57), channel_id=1, source_target_pairs={{0,2},{1,3},{2,4},{3,5},{4,6},{5,7},{6,0},{7,1},{8,10},{9,11},{10,... | collective-permute-start | bytes 196616 | tf_op jit(solution)/shard_map/ppermute | solution.py:465
  100.7 2.7 %collective-permute-start.14 = (bf16[64,512]{1,0:T(8,128)(2,1)}, bf16[64,512]{1,0:T(8,128)(2,1)S(1)}, u32[]{:S(2)}, u32[]{:S(2)}) collective-permute-start(bf16[64,512]{1,0:T(8,128)(2,1)} %get-tuple-element.58), channel_id=1, source_target_pairs={{0,6},{1,7},{2,0},{3,1},{4,2},{5,3},{6,4},{7,5},{8,14},{9,15},{10,... | collective-permute-start | bytes 196616 | tf_op jit(solution)/shard_map/ppermute | solution.py:465
  104.7 1.9 %collective-permute-start.16 = (bf16[64,512]{1,0:T(8,128)(2,1)}, bf16[64,512]{1,0:T(8,128)(2,1)S(1)}, u32[]{:S(2)}, u32[]{:S(2)}) collective-permute-start(bf16[64,512]{1,0:T(8,128)(2,1)} %get-tuple-element.60), channel_id=1, source_target_pairs={{0,7},{1,0},{2,1},{3,2},{4,3},{5,4},{6,5},{7,6},{8,15},{9,8},{10,9... | collective-permute-start | bytes 196616 | tf_op jit(solution)/shard_map/ppermute | solution.py:465
  106.7 2.3 %stage.1 = (bf16[512,512]{1,0:T(8,128)(2,1)S(1)}, bf16[512,512]{1,0:T(8,128)(2,1)S(1)}, bf16[8,256,512]{2,1,0:T(8,128)(2,1)S(1)}, bf16[8,256,512]{2,1,0:T(8,128)(2,1)S(1)}) custom-call(s32[1]{0:T(128)} %bitcast.share_ref, bf16[4096,512]{1,0:T(8,128)(2,1)S(1)} %copy-done, bf16[512,512]{1,0:T(8,128)(2,1)S(1)} %copy-done.2, ...), custom_call_target="tpu_custom_call" | custom-call | tf_op jit(solution)/shard_map/stage/pallas_call | solution.py:371
  109.2 4.6 %tail.1 = bf16[512,512]{1,0:T(8,128)(2,1)} custom-call(s32[2]{0:T(128)S(1)} %pad_add_fusion.place_ref, bf16[512,512]{1,0:T(8,128)(2,1)S(1)} %get-tuple-element.41.own_ref, bf16[512,512]{1,0:T(8,128)(2,1)S(1)} %get-tuple-element.42.output_ref, bf16[8,256,512]{2,1,0:T(8,128)(2,1)S(1)} %get-tuple-element.43.mine_ref, ...), custom_call_target="tpu_custom_call" | custom-call | tf_op jit(solution)/shard_map/tail/pallas_call | solution.py:418
  (68 shorter events, 13.4 us)
Async XLA Ops:
  1.7 14.1 %all-to-all-start = ((bf16[32,16,128]{2,1,0:T(8,128)(2,1)}), bf16[32,16,128]{2,1,0:T(8,128)(2,1)S(1)}, u32[]{:S(2)}, u32[]{:S(2)}) async-start(bf16[32,16,128]{2,1,0:T(8,128)(2,1)} %get-tuple-element.34), calls=%async_computation | async-start | bytes 262144 | tf_op jit(solution)/shard_map/all_to_all | solution.py:456
  19.3 61.7 %all-to-all-start.1 = ((bf16[32,512,128]{2,1,0:T(8,128)(2,1)}), bf16[32,512,128]{2,1,0:T(8,128)(2,1)}, u32[]{:S(2)}, u32[]{:S(2)}) async-start(bf16[32,512,128]{2,1,0:T(8,128)(2,1)} %bitcast.32), calls=%async_computation.1 | async-start | bytes 8388608 | tf_op jit(solution)/shard_map/all_to_all | solution.py:470
  27.5 42.4 %copy-start.11 = (s32[32,4]{0,1:T(4,128)S(1)}, s32[32,4]{0,1:T(4,128)}, u32[]{:S(2)}) copy-start(s32[32,4]{0,1:T(4,128)} %param.20) | copy-start | bytes 1540
  27.5 42.5 %copy-start.9 = (s32[32,4]{0,1:T(4,128)S(1)}, s32[32,4]{0,1:T(4,128)}, u32[]{:S(2)}) copy-start(s32[32,4]{0,1:T(4,128)} %param.22) | copy-start | bytes 1540
  27.5 42.6 %copy-start.13 = (bf16[1,128,128]{2,1,0:T(8,128)(2,1)S(1)}, bf16[1,128,128]{2,1,0:T(8,128)(2,1)}, u32[]{:S(2)}) copy-start(bf16[1,128,128]{2,1,0:T(8,128)(2,1)} %get-tuple-element.49) | copy-start | bytes 98308
  27.5 43.1 %copy-start.12 = (bf16[1,128,128]{2,1,0:T(8,128)(2,1)S(1)}, bf16[1,128,128]{2,1,0:T(8,128)(2,1)}, u32[]{:S(2)}) copy-start(bf16[1,128,128]{2,1,0:T(8,128)(2,1)} %get-tuple-element.48) | copy-start | bytes 98308
  27.5 43.8 %copy-start.10 = (s32[32,4]{0,1:T(4,128)S(1)}, s32[32,4]{0,1:T(4,128)}, u32[]{:S(2)}) copy-start(s32[32,4]{0,1:T(4,128)} %param.25) | copy-start | bytes 1540
  27.5 12.6 %collective-permute-start = (bf16[256,512]{1,0:T(8,128)(2,1)S(1)}, bf16[256,512]{1,0:T(8,128)(2,1)S(1)}, u32[]{:S(2)}, u32[]{:S(2)}) collective-permute-start(bf16[256,512]{1,0:T(8,128)(2,1)S(1)} %copy-done.6), channel_id=1, source_target_pairs={{0,1},{1,2},{2,3},{3,4},{4,5},{5,6},{6,7},{7,0},{8,9},{9,10},{10,1... | collective-permute-start | bytes 786440 | tf_op jit(solution)/shard_map/ppermute | solution.py:465
  29.5 18.2 %collective-permute-start.1 = (bf16[256,512]{1,0:T(8,128)(2,1)S(1)}, bf16[256,512]{1,0:T(8,128)(2,1)S(1)}, u32[]{:S(2)}, u32[]{:S(2)}) collective-permute-start(bf16[256,512]{1,0:T(8,128)(2,1)S(1)} %copy-done.6), channel_id=1, source_target_pairs={{0,7},{1,0},{2,1},{3,2},{4,3},{5,4},{6,5},{7,6},{8,15},{9,8},{10,9... | collective-permute-start | bytes 786440 | tf_op jit(solution)/shard_map/ppermute | solution.py:465
  34.3 34.8 %collective-permute-start.6 = (bf16[256,512]{1,0:T(8,128)(2,1)S(1)}, bf16[256,512]{1,0:T(8,128)(2,1)S(1)}, u32[]{:S(2)}, u32[]{:S(2)}) collective-permute-start(bf16[256,512]{1,0:T(8,128)(2,1)S(1)} %copy-done.6), channel_id=1, source_target_pairs={{0,4},{1,5},{2,6},{3,7},{4,0},{5,1},{6,2},{7,3},{8,12},{9,13},{10,... | collective-permute-start | bytes 786440 | tf_op jit(solution)/shard_map/ppermute | solution.py:465
  40.1 18.0 %collective-permute-start.2 = (bf16[256,512]{1,0:T(8,128)(2,1)S(1)}, bf16[256,512]{1,0:T(8,128)(2,1)S(1)}, u32[]{:S(2)}, u32[]{:S(2)}) collective-permute-start(bf16[256,512]{1,0:T(8,128)(2,1)S(1)} %collective-permute-done), channel_id=1, source_target_pairs={{0,1},{1,2},{2,3},{3,4},{4,5},{5,6},{6,7},{7,0},{8,9},{9,10},{10,1... | collective-permute-start | bytes 786440 | tf_op jit(solution)/shard_map/ppermute | solution.py:465
  47.7 11.2 %collective-permute-start.3 = (bf16[256,512]{1,0:T(8,128)(2,1)S(1)}, bf16[256,512]{1,0:T(8,128)(2,1)S(1)}, u32[]{:S(2)}, u32[]{:S(2)}) collective-permute-start(bf16[256,512]{1,0:T(8,128)(2,1)S(1)} %collective-permute-done.1), channel_id=1, source_target_pairs={{0,7},{1,0},{2,1},{3,2},{4,3},{5,4},{6,5},{7,6},{8,15},{9,8},{10,9... | collective-permute-start | bytes 786440 | tf_op jit(solution)/shard_map/ppermute | solution.py:465
  58.1 9.5 %collective-permute-start.4 = (bf16[256,512]{1,0:T(8,128)(2,1)S(1)}, bf16[256,512]{1,0:T(8,128)(2,1)S(1)}, u32[]{:S(2)}, u32[]{:S(2)}) collective-permute-start(bf16[256,512]{1,0:T(8,128)(2,1)S(1)} %collective-permute-done.2), channel_id=1, source_target_pairs={{0,1},{1,2},{2,3},{3,4},{4,5},{5,6},{6,7},{7,0},{8,9},{9,10},{10,1... | collective-permute-start | bytes 786440 | tf_op jit(solution)/shard_map/ppermute | solution.py:465
  58.8 9.6 %collective-permute-start.5 = (bf16[256,512]{1,0:T(8,128)(2,1)S(1)}, bf16[256,512]{1,0:T(8,128)(2,1)S(1)}, u32[]{:S(2)}, u32[]{:S(2)}) collective-permute-start(bf16[256,512]{1,0:T(8,128)(2,1)S(1)} %collective-permute-done.3), channel_id=1, source_target_pairs={{0,7},{1,0},{2,1},{3,2},{4,3},{5,4},{6,5},{7,6},{8,15},{9,8},{10,9... | collective-permute-start | bytes 786440 | tf_op jit(solution)/shard_map/ppermute | solution.py:465
  69.9 30.9 %collective-permute-start.7 = (bf16[8,256,512]{2,1,0:T(8,128)(2,1)}, bf16[8,256,512]{2,1,0:T(8,128)(2,1)}, u32[]{:S(2)}, u32[]{:S(2)}) collective-permute-start(bf16[8,256,512]{2,1,0:T(8,128)(2,1)} %bitcast_dynamic-update-slice_fusion.refs_1_), channel_id=1, source_target_pairs={{0,8},{8,0},{16,24},{24,16},{32,40},{40,32},{48,56},{56,48},{64,72... | collective-permute-start | bytes 6291464 | tf_op jit(solution)/shard_map/ppermute | solution.py:515
  70.1 3.6 %collective-permute-start.9 = (bf16[1,128,128]{2,1,0:T(8,128)(2,1)S(1)}, bf16[1,128,128]{2,1,0:T(8,128)(2,1)S(1)}, u32[]{:S(2)}, u32[]{:S(2)}) collective-permute-start(bf16[1,128,128]{2,1,0:T(8,128)(2,1)S(1)} %copy-done.13), channel_id=1, source_target_pairs={{0,8},{8,0},{16,24},{24,16},{32,40},{40,32},{48,56},{56,48},{64,72... | collective-permute-start | bytes 98312 | tf_op jit(solution)/shard_map/ppermute | solution.py:478
  70.6 10.2 %collective-permute-start.8 = (bf16[1,128,128]{2,1,0:T(8,128)(2,1)S(1)}, bf16[1,128,128]{2,1,0:T(8,128)(2,1)S(1)}, u32[]{:S(2)}, u32[]{:S(2)}) collective-permute-start(bf16[1,128,128]{2,1,0:T(8,128)(2,1)S(1)} %copy-done.12), channel_id=1, source_target_pairs={{0,248},{8,16},{16,8},{24,32},{32,24},{40,48},{48,40},{56,64},{64,... | collective-permute-start | bytes 98312 | tf_op jit(solution)/shard_map/ppermute | solution.py:479
  87.2 16.2 %collective-permute-start.10 = (bf16[64,512]{1,0:T(8,128)(2,1)}, bf16[64,512]{1,0:T(8,128)(2,1)S(1)}, u32[]{:S(2)}, u32[]{:S(2)}) collective-permute-start(bf16[64,512]{1,0:T(8,128)(2,1)} %get-tuple-element.54), channel_id=1, source_target_pairs={{0,4},{1,5},{2,6},{3,7},{4,0},{5,1},{6,2},{7,3},{8,12},{9,13},{10,... | collective-permute-start | bytes 196616 | tf_op jit(solution)/shard_map/ppermute | solution.py:465
  94.2 10.5 %collective-permute-start.11 = (bf16[64,512]{1,0:T(8,128)(2,1)}, bf16[64,512]{1,0:T(8,128)(2,1)S(1)}, u32[]{:S(2)}, u32[]{:S(2)}) collective-permute-start(bf16[64,512]{1,0:T(8,128)(2,1)} %get-tuple-element.55), channel_id=1, source_target_pairs={{0,3},{1,4},{2,5},{3,6},{4,7},{5,0},{6,1},{7,2},{8,11},{9,12},{10,... | collective-permute-start | bytes 196616 | tf_op jit(solution)/shard_map/ppermute | solution.py:465
  96.2 12.9 %collective-permute-start.12 = (bf16[64,512]{1,0:T(8,128)(2,1)}, bf16[64,512]{1,0:T(8,128)(2,1)S(1)}, u32[]{:S(2)}, u32[]{:S(2)}) collective-permute-start(bf16[64,512]{1,0:T(8,128)(2,1)} %get-tuple-element.56), channel_id=1, source_target_pairs={{0,5},{1,6},{2,7},{3,0},{4,1},{5,2},{6,3},{7,4},{8,13},{9,14},{10,... | collective-permute-start | bytes 196616 | tf_op jit(solution)/shard_map/ppermute | solution.py:465
  99.3 9.8 %collective-permute-start.13 = (bf16[64,512]{1,0:T(8,128)(2,1)}, bf16[64,512]{1,0:T(8,128)(2,1)S(1)}, u32[]{:S(2)}, u32[]{:S(2)}) collective-permute-start(bf16[64,512]{1,0:T(8,128)(2,1)} %get-tuple-element.57), channel_id=1, source_target_pairs={{0,2},{1,3},{2,4},{3,5},{4,6},{5,7},{6,0},{7,1},{8,10},{9,11},{10,... | collective-permute-start | bytes 196616 | tf_op jit(solution)/shard_map/ppermute | solution.py:465
  100.7 8.4 %collective-permute-start.14 = (bf16[64,512]{1,0:T(8,128)(2,1)}, bf16[64,512]{1,0:T(8,128)(2,1)S(1)}, u32[]{:S(2)}, u32[]{:S(2)}) collective-permute-start(bf16[64,512]{1,0:T(8,128)(2,1)} %get-tuple-element.58), channel_id=1, source_target_pairs={{0,6},{1,7},{2,0},{3,1},{4,2},{5,3},{6,4},{7,5},{8,14},{9,15},{10,... | collective-permute-start | bytes 196616 | tf_op jit(solution)/shard_map/ppermute | solution.py:465
  103.4 5.7 %collective-permute-start.15 = (bf16[64,512]{1,0:T(8,128)(2,1)}, bf16[64,512]{1,0:T(8,128)(2,1)S(1)}, u32[]{:S(2)}, u32[]{:S(2)}) collective-permute-start(bf16[64,512]{1,0:T(8,128)(2,1)} %get-tuple-element.59), channel_id=1, source_target_pairs={{0,1},{1,2},{2,3},{3,4},{4,5},{5,6},{6,7},{7,0},{8,9},{9,10},{10,1... | collective-permute-start | bytes 196616 | tf_op jit(solution)/shard_map/ppermute | solution.py:465
  104.7 4.5 %collective-permute-start.16 = (bf16[64,512]{1,0:T(8,128)(2,1)}, bf16[64,512]{1,0:T(8,128)(2,1)S(1)}, u32[]{:S(2)}, u32[]{:S(2)}) collective-permute-start(bf16[64,512]{1,0:T(8,128)(2,1)} %get-tuple-element.60), channel_id=1, source_target_pairs={{0,7},{1,0},{2,1},{3,2},{4,3},{5,4},{6,5},{7,6},{8,15},{9,8},{10,9... | collective-permute-start | bytes 196616 | tf_op jit(solution)/shard_map/ppermute | solution.py:465
  (9 other events, 114.5 us)
